TPU v7x, 32 devices: a whole 2x2x4 slice. The times are simulated.
32 devices in a mesh: batch: 8 (over z, y), chan: 4 (over x, core).
Axes of the slice: x: 2, y: 2, z: 4, core: 2. Of those that a mesh axis runs over, the one named last changes fastest.
Arguments:
- features: bfloat16 [256, 256, 128], P('batch', 'chan'), may hold values from -6 to 6
- skip_feature: bfloat16 [256, 128, 128], P('batch', 'chan'), may hold values from -6 to 6
- section_ids: int32 [256], P('batch'), may hold values from 0 to 2
- micro_ids: int32 [256], P('batch'), may hold values from 0 to 3, as said below
- widener: bfloat16 [9, 2, 256, 512], P(None, None, 'chan', 'batch'), may hold values from -0.09375 to 0.09375
- refiner: bfloat16 [9, 2, 256, 256], P(None, None, 'chan', 'batch'), may hold values from -0.125 to 0.125
- squeezer: bfloat16 [16, 256, 1024], P(None, 'chan', 'batch'), may hold values from -0.09375 to 0.09375
- exciter: bfloat16 [256, 256], P('chan', 'batch'), may hold values from -0.75 to 0.75
- gain_one: float32 [256], P('chan'), may hold values from 0.5 to 1.5
- bias_one: float32 [256], P('chan'), may hold values from -3 to 3
- gain_two: float32 [256], P('chan'), may hold values from 0.5 to 1.5
- bias_two: float32 [256], P('chan'), may hold values from -3 to 3
- upstream: bfloat16 [256, 256, 256], P('batch', 'chan'), may hold values from -6 to 6
Outputs:
- output: bfloat16 [256, 256, 256], P('batch', 'chan')
- input_grad: float32 [256, 256, 128], P('batch', 'chan')
- skip_grad: float32 [256, 128, 128], P('batch', 'chan')
- widener_grad: float32 [9, 2, 256, 512], P(None, None, 'chan', 'batch')
- refiner_grad: float32 [9, 2, 256, 256], P(None, None, 'chan', 'batch')
- squeezer_grad: float32 [16, 256, 1024], P(None, 'chan', 'batch')
- exciter_grad: float32 [256, 256], P('chan', 'batch')
- norm_grads: float32 [4, 256], P(None, 'chan')
Inputs may be any that keep to these rules, and one draw needn't show every extreme that they name: `micro_ids`: each of the 4 micro-batches holds exactly 64 samples.
All inputs are finite; a program needn't handle non-finite values.
Results may differ from a plain program's by a relative error of at most 0.015.
Values may be sent and summed in bfloat16 or wider, within the bound.
No kernel may reach another device: no remote copies, remote signals or barrier semaphores. Data moves between devices by JAX's collectives and lax.ppermute only.
A program may use at most 384 MiB of HBM per device.

v0:
```python
import jax
import jax.numpy as jnp
from jax import lax
from jax.sharding import PartitionSpec as P

MB = 4


precise = lax.Precision.HIGHEST
epsilon = 1e-05


def window(padded, offset):
    vertical = offset // 3
    across = offset % 3
    return padded[:, :, vertical : vertical + 16, across : across + 16].reshape(
        padded.shape[0], padded.shape[1], 256
    )


def pad_field(field):
    return jnp.pad(field, ((0, 0), (0, 0), (1, 1), (1, 1)))


def conv_forward(padded, kernel):
    total = None
    for offset in range(9):
        term = jnp.einsum(
            "hoc,bcp->bhop",
            kernel[offset],
            window(padded, offset),
            preferred_element_type=jnp.float32,
        )
        total = term if total is None else total + term
    return total


def conv_kernel_grad(padded, grad_out):
    pieces = []
    for offset in range(9):
        pieces.append(
            jnp.einsum(
                "bhop,bcp->hoc",
                grad_out,
                window(padded, offset),
                preferred_element_type=jnp.float32,
            )
        )
    return jnp.stack(pieces, axis=0)


def conv_field_grad(kernel, grad_out):
    samples = grad_out.shape[0]
    halves = grad_out.shape[1]
    outputs = grad_out.shape[2]
    padded = jnp.pad(
        grad_out.reshape(samples, halves, outputs, 16, 16), ((0, 0), (0, 0), (0, 0), (1, 1), (1, 1))
    )
    total = None
    for offset in range(9):
        vertical = 2 - offset // 3
        across = 2 - offset % 3
        shifted = padded[:, :, :, vertical : vertical + 16, across : across + 16].reshape(
            samples, halves, outputs, 256
        )
        term = jnp.einsum(
            "hoc,bhop->bcp", kernel[offset], shifted, preferred_element_type=jnp.float32
        )
        total = term if total is None else total + term
    return total


def gated_unit(conv):
    return conv[:, 0] * jax.nn.sigmoid(conv[:, 1])


def gated_back(conv, grad):
    sigmoid_part = jax.nn.sigmoid(conv[:, 1])
    first = grad * sigmoid_part
    second = grad * conv[:, 0] * sigmoid_part * (1.0 - sigmoid_part)
    return jnp.stack([first, second], axis=1)


def group_stats(values, onehot, entries):
    totals = lax.psum(jnp.dot(onehot.T, jnp.sum(values, axis=2), precision=precise), "batch")
    means = totals / entries
    centered = values - jnp.dot(onehot, means, precision=precise)[:, :, None]
    squares = lax.psum(
        jnp.dot(onehot.T, jnp.sum(centered * centered, axis=2), precision=precise), "batch"
    )
    spread = squares / entries
    inverse = lax.rsqrt(spread + epsilon)
    return (centered * jnp.dot(onehot, inverse, precision=precise)[:, :, None], inverse)


def norm_back(grad, normed, inverse, gain, onehot, entries):
    sum_grad, sum_cross = lax.psum(
        (
            jnp.dot(onehot.T, jnp.sum(grad, axis=2), precision=precise),
            jnp.dot(onehot.T, jnp.sum(grad * normed, axis=2), precision=precise),
        ),
        "batch",
    )
    gain_grad = jnp.sum(sum_cross, axis=0)
    shift_grad = jnp.sum(sum_grad, axis=0)
    per_grad = jnp.dot(onehot, sum_grad, precision=precise)[:, :, None] / entries
    per_cross = jnp.dot(onehot, sum_cross, precision=precise)[:, :, None] / entries
    scale = jnp.dot(onehot, inverse, precision=precise)[:, :, None] * gain[None, :, None]
    return (scale * (grad - per_grad - normed * per_cross), gain_grad, shift_grad)


def on_device(
    features,
    skip_feature,
    section_ids,
    micro_ids,
    widener,
    refiner,
    squeezer,
    exciter,
    gain_one,
    bias_one,
    gain_two,
    bias_two,
    upstream,
):
    samples = features.shape[0]
    entries = float(samples * lax.axis_size("batch") // MB * 256)
    onehot = (micro_ids[:, None] == jnp.arange(MB, dtype=jnp.int32)[None, :]).astype(jnp.float32)
    feature_full, skip_full = (
        lax.all_gather(features, "chan", axis=1, tiled=True),
        lax.all_gather(skip_feature, "chan", axis=1, tiled=True),
    )
    widener_full, refiner_full, squeezer_full, exciter_full = (
        lax.all_gather(widener, "batch", axis=3, tiled=True),
        lax.all_gather(refiner, "batch", axis=3, tiled=True),
        lax.all_gather(squeezer, "batch", axis=2, tiled=True),
        lax.all_gather(exciter, "batch", axis=1, tiled=True),
    )
    upsampled = jnp.repeat(
        jnp.repeat(feature_full.reshape(samples, -1, 8, 8), 2, axis=2), 2, axis=3
    )
    up_padded = pad_field(upsampled)
    conv_one = conv_forward(up_padded, widener_full)
    normed_one, inverse_one = group_stats(gated_unit(conv_one), onehot, entries)
    hidden = (normed_one * gain_one[None, :, None] + bias_one[None, :, None]).astype(jnp.bfloat16)
    hidden_full = lax.all_gather(hidden, "chan", axis=1, tiled=True)
    hidden_padded = pad_field(hidden_full.reshape(samples, -1, 16, 16))
    conv_two = conv_forward(hidden_padded, refiner_full)
    normed_two, inverse_two = group_stats(gated_unit(conv_two), onehot, entries)
    norm_two = normed_two * gain_two[None, :, None] + bias_two[None, :, None]
    pooled = skip_full.reshape(samples, -1, 16)
    squeezed = jnp.einsum("toc,bct->bo", squeezer_full, pooled, preferred_element_type=jnp.float32)
    squeeze_sig = jax.nn.sigmoid(squeezed)
    swish = (squeezed * squeeze_sig).astype(jnp.bfloat16)
    swish_full = lax.all_gather(swish, "chan", axis=1, tiled=True)
    excited = jnp.einsum("oc,bc->bo", exciter_full, swish_full, preferred_element_type=jnp.float32)
    gate = jax.nn.sigmoid(excited)
    output = norm_two * gate[:, :, None]
    weight_of = jnp.where(section_ids == 0, 1.0, jnp.where(section_ids == 1, 2.0, 4.0)).astype(
        jnp.float32
    )
    grad_out = upstream.astype(jnp.float32) * weight_of[:, None, None]
    grad_gate = jnp.sum(grad_out * norm_two, axis=2)
    grad_excited = (grad_gate * gate * (1.0 - gate)).astype(jnp.bfloat16)
    grad_glu_two, gain_two_grad, bias_two_grad = norm_back(
        grad_out * gate[:, :, None], normed_two, inverse_two, gain_two, onehot, entries
    )
    grad_conv_two = gated_back(conv_two, grad_glu_two).astype(jnp.bfloat16)
    refiner_grad = conv_kernel_grad(hidden_padded, grad_conv_two)
    partial_hidden = conv_field_grad(refiner_full, grad_conv_two)
    grad_hidden = lax.psum_scatter(
        partial_hidden.astype(jnp.bfloat16), "chan", scatter_dimension=1, tiled=True
    ).astype(jnp.float32)
    grad_glu_one, gain_one_grad, bias_one_grad = norm_back(
        grad_hidden, normed_one, inverse_one, gain_one, onehot, entries
    )
    grad_conv_one = gated_back(conv_one, grad_glu_one).astype(jnp.bfloat16)
    widener_grad = conv_kernel_grad(up_padded, grad_conv_one)
    grad_upsampled = conv_field_grad(widener_full, grad_conv_one)
    partial_input = jnp.sum(grad_upsampled.reshape(samples, -1, 8, 2, 8, 2), axis=(3, 5)).reshape(
        samples, -1, 128
    )
    exciter_grad = jnp.einsum(
        "bo,bc->oc", grad_excited, swish_full, preferred_element_type=jnp.float32
    )
    partial_swish = jnp.einsum(
        "bo,oc->bc", grad_excited, exciter_full, preferred_element_type=jnp.float32
    )
    grad_swish = lax.psum_scatter(
        partial_swish.astype(jnp.bfloat16), "chan", scatter_dimension=1, tiled=True
    ).astype(jnp.float32)
    grad_squeezed = (grad_swish * squeeze_sig * (1.0 + squeezed * (1.0 - squeeze_sig))).astype(
        jnp.bfloat16
    )
    squeezer_grad = jnp.einsum(
        "bo,bct->toc", grad_squeezed, pooled, preferred_element_type=jnp.float32
    )
    partial_pooled = jnp.einsum(
        "bo,toc->bct", grad_squeezed, squeezer_full, preferred_element_type=jnp.float32
    ).reshape(samples, -1, 128)
    input_grad, skip_grad = (
        lax.psum_scatter(
            partial_input.astype(jnp.bfloat16), "chan", scatter_dimension=1, tiled=True
        ).astype(jnp.float32),
        lax.psum_scatter(
            partial_pooled.astype(jnp.bfloat16), "chan", scatter_dimension=1, tiled=True
        ).astype(jnp.float32),
    )
    widener_sum, refiner_sum, squeezer_sum, exciter_sum = (
        lax.psum_scatter(widener_grad, "batch", scatter_dimension=3, tiled=True),
        lax.psum_scatter(refiner_grad, "batch", scatter_dimension=3, tiled=True),
        lax.psum_scatter(squeezer_grad, "batch", scatter_dimension=2, tiled=True),
        lax.psum_scatter(exciter_grad, "batch", scatter_dimension=1, tiled=True),
    )
    norm_grads = jnp.stack([gain_one_grad, bias_one_grad, gain_two_grad, bias_two_grad], axis=0)
    return (
        output.astype(jnp.bfloat16),
        input_grad,
        skip_grad,
        widener_sum,
        refiner_sum,
        squeezer_sum,
        exciter_sum,
        norm_grads,
    )


def solution(mesh):
    placed = (
        P("batch", "chan", None),
        P("batch", "chan", None),
        P("batch"),
        P("batch"),
        P(None, None, "chan", "batch"),
        P(None, None, "chan", "batch"),
        P(None, "chan", "batch"),
        P("chan", "batch"),
        P("chan"),
        P("chan"),
        P("chan"),
        P("chan"),
        P("batch", "chan", None),
    )
    return jax.shard_map(
        on_device,
        mesh=mesh,
        in_specs=placed,
        out_specs=(
            P("batch", "chan", None),
            P("batch", "chan", None),
            P("batch", "chan", None),
            P(None, None, "chan", "batch"),
            P(None, None, "chan", "batch"),
            P(None, "chan", "batch"),
            P("chan", "batch"),
            P(None, "chan"),
        ),
        check_vma=False,
    )
```

profile of v0, /device:TPU:0, one launch (start us, length us, event | category | flops | bytes accessed | tf_op | source)
XLA Modules:
  0.0 1322.4 jit_solution(17776991429386465852)
XLA Ops:
  11.2 54.4 %all-gather.9.cloned.1.call-done = bf16[9,2,64,512]{2,1,0,3:T(2,128)(2,1)} async-done(((bf16[9,2,64,64]{2,1,0,3:T(2,128)(2,1)}), bf16[9,2,64,512]{2,1,0,3:T(2,128)(2,1)}) %all-gather.9.cloned.1.call-update) | async-done | bytes 1179664 | tf_op jit(solution)/shard_map/all_gather | solution.py:135
  70.2 18.1 %all-gather.7.cloned.1.call-done = bf16[32,256,128]{2,1,0:T(8,128)(2,1)} async-done(((bf16[32,64,128]{2,1,0:T(8,128)(2,1)}), bf16[32,256,128]{2,1,0:T(8,128)(2,1)}) %all-gather.7.cloned.1.call-update) | async-done | bytes 2097168 | tf_op jit(solution)/shard_map/all_gather | solution.py:131
  96.3 13.4 %copy.177 = bf16[32,512,8,8]{1,2,3,0:T(8,128)(2,1)S(1)} copy(bf16[32,512,8,8]{0,3,2,1:T(8,128)(2,1)} %bitcast.726) | data formatting | bytes 4194304 | tf_op jit(solution)/shard_map/reshape | solution.py:141
  133.0 47.2 %pad_slice_fusion = (bf16[32,512,16,16]{1,2,3,0:T(8,128)(2,1)}, bf16[32,512,16,16]{1,2,3,0:T(8,128)(2,1)}, bf16[32,512,16,16]{1,2,3,0:T(8,128)(2,1)}, bf16[32,51...) fusion(bf16[32,512,16,16]{1,2,3,0:T(8,128)(2,1)} %bitcast.725), kind=kLoop, calls=%fused_computation | loop fusion | bytes 75497472 | tf_op jit(solution)/shard_map/slice | solution.py:16
  180.1 15.2 %copy.182 = bf16[32,512,16,16]{1,3,2,0:T(8,128)(2,1)} copy(bf16[32,512,16,16]{1,2,3,0:T(8,128)(2,1)} %get-tuple-element.46) | data formatting | bytes 16777216 | tf_op jit(solution)/shard_map/slice | solution.py:16
  195.4 15.4 %copy.185 = bf16[32,512,16,16]{1,3,2,0:T(8,128)(2,1)} copy(bf16[32,512,16,16]{1,2,3,0:T(8,128)(2,1)} %get-tuple-element.47) | data formatting | bytes 16777216 | tf_op jit(solution)/shard_map/slice | solution.py:16
  210.8 15.4 %copy.188 = bf16[32,512,16,16]{1,3,2,0:T(8,128)(2,1)} copy(bf16[32,512,16,16]{1,2,3,0:T(8,128)(2,1)} %get-tuple-element.48) | data formatting | bytes 16777216 | tf_op jit(solution)/shard_map/slice | solution.py:16
  226.1 15.7 %copy.194 = bf16[32,512,16,16]{1,3,2,0:T(8,128)(2,1)} copy(bf16[32,512,16,16]{1,2,3,0:T(8,128)(2,1)} %get-tuple-element.49) | data formatting | bytes 16777216 | tf_op jit(solution)/shard_map/slice | solution.py:16
  241.8 15.3 %copy.197 = bf16[32,512,16,16]{1,3,2,0:T(8,128)(2,1)} copy(bf16[32,512,16,16]{1,2,3,0:T(8,128)(2,1)} %get-tuple-element.50) | data formatting | bytes 16777216 | tf_op jit(solution)/shard_map/slice | solution.py:16
  257.1 15.4 %copy.200 = bf16[32,512,16,16]{1,3,2,0:T(8,128)(2,1)} copy(bf16[32,512,16,16]{1,2,3,0:T(8,128)(2,1)} %get-tuple-element.51) | data formatting | bytes 16777216 | tf_op jit(solution)/shard_map/slice | solution.py:16
  272.5 15.4 %copy.178 = bf16[32,512,16,16]{1,3,2,0:T(8,128)(2,1)} copy(bf16[32,512,16,16]{1,2,3,0:T(8,128)(2,1)} %get-tuple-element.52) | data formatting | bytes 16777216 | tf_op jit(solution)/shard_map/slice | solution.py:16
  340.5 15.4 %copy.203 = bf16[32,512,16,16]{1,3,2,0:T(8,128)(2,1)} copy(bf16[32,512,16,16]{1,2,3,0:T(8,128)(2,1)} %get-tuple-element.45) | data formatting | bytes 16777216 | tf_op jit(solution)/shard_map/slice | solution.py:16
  355.9 16.3 %add_bitcast_fusion.1 = f32[32,2,64,256]{3,2,1,0:T(8,128)S(1)} fusion(f32[32,256,2,64]{1,3,2,0:T(8,128)} %fusion.86, f32[32,256,2,64]{1,3,2,0:T(8,128)} %fusion.88, f32[32,256,2,64]{1,3,2,0:T(8,128)} %fusion.90, f32[32,256,2,64]{1,3,2,0:T(8,128)} %fusion.9, f32[32,256,2,64]{1,3,2,0:T(8,128)} %fusion.93, f32[32,256,2,64]{1,3,2,0:T(8,128)} %fusion.95, ...), kind=kOutput, calls=%fused_computation.57 | convolution fusion | flops 1082130432 | bytes 46268416 | tf_op jit(solution)/shard_map/hoc,bcp->bhop/dot_general | solution.py:28
  375.2 21.2 %psum.56 = f32[4,64]{1,0:T(4,128)S(1)} all-reduce(f32[4,64]{1,0:T(4,128)S(1)} %fusion.146), channel_id=1, replica_groups=mesh['batch'=8,'chan'=4] {'batch'}, use_global_device_ids=true, to_apply=%region_1.2 | all-reduce | flops 256 | bytes 2048 | tf_op jit(solution)/shard_map/psum | solution.py:85
  397.5 17.2 %psum.57 = f32[4,64]{1,0:T(4,128)S(1)} all-reduce(f32[4,64]{1,0:T(4,128)S(1)} %fusion.144), channel_id=1, replica_groups=mesh['batch'=8,'chan'=4] {'batch'}, use_global_device_ids=true, to_apply=%region_3.4 | all-reduce | flops 256 | bytes 2048 | tf_op jit(solution)/shard_map/psum | solution.py:88
  417.9 33.2 %all_gather.27 = bf16[9,2,64,256]{2,1,0,3:T(2,128)(2,1)S(1)} all-gather(bf16[9,2,64,32]{2,1,0,3:T(2,128)(2,1)S(1)} %copy.210), channel_id=1, replica_groups=mesh['batch'=8,'chan'=4] {'batch'}, dimensions={3}, use_global_device_ids=true | all-gather | bytes 663552 | tf_op jit(solution)/shard_map/all_gather | solution.py:136
  454.2 30.5 %all_gather.31 = bf16[64,256]{0,1:T(8,128)(2,1)S(1)} all-gather(bf16[64,32]{0,1:T(8,128)(2,1)S(1)} %copy-done.83), channel_id=1, replica_groups=mesh['batch'=8,'chan'=4] {'batch'}, dimensions={1}, use_global_device_ids=true | all-gather | bytes 36864 | tf_op jit(solution)/shard_map/all_gather | solution.py:138
  509.8 21.1 %pad_slice_fusion.14 = (bf16[32,256,16,16]{1,3,2,0:T(8,128)(2,1)}, bf16[32,256,16,16]{1,3,2,0:T(8,128)(2,1)}, bf16[32,256,16,16]{1,3,2,0:T(8,128)(2,1)}, bf16[32...) fusion(bf16[32,256,16,16]{1,3,2,0:T(8,128)(2,1)} %bitcast.758), kind=kLoop, calls=%fused_computation.30 | loop fusion | bytes 37748736 | tf_op jit(solution)/shard_map/slice | solution.py:16
  580.9 19.6 %psum.58 = f32[4,64]{1,0:T(4,128)} all-reduce(f32[4,64]{1,0:T(4,128)S(1)} %fusion.142), channel_id=1, replica_groups=mesh['batch'=8,'chan'=4] {'batch'}, use_global_device_ids=true, to_apply=%region_5.6 | all-reduce | flops 256 | bytes 2048 | tf_op jit(solution)/shard_map/psum | solution.py:85
  603.5 18.1 %psum.59 = f32[4,64]{1,0:T(4,128)} all-reduce(f32[4,64]{1,0:T(4,128)} %fusion.140), channel_id=1, replica_groups=mesh['batch'=8,'chan'=4] {'batch'}, use_global_device_ids=true, to_apply=%region_7.8 | all-reduce | flops 256 | bytes 2048 | tf_op jit(solution)/shard_map/psum | solution.py:88
  627.2 19.0 %all-reduce.6 = (f32[4,64]{1,0:T(4,128)S(1)}, f32[4,64]{1,0:T(4,128)S(1)}) all-reduce(f32[4,64]{1,0:T(4,128)S(1)} %fusion.137, f32[4,64]{1,0:T(4,128)S(1)} %fusion.138), channel_id=1, replica_groups=mesh['batch'=8,'chan'=4] {'batch'}, use_global_device_ids=true, to_apply=%region_11.12 | all-reduce | flops 512 | bytes 4096 | tf_op jit(solution)/shard_map/psum | solution.py:97
  713.7 23.7 %fusion.16 = bf16[32,256,256]{2,1,0:T(8,128)(2,1)} fusion(f32[32,256,256,1]{1,2,0,3:T(8,128)} %fusion.101, f32[32,256,256,1]{1,2,0,3:T(8,128)} %fusion.105, f32[32,256,256,1]{1,2,0,3:T(8,128)} %fusion.109, f32[32,256,256,1]{1,2,0,3:T(8,128)} %fusion.113, f32[32,256,256,1]{1,2,0,3:T(8,128)} %fusion.117, f32[32,256,256,1]{1,2,0,3:T(8,128)} %fusion.121, ...), kind=kOutput, calls=%fused_computation.51 | convolution fusion | flops 556793856 | bytes 73465856 | tf_op jit(solution)/shard_map/hoc,bhop->bcp/dot_general | solution.py:66
  762.5 14.0 %copy.291 = bf16[32,512,256]{2,1,0:T(8,128)(2,1)} copy(bf16[32,512,256]{1,0,2:T(8,128)(2,1)} %bitcast.729) | data formatting | bytes 16777216 | tf_op jit(solution)/shard_map/reshape | solution.py:16
  786.3 18.0 %all-reduce.5 = (f32[4,64]{1,0:T(4,128)S(1)}, f32[4,64]{1,0:T(4,128)S(1)}) all-reduce(f32[4,64]{1,0:T(4,128)S(1)} %fusion.135, f32[4,64]{1,0:T(4,128)S(1)} %fusion.136), channel_id=1, replica_groups=mesh['batch'=8,'chan'=4] {'batch'}, use_global_device_ids=true, to_apply=%region_16.17 | all-reduce | flops 512 | bytes 4096 | tf_op jit(solution)/shard_map/psum | solution.py:97
  897.7 51.3 %fusion = f32[32,512,256]{1,2,0:T(8,128)} fusion(f32[32,256,512,1]{2,1,0,3:T(8,128)} %fusion.69, f32[32,256,512,1]{2,1,0,3:T(8,128)} %fusion.71, f32[32,256,512,1]{2,1,0,3:T(8,128)} %fusion.73, f32[32,256,512,1]{2,1,0,3:T(8,128)} %fusion.75, f32[32,256,512,1]{2,1,0,3:T(8,128)} %fusion.77, f32[32,256,512,1]{2,1,0,3:T(8,128)} %fusion.79, ...), kind=kOutput, calls=%fused_computation.13 | convolution fusion | flops 1107296256 | bytes 153223168 | tf_op jit(solution)/shard_map/hoc,bhop->bcp/dot_general | solution.py:66
  949.0 20.0 %reshape.259 = f32[32,512,8,2,8,2]{1,5,4,3,2,0:T(2,128)} reshape(f32[32,512,256]{1,2,0:T(8,128)} %fusion) | data formatting | bytes 33554432 | tf_op jit(solution)/shard_map/reshape | solution.py:181
  969.0 15.8 %reduce_sum.134 = bf16[32,512,8,8]{1,3,2,0:T(8,128)(2,1)} reduce(f32[32,512,8,2,8,2]{1,5,4,3,2,0:T(2,128)} %reshape.259, f32[]{:T(128)} %constant.11.clone.1), dimensions={3,5}, to_apply=%region_17.18 | reduce | flops 3145728 | bytes 18874372 | tf_op jit(solution)/shard_map/reduce_sum | solution.py:181
  984.8 15.5 %copy.285 = bf16[32,512,8,8]{0,3,2,1:T(8,128)(2,1)} copy(bf16[32,512,8,8]{1,3,2,0:T(8,128)(2,1)} %reduce_sum.134) | data formatting | bytes 4194304 | tf_op jit(solution)/shard_map/convert_element_type | solution.py:204
  1063.7 22.7 %reduce-scatter.14.cloned.1.call-done = bf16[32,64,128]{0,2,1:T(8,128)(2,1)} async-done(((bf16[32,256,128]{0,2,1:T(8,128)(2,1)}), bf16[32,64,128]{0,2,1:T(8,128)(2,1)}) %reduce-scatter.14.cloned.1.call-update) | async-done | bytes 524304 | tf_op jit(solution)/shard_map/reduce_scatter | solution.py:203
  1089.2 70.0 %reduce-scatter.24.cloned.1.call-done = f32[64,1152]{1,0:T(8,128)} async-done(((f32[512,1152]{1,0:T(8,128)}), f32[64,1152]{1,0:T(8,128)}) %reduce-scatter.24.cloned.1.call-update) | async-done | bytes 294928
  1161.7 61.6 %reduce-scatter.20.cloned.1.call-done = f32[64,32]{0,1:T(8,128)} async-done(((f32[64,256]{0,1:T(8,128)}), f32[64,32]{0,1:T(8,128)}) %reduce-scatter.20.cloned.1.call-update) | async-done | bytes 8208 | tf_op jit(solution)/shard_map/reduce_scatter | solution.py:214
  1223.3 92.2 %reduce-scatter.18.cloned.1.call-done = f32[16,64,128]{2,1,0:T(8,128)} async-done(((f32[16,64,1024]{2,1,0:T(8,128)}), f32[16,64,128]{2,1,0:T(8,128)}) %reduce-scatter.18.cloned.1.call-update) | async-done | bytes 524304 | tf_op jit(solution)/shard_map/reduce_scatter | solution.py:213
  (431 shorter events, 448.9 us)
Async XLA Ops:
  7.2 58.4 %all-gather.9.cloned.1.call-start = ((), (), s32[]{:S(2)}) async-start(), calls=%async_computation.8 | async-start | bytes 2654208 | tf_op jit(solution)/shard_map/all_gather | solution.py:135
  9.1 79.2 %all-gather.7.cloned.1.call-start = ((), (), s32[]{:S(2)}) async-start(), calls=%async_computation.7 | async-start | bytes 2621440 | tf_op jit(solution)/shard_map/all_gather | solution.py:131
  9.8 475.5 %all-gather.13.cloned.1.call-start = ((), (), s32[]{:S(2)}) async-start(), calls=%async_computation.10 | async-start | bytes 1310720 | tf_op jit(solution)/shard_map/all_gather | solution.py:132
  10.6 484.0 %all-gather.15.cloned.1.call-start = ((), (), s32[]{:S(2)}) async-start(), calls=%async_computation.11 | async-start | bytes 2359296 | tf_op jit(solution)/shard_map/all_gather | solution.py:137
  11.2 492.1 %all-gather.11.cloned.1.call-start = ((), (), s32[]{:S(2)}) async-start(), calls=%async_computation.9 | async-start | bytes 5242880 | tf_op jit(solution)/shard_map/all_gather | solution.py:147
  68.9 287.0 %copy-start.41 = (bf16[1,2,64,512]{3,2,1,0:T(8,128)(2,1)}, bf16[1,2,64,512]{3,2,1,0:T(8,128)(2,1)S(1)}, u32[]{:S(2)}) copy-start(bf16[1,2,64,512]{3,2,1,0:T(8,128)(2,1)S(1)} %copy.523) | copy-start | bytes 393220
  69.0 261.6 %copy-start.55 = (bf16[1,2,64,512]{3,2,1,0:T(8,128)(2,1)}, bf16[1,2,64,512]{3,2,1,0:T(8,128)(2,1)S(1)}, u32[]{:S(2)}) copy-start(bf16[1,2,64,512]{3,2,1,0:T(8,128)(2,1)S(1)} %copy.522) | copy-start | bytes 393220
  69.2 256.5 %copy-start.51 = (bf16[1,2,64,512]{3,2,1,0:T(8,128)(2,1)}, bf16[1,2,64,512]{3,2,1,0:T(8,128)(2,1)S(1)}, u32[]{:S(2)}) copy-start(bf16[1,2,64,512]{3,2,1,0:T(8,128)(2,1)S(1)} %copy.521) | copy-start | bytes 393220
  69.4 251.4 %copy-start.47 = (bf16[1,2,64,512]{3,2,1,0:T(8,128)(2,1)}, bf16[1,2,64,512]{3,2,1,0:T(8,128)(2,1)S(1)}, u32[]{:S(2)}) copy-start(bf16[1,2,64,512]{3,2,1,0:T(8,128)(2,1)S(1)} %copy.520) | copy-start | bytes 393220
  69.5 225.5 %copy-start.62 = (bf16[1,2,64,512]{3,2,1,0:T(8,128)(2,1)}, bf16[1,2,64,512]{3,2,1,0:T(8,128)(2,1)S(1)}, u32[]{:S(2)}) copy-start(bf16[1,2,64,512]{3,2,1,0:T(8,128)(2,1)S(1)} %copy.519) | copy-start | bytes 393220
  69.7 245.8 %copy-start.53 = (bf16[1,2,64,512]{3,2,1,0:T(8,128)(2,1)}, bf16[1,2,64,512]{3,2,1,0:T(8,128)(2,1)S(1)}, u32[]{:S(2)}) copy-start(bf16[1,2,64,512]{3,2,1,0:T(8,128)(2,1)S(1)} %copy.518) | copy-start | bytes 393220
  69.9 240.8 %copy-start.49 = (bf16[1,2,64,512]{3,2,1,0:T(8,128)(2,1)}, bf16[1,2,64,512]{3,2,1,0:T(8,128)(2,1)S(1)}, u32[]{:S(2)}) copy-start(bf16[1,2,64,512]{3,2,1,0:T(8,128)(2,1)S(1)} %copy.517) | copy-start | bytes 393220
  70.0 235.8 %copy-start.43 = (bf16[1,2,64,512]{3,2,1,0:T(8,128)(2,1)}, bf16[1,2,64,512]{3,2,1,0:T(8,128)(2,1)S(1)}, u32[]{:S(2)}) copy-start(bf16[1,2,64,512]{3,2,1,0:T(8,128)(2,1)S(1)} %copy.516) | copy-start | bytes 393220
  70.2 265.3 %copy-start.45 = (bf16[1,2,64,512]{3,2,1,0:T(8,128)(2,1)}, bf16[1,2,64,512]{3,2,1,0:T(8,128)(2,1)S(1)}, u32[]{:S(2)}) copy-start(bf16[1,2,64,512]{3,2,1,0:T(8,128)(2,1)S(1)} %copy.515) | copy-start | bytes 393220
  374.3 40.5 %copy-start.93 = (f32[64]{0:T(128)S(1)}, f32[64]{0:T(128)}, u32[]{:S(2)}) copy-start(f32[64]{0:T(128)} %param.21) | copy-start | bytes 772
  374.3 41.9 %copy-start.92 = (f32[64]{0:T(128)S(1)}, f32[64]{0:T(128)}, u32[]{:S(2)}) copy-start(f32[64]{0:T(128)} %param.22) | copy-start | bytes 772
  374.9 77.2 %copy-start = (f32[32,64,256]{2,1,0:T(8,128)}, f32[32,64,256]{2,1,0:T(8,128)S(1)}, u32[]{:S(2)}) copy-start(f32[32,64,256]{2,1,0:T(8,128)S(1)} %get-tuple-element.44) | copy-start | bytes 6291460
  374.9 42.8 %copy-start.74 = (bf16[9,2,64,32]{2,3,1,0:T(8,128)(2,1)S(1)}, bf16[9,2,64,32]{2,3,1,0:T(8,128)(2,1)}, u32[]{:S(2)}) copy-start(bf16[9,2,64,32]{2,3,1,0:T(8,128)(2,1)} %param.18) | copy-start | bytes 221188
  417.7 36.5 %copy-start.83 = (bf16[64,32]{0,1:T(8,128)(2,1)S(1)}, bf16[64,32]{0,1:T(8,128)(2,1)}, u32[]{:S(2)}) copy-start(bf16[64,32]{0,1:T(8,128)(2,1)} %param.20) | copy-start | bytes 12292
  417.7 67.1 %copy-start.94 = (s32[32]{0:T(128)S(1)}, s32[32]{0:T(128)}, u32[]{:S(2)}) copy-start(s32[32]{0:T(128)} %param.15) | copy-start | bytes 388
  417.7 358.8 %reduce-scatter.22.cloned.1.call-start = ((), (), s32[]{:S(2)}) async-start(), calls=%async_computation.17 | async-start | bytes 81920
  452.9 100.9 %copy-start.57 = (bf16[1,2,64,256]{3,2,1,0:T(8,128)(2,1)}, bf16[1,2,64,256]{3,2,1,0:T(8,128)(2,1)S(1)}, u32[]{:S(2)}) copy-start(bf16[1,2,64,256]{3,2,1,0:T(8,128)(2,1)S(1)} %copy.532) | copy-start | bytes 196612
  530.8 26.5 %copy-start.10 = (bf16[32,256,16,16]{1,3,2,0:T(8,128)(2,1)}, bf16[32,256,16,16]{1,3,2,0:T(8,128)(2,1)S(1)}, u32[]{:S(2)}) copy-start(bf16[32,256,16,16]{1,3,2,0:T(8,128)(2,1)S(1)} %get-tuple-element.79) | copy-start | bytes 12582916
  580.0 43.1 %copy-start.40 = (bf16[32,64,256]{2,1,0:T(8,128)(2,1)S(1)}, bf16[32,64,256]{2,1,0:T(8,128)(2,1)}, u32[]{:S(2)}) copy-start(bf16[32,64,256]{2,1,0:T(8,128)(2,1)} %param.25) | copy-start | bytes 3145732
  626.6 23.4 %copy-start.77 = (bf16[32,64]{1,0:T(8,128)(2,1)}, bf16[32,64]{1,0:T(8,128)(2,1)S(1)}, u32[]{:S(2)}) copy-start(bf16[32,64]{1,0:T(8,128)(2,1)S(1)} %multiply_convert_fusion.6) | copy-start | bytes 12292
  649.9 133.3 %reduce-scatter.12.cloned.1.call-start = ((), (), s32[]{:S(2)}) async-start(), calls=%async_computation.12 | async-start | bytes 5242880 | tf_op jit(solution)/shard_map/reduce_scatter | solution.py:172
  737.4 321.5 %all-reduce.9.cloned.1.call-start = ((), (), s32[]{:S(2)}) async-start(), calls=%async_computation.19 | async-start | bytes 4718592
  762.4 298.2 %reduce-scatter.16.cloned.1.call-start = ((), (), s32[]{:S(2)}) async-start(), calls=%async_computation.14 | async-start | bytes 5242880 | tf_op jit(solution)/shard_map/reduce_scatter | solution.py:206
  783.1 303.2 %reduce-scatter.14.cloned.1.call-start = ((), (), s32[]{:S(2)}) async-start(), calls=%async_computation.13 | async-start | bytes 10485760 | tf_op jit(solution)/shard_map/reduce_scatter | solution.py:203
  1016.4 142.9 %reduce-scatter.24.cloned.1.call-start = ((), (), s32[]{:S(2)}) async-start(), calls=%async_computation.18 | async-start | bytes 2654208
  1053.6 169.7 %reduce-scatter.20.cloned.1.call-start = ((), (), s32[]{:S(2)}) async-start(), calls=%async_computation.16 | async-start | bytes 147456 | tf_op jit(solution)/shard_map/reduce_scatter | solution.py:214
  1054.6 260.9 %reduce-scatter.18.cloned.1.call-start = ((), (), s32[]{:S(2)}) async-start(), calls=%async_computation.15 | async-start | bytes 4718592 | tf_op jit(solution)/shard_map/reduce_scatter | solution.py:213
  (102 other events, 721.5 us)
Sparse Core Ops, SparseCore 0:
  10.8 54.7 all-gather.8
  67.1 21.1 all-gather.6
  89.8 16.7 all-gather.12
  108.5 51.0 all-gather.14
  417.8 32.1 all-gather.10
  650.0 15.7 reduce-scatter.21
  737.5 40.8 reduce-scatter.11
  781.9 109.0 all-reduce.8
  893.7 43.5 reduce-scatter.15
  1016.5 69.8 reduce-scatter.13
  1090.3 68.9 reduce-scatter.23
  1163.4 59.8 reduce-scatter.19
  1227.9 87.4 reduce-scatter.17
where the time goes:
time: 1330 us; the launch traced here: 1320 us
  local copies, waits for them, and re-layouts  399 us (30%)
  matrix products  358 us (27%)
  waiting for transfers between devices  321 us (24%)
  blocking collectives  182 us (14%)
  other arithmetic  45.6 us (3%)
  between operations  16.2 us (1%)
    slice x10, local copies, waits for them, and re-layouts, window(): padded[:, :, vertical:vertical + 16, across:across + 16]  191 us
    dot_general x18, matrix products, conv_field_grad(): jnp.einsum('hoc,bhop->bcp', kernel[offset], shifted, preferred_element_ty...  183 us
    dot_general x18, matrix products, conv_forward(): jnp.einsum('hoc,bcp->bhop', kernel[offset], window(padded, offset), prefe...  107 us
    reduce_scatter x1, waiting for transfers between devices, on_device(): lax.psum_scatter(squeezer_grad, 'batch', scatter_dimension=2, tiled=True)  92.2 us
    unnamed x16, waiting for transfers between devices  72.1 us
    reduce_scatter x1, waiting for transfers between devices, on_device(): lax.psum_scatter(exciter_grad, 'batch', scatter_dimension=1, tiled=True)  61.6 us
    unnamed x275, local copies, waits for them, and re-layouts  55.8 us
    all_gather x1, waiting for transfers between devices, on_device(): lax.all_gather(widener, 'batch', axis=3, tiled=True)  54.4 us
  transfers between devices with their start and end apart: 13, of which 6 were waited for; matrix products, arithmetic and copies ran while one was open for 53% of the time, Pallas kernels for 0%

commit v1 on v0

v1 whole, which is shorter than its diff:
```python
import jax
import jax.numpy as jnp
from jax import lax
from jax.experimental import pallas as pl
from jax.experimental.pallas import tpu as pltpu
from jax.sharding import PartitionSpec as P

MB = 4
epsilon = 1e-05
f32 = jnp.float32
bf16 = jnp.bfloat16
MIB = 2**20

NT = (((1,), (1,)), ((), ()))
TN = (((0,), (0,)), ((), ()))


def dot(a, b, dims=None):
    if dims is None:
        return jnp.dot(a, b, preferred_element_type=f32)
    return lax.dot_general(a, b, dims, preferred_element_type=f32)


def call(body, outs, args, name, scratch=(), flops=0, smem=1, limit=48):
    outs = [jax.ShapeDtypeStruct(shape, dtype) for shape, dtype in outs]
    moved = sum(a.size * a.dtype.itemsize for a in args) + sum(
        o.size * o.dtype.itemsize for o in outs
    )
    specs = [pl.BlockSpec(memory_space=pltpu.SMEM)] * smem + [
        pl.BlockSpec(memory_space=pltpu.VMEM)
    ] * (len(args) - smem)
    return pl.pallas_call(
        body,
        out_shape=outs,
        in_specs=specs,
        out_specs=[pl.BlockSpec(memory_space=pltpu.VMEM)] * len(outs),
        scratch_shapes=list(scratch),
        compiler_params=pltpu.CompilerParams(vmem_limit_bytes=limit * MIB),
        cost_estimate=pl.CostEstimate(
            flops=int(flops), bytes_accessed=int(moved), transcendentals=0
        ),
        name=name,
    )(*args)


def iota(shape, dim):
    return lax.broadcasted_iota(jnp.int32, shape, dim)


def onehot(cond):
    return jnp.where(cond, 1.0, 0.0).astype(f32).astype(bf16)


def eye(n):
    return onehot(iota((n, n), 0) == iota((n, n), 1))


def sixteen_swap():
    r, q = iota((256, 256), 0), iota((256, 256), 1)
    return onehot(((r % 16) == (q // 16)) & ((r // 16) == (q % 16)))


def tree(parts):
    parts = list(parts)
    while len(parts) > 1:
        parts = [parts[n] + parts[n + 1] for n in range(0, len(parts), 2)]
    return parts[0]


def pack_body(w, r, e, wout, rout):
    wout[...] = jnp.concatenate([w[:, 0], w[:, 1]], axis=-1)
    slots = [r[q // 2, q % 2] for q in range(18)] + [e[...], jnp.zeros_like(e[...])]
    for row in range(5):
        rout[row] = jnp.concatenate(slots[4 * row : 4 * row + 4], axis=-1)


def widener_body(idx, *refs):
    own, other, out = refs[:8], refs[8:16], refs[16]
    core = idx[2]
    for blocks, side in ((own, core), (other, 1 - core)):
        for half in range(2):
            rows = pl.ds(pl.multiple_of(half * 128 + side * 64, 64), 64)
            lanes = slice(half * 64, half * 64 + 64)
            for group in range(4):
                w = [
                    jnp.concatenate(
                        [blocks[2 * group][t][:, lanes], blocks[2 * group + 1][t][:, lanes]],
                        axis=-1,
                    ).astype(f32)
                    for t in range(9)
                ]
                down = {
                    (0, 0): w[0:3],
                    (0, 1): [w[3 + s] + w[6 + s] for s in range(3)],
                    (1, 0): [w[s] + w[3 + s] for s in range(3)],
                    (1, 1): w[6:9],
                }
                for a in range(2):
                    for u in range(2):
                        d = down[(a, u)]
                        across = {
                            (0, 0): d[0],
                            (0, 1): d[1] + d[2],
                            (1, 0): d[0] + d[1],
                            (1, 1): d[2],
                        }
                        for b in range(2):
                            for v in range(2):
                                out[
                                    a * 8 + b * 4 + u * 2 + v,
                                    rows,
                                    group * 128 : group * 128 + 128,
                                ] = across[(b, v)].astype(bf16)


def refiner_select(base, chip):
    r, q = iota((1024, 1024), 0), iota((1024, 1024), 1)
    channel = ((r // 128) ^ base) * 32 + r % 32
    return onehot((((r // 32) % 4) == (q // 256)) & ((channel ^ (chip * 128)) == (q % 256)))


def refiner_body(idx, *refs):
    own, other, out, ex = refs[:8], refs[8:16], refs[16], refs[17]
    base, core, chip = idx[0], idx[2], idx[3]
    select = refiner_select(base, chip)
    for blocks, side in ((own, core), (other, 1 - core)):
        rows = pl.multiple_of(side * 64, 64)
        raw = jnp.concatenate([blocks[k][...].reshape(320, 128) for k in range(8)], axis=-1)
        got = dot(raw, select).astype(bf16)
        for q in range(18):
            piece = got[(q // 4) * 64 : (q // 4) * 64 + 64, (q % 4) * 256 : (q % 4) * 256 + 256]
            out[q // 2, pl.ds(rows + (q % 2) * 128, 64), :] = piece
        ex[pl.ds(rows, 64), :] = got[256:320, 512:768]


def feature_select(base, place):
    r, q = iota((512, 512), 0), iota((512, 512), 1)
    kept = r % 256
    have = (((kept // 64) ^ place) * 64 + kept % 64) * 2 + r // 256
    want = ((q // 64) ^ base) * 64 + q % 64
    return onehot(have == want)


def feature_body(idx, b0, b1, b2, b3, out, turned):
    ident = eye(128)

    def turn(s, carry):
        x = jnp.concatenate([b0[s], b1[s], b2[s], b3[s]], axis=0)
        t = dot(ident, x, NT).astype(bf16)
        turned[s] = jnp.concatenate([t[:64], t[64:]], axis=-1)
        return carry

    lax.fori_loop(0, 16, turn, 0)
    swap = sixteen_swap()
    select = feature_select(idx[0], idx[1])
    zero = jnp.zeros((10, 16, 512), bf16)
    out[0] = zero
    out[9] = zero
    out[:, 0] = zero
    out[:, 9] = zero
    for block in range(4):
        a = turned[:, block * 16 : block * 16 + 16, :].reshape(256, 512)
        c = dot(dot(swap, a).astype(bf16), select).astype(bf16)
        out[1 + 2 * block : 3 + 2 * block, 1:9] = c.reshape(2, 8, 16, 512)


def input_back_body(idx, d, w, b0, b1, b2, b3, turned):
    swap = sixteen_swap()
    select = feature_select(idx[0], idx[1])

    def block_step(block, carry):
        parts = []
        for a in range(2):
            for b in range(2):
                for u in range(2):
                    for v in range(2):
                        parts.append(
                            d[a, b, pl.ds(2 * block + 2 - u - a, 2), 2 - v - b : 10 - v - b].reshape(
                                256, 256
                            )
                        )
        x = dot(jnp.concatenate(parts, axis=-1), w[...].reshape(4096, 512)).astype(bf16)
        x = dot(x, select, NT).astype(bf16)
        x = dot(swap, x).astype(bf16)
        turned[:, pl.ds(pl.multiple_of(block * 16, 16), 16), :] = x.reshape(16, 16, 512)
        return carry

    lax.fori_loop(0, 4, block_step, 0)
    ident = eye(256)

    def turn(s, carry):
        t = turned[s]
        t = jnp.concatenate([t[:, :256], t[:, 256:]], axis=0)
        o = dot(ident, t, NT).astype(bf16)
        b0[s] = o[0:64]
        b1[s] = o[64:128]
        b2[s] = o[128:192]
        b3[s] = o[192:256]
        return carry

    lax.fori_loop(0, 16, turn, 0)


def upstream_body(idx, own, other, out, turned):
    first = idx[2] == 0
    ident = eye(256)

    def turn(s, carry):
        p, q = own[s], other[s]
        lo = jnp.where(first, p, q)
        hi = jnp.where(first, q, p)
        turned[s] = dot(ident, jnp.concatenate([lo, hi], axis=0), NT).astype(bf16)
        return carry

    lax.fori_loop(0, 16, turn, 0)
    swap = sixteen_swap()

    def mix(y, carry):
        a = turned[:, pl.ds(pl.multiple_of(y * 16, 16), 16), :].reshape(256, 128)
        out[y] = dot(swap, a).astype(bf16).reshape(16, 16, 128)
        return carry

    lax.fori_loop(0, 16, mix, 0)


def over_samples(mask, values):
    return jnp.concatenate(
        [jnp.sum(mask[m] * values, axis=0, keepdims=True) for m in range(MB)], axis=0
    )


def per_sample(mask, rows):
    return sum(mask[m] * rows[m : m + 1] for m in range(MB))


def local_stats(mask, mean_s, squares_s):
    ones = jnp.ones_like(mean_s)
    n = over_samples(mask, ones) * 256.0
    mean = over_samples(mask, mean_s) * 256.0 / jnp.maximum(n, 1.0)
    gap = mean_s - per_sample(mask, mean)
    squares = over_samples(mask, squares_s + 256.0 * gap * gap)
    return n, mean, squares


def total_stats(messages, entries):
    parts = [(g[0:4], g[4:8], g[8:12]) for g in messages]
    mean = tree([n * m for n, m, _ in parts]) / entries
    squares = tree([q + n * (m - mean) * (m - mean) for n, m, q in parts])
    inverse = lax.rsqrt(squares / entries + epsilon)
    return mean, inverse


def message_list(refs):
    return [ref[c] for ref in refs for c in range(ref.shape[0])]


def conv_one_body(x, w, mask, glu, sig, msg):
    total = jnp.zeros((16, 128), f32)
    for a in range(2):
        for b in range(2):
            kept = []
            for u in range(2):
                for v in range(2):
                    kept.append(x[u + a : u + a + 8, v + b : v + b + 8].reshape(1024, 512))
            base = a * 8 + b * 4
            rhs = jnp.concatenate([w[base + n] for n in range(4)], axis=-1)
            c = dot(jnp.concatenate(kept, axis=-1), rhs, NT)
            s = 1.0 / (1.0 + jnp.exp(-c[:, 128:]))
            g = (c[:, :128] * s).reshape(8, 8, 16, 128)
            sig[a, b] = s.reshape(8, 8, 16, 128)
            glu[a, b] = g
            total = total + jnp.sum(g, axis=(0, 1))
    mean_s = total * (1.0 / 256.0)

    def spread(n, acc):
        gap = glu[n // 16, (n // 8) % 2, n % 8] - mean_s[None]
        return acc + jnp.sum(gap * gap, axis=0)

    squares = lax.fori_loop(0, 32, spread, jnp.zeros((16, 128), f32))
    n, mean, squares = local_stats(mask[...], mean_s, squares)
    msg[0:4] = n
    msg[4:8] = mean
    msg[8:12] = squares
    msg[12:16] = jnp.zeros((4, 128), f32)


def make_hidden_body(entries):
    def body(glu, mask, gains, *refs):
        out, stat = refs[-2], refs[-1]
        mean, inverse = total_stats(message_list(refs[:-2]), entries)
        m = mask[...]
        mean_s, inverse_s = per_sample(m, mean), per_sample(m, inverse)
        stat[0] = mean_s
        stat[1] = inverse_s
        gain, shift = gains[0:1], gains[1:2]

        def step(i, carry):
            for a in range(2):
                for b in range(2):
                    h = ((glu[a, b, i] - mean_s) * inverse_s) * gain + shift
                    out[i, a, :, b] = h.astype(bf16)
            return carry

        lax.fori_loop(0, 8, step, 0)

    return body


def conv_two_body(own, other, w, up, mask, pull, held, glu, sig, sums, msg):
    zero = jnp.zeros((18, 16, 256), bf16)
    held[0] = zero
    held[17] = zero
    held[:, 0] = zero
    held[:, 17] = zero
    held[1:17, 1:17, :, 0:128] = own[...]
    held[1:17, 1:17, :, 128:256] = other[...]

    def rows(step, total):
        y = step * 4
        lhs = jnp.concatenate(
            [
                held[pl.ds(y + t // 3, 4), t % 3 : t % 3 + 16].reshape(1024, 256)
                for t in range(9)
            ],
            axis=-1,
        )
        rhs = jnp.concatenate([w[t] for t in range(9)], axis=-1)
        c = dot(lhs, rhs, NT)
        s = 1.0 / (1.0 + jnp.exp(-c[:, 128:]))
        g = (c[:, :128] * s).reshape(4, 16, 16, 128)
        sig[pl.ds(y, 4)] = s.reshape(4, 16, 16, 128)
        glu[pl.ds(y, 4)] = g
        return total + jnp.sum(g, axis=(0, 1))

    total = lax.fori_loop(0, 4, rows, jnp.zeros((16, 128), f32))
    mean_s = total * (1.0 / 256.0)

    def spread(y, acc):
        gap = glu[y] - mean_s[None]
        u = up[y].astype(f32)
        return (
            acc[0] + jnp.sum(gap * gap, axis=0),
            acc[1] + jnp.sum(u, axis=0),
            acc[2] + jnp.sum(u * gap, axis=0),
        )

    none = jnp.zeros((16, 128), f32)
    squares, plain, cross = lax.fori_loop(0, 16, spread, (none, none, none))
    sums[0] = mean_s
    sums[1] = plain
    sums[2] = cross
    m = mask[...]
    n, mean, squares = local_stats(m, mean_s, squares)
    factor = pull[0] * pull[1]
    msg[0:4] = n
    msg[4:8] = mean
    msg[8:12] = squares
    msg[12:16] = over_samples(m, factor * plain)
    msg[16:20] = over_samples(m, factor * (cross + plain * (mean_s - per_sample(m, mean))))
    msg[20:24] = jnp.zeros((4, 128), f32)


def make_back_two_body(entries):
    def body(glu, sig, up, mask, pull, gains, sums, w, *refs):
        grad, own, other, small, stat = refs[-5:]
        messages = message_list(refs[:-5])
        mean, inverse = total_stats(messages, entries)
        plain = tree([g[12:16] for g in messages])
        cross = inverse * tree([g[16:20] + g[12:16] * (g[4:8] - mean) for g in messages])
        m = mask[...]
        mean_s, inverse_s = per_sample(m, mean), per_sample(m, inverse)
        gain, shift = gains[2:3], gains[3:4]
        stat[0] = mean_s
        stat[1] = inverse_s
        weight, gate = pull[0], pull[1]
        centred = sums[2] + sums[1] * (sums[0] - mean_s)
        small[0:16] = weight * (gain * inverse_s * centred + shift * sums[1])
        small[16:17] = jnp.sum(cross, axis=0, keepdims=True)
        small[17:18] = jnp.sum(plain, axis=0, keepdims=True)
        small[18:24] = jnp.zeros((6, 128), f32)
        plain_s = per_sample(m, plain) * (1.0 / entries)
        cross_s = per_sample(m, cross) * (1.0 / entries)
        scale = inverse_s * gain
        factor = weight * gate
        zero = jnp.zeros((18, 16, 256), bf16)
        grad[0] = zero
        grad[17] = zero
        grad[:, 0] = zero
        grad[:, 17] = zero

        def step(y, carry):
            g = glu[y]
            s = sig[y]
            hat = (g - mean_s) * inverse_s
            d = scale * (up[y].astype(f32) * factor - plain_s - hat * cross_s)
            grad[y + 1, 1:17, :, 0:128] = (d * s).astype(bf16)
            grad[y + 1, 1:17, :, 128:256] = (d * g * (1.0 - s)).astype(bf16)
            return carry

        lax.fori_loop(0, 16, step, 0)

        def rows(step, carry):
            y = step * 4
            lhs = jnp.concatenate(
                [
                    grad[pl.ds(y + 2 - t // 3, 4), 2 - t % 3 : 18 - t % 3].reshape(1024, 256)
                    for t in range(9)
                ],
                axis=-1,
            )
            c = dot(lhs, w[...].reshape(2304, 256)).astype(bf16)
            own[pl.ds(y, 4)] = c[:, :128].reshape(4, 16, 16, 128)
            other[pl.ds(y, 4)] = c[:, 128:].reshape(4, 16, 16, 128)
            return carry

        lax.fori_loop(0, 4, rows, 0)

    return body


def output_body(idx, glu, stat, pull, gains, own, other, turned):
    swap = sixteen_swap()
    mean_s, inverse_s = stat[0], stat[1]
    gain, shift = gains[2:3], gains[3:4]
    gate = pull[1]

    def step(y, carry):
        o = (((glu[y] - mean_s) * inverse_s) * gain + shift) * gate
        o = dot(swap, o.astype(bf16).reshape(256, 128)).astype(bf16)
        turned[:, pl.ds(pl.multiple_of(y * 16, 16), 16), :] = o.reshape(16, 16, 128)
        return carry

    lax.fori_loop(0, 16, step, 0)
    ident = eye(128)
    first = idx[2] == 0

    def turn(s, carry):
        t = dot(ident, turned[s], NT).astype(bf16)
        own[s] = jnp.where(first, t[:64], t[64:])
        other[s] = jnp.where(first, t[64:], t[:64])
        return carry

    lax.fori_loop(0, 16, turn, 0)


def refiner_grad_body(idx, grad, held, own, other, work):
    base, core, chip = idx[0], idx[2], idx[3]

    def tap(t, carry):
        d = grad[1:17, 1:17].reshape(4096, 256)
        h = held[pl.ds(t // 3, 16), pl.ds(t % 3, 16)].reshape(4096, 256)
        work[t] = dot(d, h, TN).astype(bf16)
        return carry

    lax.fori_loop(0, 9, tap, 0)
    select = refiner_select(base, chip)
    for out, side in ((own, core), (other, 1 - core)):
        start = pl.multiple_of(side * 64, 64)
        rows = []
        for row in range(5):
            pieces = []
            for q in range(4 * row, 4 * row + 4):
                if q < 18:
                    pieces.append(work[q // 2, pl.ds(start + (q % 2) * 128, 64), :])
                else:
                    pieces.append(jnp.zeros((64, 256), bf16))
            rows.append(jnp.concatenate(pieces, axis=-1))
        got = dot(jnp.concatenate(rows, axis=0), select, NT).astype(bf16)
        for k in range(8):
            out[k] = got[:, k * 128 : k * 128 + 128].reshape(5, 64, 128)


def refiner_sum_body(*refs):
    out = refs[-1]
    total = tree([ref[...].astype(f32) for ref in refs[:-1]])
    for q in range(18):
        out[q // 2, q % 2] = total[q // 4][:, (q % 4) * 32 : (q % 4) * 32 + 32]


def first_sums_body(glu, own, other, mask, stat, msg):
    mean_s, inverse_s = stat[0], stat[1]

    def step(i, acc):
        plain, cross = acc
        for a in range(2):
            for b in range(2):
                d = own[i, a, :, b].astype(f32) + other[i, a, :, b].astype(f32)
                plain = plain + jnp.sum(d, axis=0)
                cross = cross + jnp.sum(d * (glu[a, b, i] - mean_s), axis=0)
        return plain, cross

    none = jnp.zeros((16, 128), f32)
    plain, cross = lax.fori_loop(0, 8, step, (none, none))
    m = mask[...]
    msg[0:4] = over_samples(m, plain)
    msg[4:8] = over_samples(m, cross * inverse_s)


def make_back_one_body(entries):
    def body(glu, sig, own, other, mask, stat, gains, *refs):
        grad, small = refs[-2:]
        messages = message_list(refs[:-2])
        plain = tree([g[0:4] for g in messages])
        cross = tree([g[4:8] for g in messages])
        small[0:1] = jnp.sum(cross, axis=0, keepdims=True)
        small[1:2] = jnp.sum(plain, axis=0, keepdims=True)
        small[2:8] = jnp.zeros((6, 128), f32)
        m = mask[...]
        plain_s = per_sample(m, plain) * (1.0 / entries)
        cross_s = per_sample(m, cross) * (1.0 / entries)
        mean_s, inverse_s = stat[0], stat[1]
        scale = inverse_s * gains[0:1]
        zero = jnp.zeros((10, 16, 256), bf16)
        for a in range(2):
            for b in range(2):
                grad[a, b, 0] = zero
                grad[a, b, 9] = zero
                grad[a, b, :, 0] = zero
                grad[a, b, :, 9] = zero

        def step(i, carry):
            for a in range(2):
                for b in range(2):
                    g = glu[a, b, i]
                    s = sig[a, b, i]
                    hat = (g - mean_s) * inverse_s
                    d = own[i, a, :, b].astype(f32) + other[i, a, :, b].astype(f32)
                    d = scale * (d - plain_s - hat * cross_s)
                    grad[a, b, i + 1, 1:9, :, 0:128] = (d * s).astype(bf16)
                    grad[a, b, i + 1, 1:9, :, 128:256] = (d * g * (1.0 - s)).astype(bf16)
            return carry

        lax.fori_loop(0, 8, step, 0)

    return body


def widener_grad_body(idx, grad, x, own, other, work):
    core = idx[2]

    def phase(n, carry):
        a, b = n // 2, n % 2
        d = grad[a, b, 1:9, 1:9].reshape(1024, 256)
        for u in range(2):
            for v in range(2):
                f = x[pl.ds(u + a, 8), pl.ds(v + b, 8)].reshape(1024, 512)
                work[n, 2 * u + v] = dot(d, f, TN)
        return carry

    lax.fori_loop(0, 4, phase, 0)
    source = {0: (0, 0), 1: (1, 0), 2: (1, 1)}
    for out, side in ((own, core), (other, 1 - core)):
        start = pl.multiple_of(side * 64, 64)
        for pair in range(4):
            lanes = slice(pair * 128, pair * 128 + 128)
            for r in range(3):
                for s in range(3):
                    both = []
                    for half in range(2):
                        rows = pl.ds(start + half * 128, 64)
                        both.append(
                            sum(
                                work[2 * a + b, 2 * source[r][a] + source[s][b], rows, lanes]
                                for a in range(2)
                                for b in range(2)
                            )
                        )
                    first, second = both
                    out[2 * pair, 3 * r + s] = jnp.concatenate(
                        [first[:, :64], second[:, :64]], axis=-1
                    ).astype(bf16)
                    out[2 * pair + 1, 3 * r + s] = jnp.concatenate(
                        [first[:, 64:], second[:, 64:]], axis=-1
                    ).astype(bf16)


def widener_sum_body(*refs):
    out = refs[-1]
    for t in range(9):
        total = tree([ref[t].astype(f32) for ref in refs[:-1]])
        out[t, 0] = total[:, :64]
        out[t, 1] = total[:, 64:]


def swap_with(v, axis, k):
    return lax.ppermute(v, axis, [(n, n ^ k) for n in range(lax.axis_size(axis))])


def on_device(
    features,
    skip_feature,
    section_ids,
    micro_ids,
    widener,
    refiner,
    squeezer,
    exciter,
    gain_one,
    bias_one,
    gain_two,
    bias_two,
    upstream,
):
    nb = lax.axis_size("batch")
    eight = nb == 8
    samples = features.shape[0]
    entries = float(samples * nb // MB * 256)
    i = lax.axis_index("batch")
    j = lax.axis_index("chan")
    core, chip = j % 2, j // 2
    base = i if eight else 0 * i
    idx = jnp.stack([base, j, core, chip]).astype(jnp.int32)

    def half(v, which):
        return lax.dynamic_slice_in_dim(v, which * 16, 16, axis=0)

    def natural(own, other, axis):
        return jnp.where(
            core == 0,
            jnp.concatenate([own, other], axis=axis),
            jnp.concatenate([other, own], axis=axis),
        )

    if eight:
        wide, fine = call(
            pack_body,
            [((9, 64, 128), bf16), ((5, 64, 128), bf16)],
            (widener, refiner, exciter),
            "pack",
            smem=0,
        )
        f_keep, f_send = half(features, core), half(features, 1 - core)
        f_blocks = [f_keep] + [
            swap_with(f_send if k % 2 else f_keep, "chan", k) for k in range(1, 4)
        ]
        wide_own = [wide] + [swap_with(wide, "batch", k) for k in range(1, 8)]
        fine_own = [fine] + [swap_with(fine, "batch", k) for k in range(1, 8)]
    else:
        f_keep, f_send = half(features, core), half(features, 1 - core)
        f_blocks = [f_keep] + [
            swap_with(f_send if k % 2 else f_keep, "chan", k) for k in range(1, 4)
        ]
        w_all = lax.all_gather(widener, "batch", axis=3, tiled=True)
        r_all = lax.all_gather(refiner, "batch", axis=3, tiled=True)
        e_all = lax.all_gather(exciter, "batch", axis=1, tiled=True)
        w_all = w_all.reshape(9, 2, 64, 8, 64).transpose(3, 0, 2, 1, 4).reshape(8, 9, 64, 128)
        r_all = jnp.concatenate(
            [r_all.reshape(18, 64, 256), e_all[None], jnp.zeros((1, 64, 256), bf16)], axis=0
        )
        r_all = r_all.reshape(5, 4, 64, 8, 32).transpose(3, 0, 2, 1, 4).reshape(8, 5, 64, 128)
        wide_own = [w_all[k] for k in range(8)]
        fine_own = [r_all[k] for k in range(8)]
    wide_other = [swap_with(v, "chan", 1) for v in wide_own]
    fine_other = [swap_with(v, "chan", 1) for v in fine_own]

    gains = jnp.stack([gain_one, bias_one, gain_two, bias_two], axis=0)
    gains = natural(gains, swap_with(gains, "chan", 1), 1)
    ids = half(micro_ids, core)
    mask = jnp.broadcast_to(
        (ids[None, :, None] == jnp.arange(MB, dtype=jnp.int32)[:, None, None]).astype(f32),
        (MB, 16, 128),
    )
    weight_of = jnp.where(section_ids == 0, 1.0, jnp.where(section_ids == 1, 2.0, 4.0)).astype(f32)
    weight = jnp.broadcast_to(half(weight_of, core)[:, None], (16, 128))

    def share(msg):
        pair = jnp.stack([msg, swap_with(msg, "chan", 1)], axis=0)
        if eight:
            return [pair] + [swap_with(pair, "batch", k) for k in range(1, 8)]
        rows = lax.all_gather(pair, "batch")
        return [rows.reshape((-1,) + msg.shape)]

    (field,) = call(
        feature_body,
        [((10, 10, 16, 512), bf16)],
        (idx, *f_blocks),
        "features_turned",
        scratch=[pltpu.VMEM((16, 64, 512), bf16)],
        flops=1.4e9,
    )
    (wide_w,) = call(
        widener_body,
        [((16, 256, 512), bf16)],
        (idx, *wide_own, *wide_other),
        "widener_taps",
        flops=1e8,
    )
    glu_one, sig_one, msg_one = call(
        conv_one_body,
        [((2, 2, 8, 8, 16, 128), f32), ((2, 2, 8, 8, 16, 128), f32), ((16, 128), f32)],
        (field, wide_w, mask),
        "conv_one",
        flops=4.3e9,
        smem=0,
    )
    shared_one = share(msg_one)
    hidden, stat_one = call(
        make_hidden_body(entries),
        [((8, 2, 8, 2, 16, 128), bf16), ((2, 16, 128), f32)],
        (glu_one, mask, gains, *shared_one),
        "hidden",
        flops=1e7,
        smem=0,
    )
    hidden = hidden.reshape(16, 16, 16, 128)
    hidden_other = swap_with(hidden, "chan", 2)

    skip_full = lax.all_gather(skip_feature, "chan", axis=1, tiled=True)
    squeezer_full = lax.all_gather(squeezer, "batch", axis=2, tiled=True)
    pooled = skip_full.reshape(samples, -1, 16)
    squeezed = jnp.einsum("toc,bct->bo", squeezer_full, pooled, preferred_element_type=f32)
    squeeze_sig = jax.nn.sigmoid(squeezed)
    swish = (squeezed * squeeze_sig).astype(bf16)
    swish_full = lax.all_gather(swish, "chan", axis=1, tiled=True)
    exciter_full = lax.all_gather(exciter, "batch", axis=1, tiled=True)
    excited = jnp.einsum("oc,bc->bo", exciter_full, swish_full, preferred_element_type=f32)
    gate = jax.nn.sigmoid(excited)
    gate_mine = natural(half(gate, core), swap_with(half(gate, 1 - core), "chan", 1), 1)
    pull = jnp.stack([weight, gate_mine], axis=0)

    u_keep = half(upstream, core)
    u_other = swap_with(half(upstream, 1 - core), "chan", 1)
    (up,) = call(
        upstream_body,
        [((16, 16, 16, 128), bf16)],
        (idx, u_keep, u_other),
        "upstream_turned",
        scratch=[pltpu.VMEM((16, 256, 128), bf16)],
        flops=1.2e9,
    )
    fine_w, _ = call(
        refiner_body,
        [((9, 256, 256), bf16), ((128, 256), bf16)],
        (idx, *fine_own, *fine_other),
        "refiner_taps",
        flops=1.3e9,
    )
    held, glu_two, sig_two, sums_two, msg_two = call(
        conv_two_body,
        [
            ((18, 18, 16, 256), bf16),
            ((16, 16, 16, 128), f32),
            ((16, 16, 16, 128), f32),
            ((3, 16, 128), f32),
            ((24, 128), f32),
        ],
        (hidden, hidden_other, fine_w, up, mask, pull),
        "conv_two",
        flops=4.9e9,
        smem=0,
    )
    shared_two = share(msg_two)
    grad_two, dh_own, dh_send, small_two, stat_two = call(
        make_back_two_body(entries),
        [
            ((18, 18, 16, 256), bf16),
            ((16, 16, 16, 128), bf16),
            ((16, 16, 16, 128), bf16),
            ((24, 128), f32),
            ((2, 16, 128), f32),
        ],
        (glu_two, sig_two, up, mask, pull, gains, sums_two, fine_w, *shared_two),
        "back_two",
        flops=4.9e9,
        smem=0,
    )
    dh_other = swap_with(dh_send, "chan", 2)
    out_own, out_send = call(
        output_body,
        [((16, 64, 256), bf16), ((16, 64, 256), bf16)],
        (idx, glu_two, stat_two, pull, gains),
        "output_turned",
        scratch=[pltpu.VMEM((16, 256, 128), bf16)],
        flops=1.2e9,
    )
    output = natural(out_own, swap_with(out_send, "chan", 1), 0)
    fine_keep, fine_send = call(
        refiner_grad_body,
        [((8, 5, 64, 128), bf16), ((8, 5, 64, 128), bf16)],
        (idx, grad_two, held),
        "refiner_grad",
        scratch=[pltpu.VMEM((9, 256, 256), bf16)],
        flops=6e9,
    )

    def scatter(keep, send, body, shape, name, unpack):
        total = (keep.astype(f32) + swap_with(send, "chan", 1).astype(f32)).astype(bf16)
        if eight:
            parts = [total[0]] + [swap_with(total[k], "batch", k) for k in range(1, 8)]
            return call(body, [(shape, f32)], parts, name, smem=0)[0]
        return unpack(total)

    def unpack_fine(total):
        v = total.reshape(8, 5, 64, 4, 32).transpose(1, 3, 2, 0, 4).reshape(20, 64, 256)[:18]
        v = v.reshape(9, 2, 64, 256).astype(f32)
        return lax.psum_scatter(v, "batch", scatter_dimension=3, tiled=True)

    def unpack_wide(total):
        v = total.reshape(8, 9, 64, 2, 64).transpose(1, 3, 2, 0, 4).reshape(9, 2, 64, 512)
        return lax.psum_scatter(v.astype(f32), "batch", scatter_dimension=3, tiled=True)

    refiner_sum = scatter(
        fine_keep, fine_send, refiner_sum_body, refiner.shape, "refiner_sum", unpack_fine
    )

    by_phase = (8, 2, 8, 2, 16, 128)
    dh_own, dh_other = dh_own.reshape(by_phase), dh_other.reshape(by_phase)
    (msg_three,) = call(
        first_sums_body,
        [((8, 128), f32)],
        (glu_one, dh_own, dh_other, mask, stat_one),
        "first_sums",
        flops=1e7,
        smem=0,
    )
    shared_three = share(msg_three)
    grad_one, small_one = call(
        make_back_one_body(entries),
        [((2, 2, 10, 10, 16, 256), bf16), ((8, 128), f32)],
        (glu_one, sig_one, dh_own, dh_other, mask, stat_one, gains, *shared_three),
        "back_one",
        flops=1e7,
        smem=0,
    )
    wide_keep, wide_send = call(
        widener_grad_body,
        [((8, 9, 64, 128), bf16), ((8, 9, 64, 128), bf16)],
        (idx, grad_one, field),
        "widener_grad",
        scratch=[pltpu.VMEM((4, 4, 256, 512), f32)],
        flops=4.3e9,
    )
    widener_sum = scatter(
        wide_keep, wide_send, widener_sum_body, widener.shape, "widener_sum", unpack_wide
    )
    blocks = call(
        input_back_body,
        [((16, 64, 128), bf16)] * 4,
        (idx, grad_one, wide_w),
        "input_back",
        scratch=[pltpu.VMEM((16, 64, 512), bf16)],
        flops=6e9,
    )
    got = [blocks[0]] + [swap_with(blocks[k], "chan", k) for k in range(1, 4)]
    input_grad = natural(
        got[0].astype(f32) + got[2].astype(f32), got[1].astype(f32) + got[3].astype(f32), 0
    )

    grad_gate = small_two[0:16]
    lo, hi = grad_gate[:, :64], grad_gate[:, 64:]
    keep, send = jnp.where(core == 0, lo, hi), jnp.where(core == 0, hi, lo)
    grad_gate = natural(keep, swap_with(send, "chan", 1), 0)
    grad_excited = (grad_gate * gate * (1.0 - gate)).astype(bf16)
    exciter_grad = jnp.einsum("bo,bc->oc", grad_excited, swish_full, preferred_element_type=f32)
    partial_swish = jnp.einsum("bo,oc->bc", grad_excited, exciter_full, preferred_element_type=f32)
    grad_swish = lax.psum_scatter(
        partial_swish.astype(bf16), "chan", scatter_dimension=1, tiled=True
    ).astype(f32)
    grad_squeezed = (grad_swish * squeeze_sig * (1.0 + squeezed * (1.0 - squeeze_sig))).astype(bf16)
    squeezer_grad = jnp.einsum("bo,bct->toc", grad_squeezed, pooled, preferred_element_type=f32)
    partial_pooled = jnp.einsum(
        "bo,toc->bct", grad_squeezed, squeezer_full, preferred_element_type=f32
    ).reshape(samples, -1, 128)
    skip_grad = lax.psum_scatter(
        partial_pooled.astype(bf16), "chan", scatter_dimension=1, tiled=True
    ).astype(f32)
    squeezer_sum = lax.psum_scatter(squeezer_grad, "batch", scatter_dimension=2, tiled=True)
    exciter_sum = lax.psum_scatter(exciter_grad, "batch", scatter_dimension=1, tiled=True)

    norms = jnp.concatenate([small_one[0:2], small_two[16:18]], axis=0)
    norm_grads = jnp.where(core == 0, norms[:, :64], norms[:, 64:])
    return (
        output,
        input_grad,
        skip_grad,
        widener_sum,
        refiner_sum,
        squeezer_sum,
        exciter_sum,
        norm_grads,
    )


def solution(mesh):
    placed = (
        P("batch", "chan", None),
        P("batch", "chan", None),
        P("batch"),
        P("batch"),
        P(None, None, "chan", "batch"),
        P(None, None, "chan", "batch"),
        P(None, "chan", "batch"),
        P("chan", "batch"),
        P("chan"),
        P("chan"),
        P("chan"),
        P("chan"),
        P("batch", "chan", None),
    )
    return jax.shard_map(
        on_device,
        mesh=mesh,
        in_specs=placed,
        out_specs=(
            P("batch", "chan", None),
            P("batch", "chan", None),
            P("batch", "chan", None),
            P(None, None, "chan", "batch"),
            P(None, None, "chan", "batch"),
            P(None, "chan", "batch"),
            P("chan", "batch"),
            P(None, "chan"),
        ),
        check_vma=False,
    )
```

time: 1330 us -> 477 us (0.36)
  local copies, waits for them, and re-layouts: 399 us -> 39.1 us
  matrix products: 358 us -> 10.8 us
  waiting for transfers between devices: 321 us -> 156 us
  blocking collectives: 182 us -> 43.3 us
  starting transfers between devices: 0.93 us -> 113 us
  Pallas kernels: 0 us -> 93.3 us
  other arithmetic: 45.6 us -> 5.33 us
    dot_general x72 -> x2, matrix products: 356 us -> 6.59 us  [the longest x1 4.01 us: on_device(): jnp.einsum('bo,bct->toc', grad_squeezed, pooled, preferred_element_type=f32)]
    slice x14 -> x2, local copies, waits for them, and re-layouts: 218 us -> 0.01 us  [on_device(): norms = jnp.concatenate([small_one[0:2], small_two[16:18]], axis=0)]
    psum x6 -> x0, blocking collectives: 113 us -> none  [the longest x2 40.8 us: group_stats(): lax.psum(jnp.dot(onehot.T, jnp.sum(values, axis=2), precision=precise), '...]
    ppermute x0 -> x83, starting transfers between devices: none -> 113 us  [swap_with(): lax.ppermute(v, axis, [(n, n ^ k) for n in range(lax.axis_size(axis))])]
    pallas_call x0 -> x17, Pallas kernels: none -> 93.3 us  [call(): pl.pallas_call(body, out_shape=outs, in_specs=specs, out_specs=[pl.BlockS...]
    all_gather x5 -> x2, waiting for transfers between devices: 72.5 us -> 0.01 us  [the longest x1 0.01 us: on_device(): skip_full = lax.all_gather(skip_feature, 'chan', axis=1, tiled=True)]
    reduce_scatter x1, waiting for transfers between devices: 61.6 us -> 0.01 us  [on_device(): lax.psum_scatter(exciter_grad, 'batch', scatter_dimension=1, tiled=True)]
    ppermute x0 -> x83, waiting for transfers between devices: none -> 57 us  [swap_with(): lax.ppermute(v, axis, [(n, n ^ k) for n in range(lax.axis_size(axis))])]
  transfers between devices with their start and end apart: 13 -> 89, of which waited for: 6 -> 24; matrix products, arithmetic and copies ran while one was open for 53% -> 7% of each run, Pallas kernels for 0% -> 15%
where the time goes in v1:
time: 477 us; the launch traced here: 476 us
  waiting for transfers between devices  156 us (33%)
  starting transfers between devices  113 us (24%)
  Pallas kernels  93.3 us (20%)
  blocking collectives  43.3 us (9%)
  local copies, waits for them, and re-layouts  39.1 us (8%)
  between operations  14.6 us (3%)
  matrix products  10.8 us (2%)
  other arithmetic  5.33 us (1%)
    ppermute x83, starting transfers between devices, swap_with(): lax.ppermute(v, axis, [(n, n ^ k) for n in range(lax.axis_size(axis))])  113 us
    pallas_call x17, Pallas kernels, call(): pl.pallas_call(body, out_shape=outs, in_specs=specs, out_specs=[pl.BlockS...  93.3 us
    reduce_scatter x1, waiting for transfers between devices, on_device(): lax.psum_scatter(squeezer_grad, 'batch', scatter_dimension=2, tiled=True)  79.1 us
    ppermute x83, waiting for transfers between devices, swap_with(): lax.ppermute(v, axis, [(n, n ^ k) for n in range(lax.axis_size(axis))])  57 us
    all_gather x1, blocking collectives, on_device(): exciter_full = lax.all_gather(exciter, 'batch', axis=1, tiled=True)  30.8 us
    unnamed x7, waiting for transfers between devices  20.3 us
    unnamed x51, local copies, waits for them, and re-layouts  18.4 us
    all_gather x1, blocking collectives, on_device(): swish_full = lax.all_gather(swish, 'chan', axis=1, tiled=True)  12.5 us
  transfers between devices with their start and end apart: 89, of which 24 were waited for; matrix products, arithmetic and copies ran while one was open for 7% of the time, Pallas kernels for 15%

profile of v1, /device:TPU:0, one launch (start us, length us, event | category | flops | bytes accessed | tf_op | source)
XLA Modules:
  0.0 475.8 jit_solution(16347210360915087704)
XLA Ops:
  12.3 5.6 %collective-permute-start.9 = (bf16[9,64,128]{2,1,0:T(8,128)(2,1)S(1)}, bf16[9,64,128]{2,1,0:T(8,128)(2,1)S(1)}, u32[]{:S(2)}, u32[]{:S(2)}) collective-permute-start(bf16[9,64,128]{2,1,0:T(8,128)(2,1)S(1)} %get-tuple-element.38.refs_0_), channel_id=1, source_target_pairs={{0,28},{4,24},{8,20},{12,16},{16,12},{20,8},{24,4},{28,0},{1,29},{... | collective-permute-start | bytes 442376 | tf_op jit(solution)/shard_map/ppermute | solution.py:586
  25.1 10.9 %collective-permute-start.4 = (bf16[9,64,128]{2,1,0:T(8,128)(2,1)S(1)}, bf16[9,64,128]{2,1,0:T(8,128)(2,1)S(1)}, u32[]{:S(2)}, u32[]{:S(2)}) collective-permute-start(bf16[9,64,128]{2,1,0:T(8,128)(2,1)S(1)} %get-tuple-element.38.refs_0_), channel_id=1, source_target_pairs={{0,8},{4,12},{8,0},{12,4},{16,24},{20,28},{24,16},{28,20},{1,9},{5... | collective-permute-start | bytes 442376 | tf_op jit(solution)/shard_map/ppermute | solution.py:586
  37.5 3.5 collective-permute-done.7.refs_5_
  41.3 5.1 %collective-permute-done.6.refs_4_ = bf16[9,64,128]{2,1,0:T(8,128)(2,1)S(1)} collective-permute-done((bf16[9,64,128]{2,1,0:T(8,128)(2,1)S(1)}, bf16[9,64,128]{2,1,0:T(8,128)(2,1)S(1)}, u32[]{:S(2)}, u32[]{:S(2)}) %collective-permute-start.6) | collective-permute-done | bytes 147488 | tf_op jit(solution)/shard_map/ppermute | solution.py:586
  57.2 3.4 collective-permute-start.34
  62.5 4.6 features_turned.1.x
  68.6 3.5 widener_taps.1.w
  77.9 7.6 %conv_one.1 = (f32[2,2,8,8,16,128]{5,4,3,2,1,0:T(8,128)S(1)}, f32[2,2,8,8,16,128]{5,4,3,2,1,0:T(8,128)S(1)}, f32[16,128]{1,0:T(8,128)S(1)}) custom-call(bf16[10,10,16,512]{3,2,1,0:T(8,128)(2,1)S(1)} %features_turned.1.x, bf16[16,256,512]{2,1,0:T(8,128)(2,1)} %widener_taps.1.w, f32[4,16,128]{2,1,0:T(8,128)S(1)} %broadcast_in_dim.20.mask), custom_call_target="tpu_custom_call" | custom-call | flops 4300000256 | bytes 10067968 | tf_op jit(solution)/shard_map/conv_one/pallas_call | solution.py:32
  86.9 30.8 %all_gather.15 = bf16[64,256]{0,1:T(8,128)(2,1)S(1)} all-gather(bf16[64,32]{0,1:T(8,128)(2,1)S(1)} %copy-done.16), channel_id=1, replica_groups=mesh['batch'=8,'chan'=4] {'batch'}, dimensions={1}, use_global_device_ids=true | all-gather | bytes 36864 | tf_op jit(solution)/shard_map/all_gather | solution.py:715
  126.1 4.4 collective-permute-start.23
  141.3 4.7 copy.35
  146.0 5.2 %copy.36 = bf16[32,1024,16]{1,0,2:T(8,128)(2,1)} copy(bf16[32,1024,16]{0,2,1:T(8,128)(2,1)} %bitcast.90) | data formatting | bytes 2097152 | tf_op jit(solution)/shard_map/reshape | solution.py:710
  153.9 12.5 %all-gather = bf16[4,64,32]{1,2,0:T(8,128)(2,1)S(1)} all-gather(bf16[1,64,32]{1,2,0:T(8,128)(2,1)S(1)} %fusion.9), channel_id=1, replica_groups=mesh['batch'=8,'chan'=4] {'chan'}, dimensions={0}, use_global_device_ids=true | all-gather | bytes 20480 | tf_op jit(solution)/shard_map/all_gather | solution.py:714
  167.1 7.1 %upstream_turned.1.up = bf16[16,16,16,128]{3,2,1,0:T(8,128)(2,1)S(1)} custom-call(s32[4]{0:T(128)S(1)} %pad_add_fusion.idx, bf16[16,64,256]{2,1,0:T(8,128)(2,1)S(1)} %get-tuple-element.101.own, bf16[16,64,256]{2,1,0:T(8,128)(2,1)} %collective-permute-done.43.other), custom_call_target="tpu_custom_call" | custom-call | flops 1200000000 | bytes 2097168 | tf_op jit(solution)/shard_map/upstream_turned/pallas_call | solution.py:32
  174.4 11.2 %conv_two.1 = (bf16[18,18,16,256]{3,2,1,0:T(8,128)(2,1)}, f32[16,16,16,128]{3,2,1,0:T(8,128)}, f32[16,16,16,128]{3,2,1,0:T(8,128)}, f32[3,16,128]{2,1,0:T(8,128)S(1)}, f32[24,128]{1,0:T(8,128)S(1)}) custom-call(bf16[16,16,16,128]{3,2,1,0:T(8,128)(2,1)} %bitcast.10.own, bf16[16,16,16,128]{3,2,1,0:T(8,128)(2,1)} %collective-permute-done.27.other, ...), custom_call_target="tpu_custom_call" | custom-call | flops 4899999744 | bytes 11259904 | tf_op jit(solution)/shard_map/conv_two/pallas_call | solution.py:32
  190.0 4.4 collective-permute-start.49
  199.7 10.4 %back_two.1 = (bf16[18,18,16,256]{3,2,1,0:T(8,128)(2,1)}, bf16[16,16,16,128]{3,2,1,0:T(8,128)(2,1)S(1)}, bf16[16,16,16,128]{3,2,1,0:T(8,128)(2,1)S(1)}, f32[24,128]{1,0:T(8,128)S(1)}, f32[2,16,128]{2,1,0:T(8,128)S(1)}) custom-call(f32[16,16,16,128]{3,2,1,0:T(8,128)} %get-tuple-element.44.glu, f32[16,16,16,128]{3,2,1,0:T(8,128)} %get-tuple-element.45.sig, ...), custom_call_target="tpu_custom_call" | custom-call | flops 4899999744 | bytes 11474944 | tf_op jit(solution)/shard_map/back_two/pallas_call | solution.py:32
  213.3 18.8 %reduce-scatter.13.cloned.1.call-done = bf16[64,32]{1,0:T(8,128)(2,1)} async-done(((bf16[256,32]{1,0:T(8,128)(2,1)}), bf16[64,32]{1,0:T(8,128)(2,1)}) %reduce-scatter.13.cloned.1.call-update) | async-done | bytes 4112
  235.9 5.8 %copy.38 = bf16[32,1024,16]{0,2,1:T(8,128)(2,1)} copy(bf16[32,1024,16]{1,0,2:T(8,128)(2,1)} %fusion) | data formatting | bytes 2097152 | tf_op jit(solution)/shard_map/convert_element_type | solution.py:865
  243.0 4.0 convolution_bitcast_fusion
  249.1 11.0 %refiner_grad.1 = (bf16[8,5,64,128]{3,2,1,0:T(8,128)(2,1)S(1)}, bf16[8,5,64,128]{3,2,1,0:T(8,128)(2,1)S(1)}) custom-call(s32[4]{0:T(128)S(1)} %pad_add_fusion.idx, bf16[18,18,16,256]{3,2,1,0:T(8,128)(2,1)S(1)} %copy-done.15, bf16[18,18,16,256]{3,2,1,0:T(8,128)(2,1)} %get-tuple-element.64.held), custom_call_target="tpu_custom_call" | custom-call | flops 6000000000 | bytes 6619152 | tf_op jit(solution)/shard_map/refiner_grad/pallas_call | solution.py:32
  260.2 22.3 %collective-permute-done.54 = bf16[16,16,16,128]{3,2,1,0:T(8,128)(2,1)S(1)} collective-permute-done((bf16[16,16,16,128]{3,2,1,0:T(8,128)(2,1)}, bf16[16,16,16,128]{3,2,1,0:T(8,128)(2,1)S(1)}, u32[]{:S(2)}, u32[]{:S(2)}) %collective-permute-start.54) | collective-permute-done | bytes 1048608 | tf_op jit(solution)/shard_map/ppermute | solution.py:586
  284.3 4.2 collective-permute-start.62
  289.0 6.3 %output_turned.1 = (bf16[16,64,256]{2,1,0:T(8,128)(2,1)S(1)}, bf16[16,64,256]{2,1,0:T(8,128)(2,1)S(1)}) custom-call(s32[4]{0:T(128)S(1)} %pad_add_fusion.idx, f32[16,16,16,128]{3,2,1,0:T(8,128)S(1)} %copy-done.10, f32[2,16,128]{2,1,0:T(8,128)S(1)} %get-tuple-element.48.stat, f32[2,16,128]{2,1,0:T(8,128)S(1)} %pad_maximum_fusion.2.pull, ...), custom_call_target="tpu_custom_call" | custom-call | flops 1200000000 | bytes 3180560 | tf_op jit(solution)/shard_map/output_turned/pallas_call | solution.py:32
  304.9 4.6 back_one.1
  309.5 8.9 %widener_grad.1 = (bf16[8,9,64,128]{3,2,1,0:T(8,128)(2,1)S(1)}, bf16[8,9,64,128]{3,2,1,0:T(8,128)(2,1)S(1)}) custom-call(s32[4]{0:T(128)S(1)} %pad_add_fusion.idx, bf16[2,2,10,10,16,256]{5,4,3,2,1,0:T(8,128)(2,1)} %get-tuple-element.55.d.grad, bf16[10,10,16,512]{3,2,1,0:T(8,128)(2,1)S(1)} %copy-done.12), custom_call_target="tpu_custom_call" | custom-call | flops 4300000256 | bytes 7274512 | tf_op jit(solution)/shard_map/widener_grad/pallas_call | solution.py:32
  318.6 3.4 collective-permute-start.82
  329.1 4.8 %collective-permute-start.77 = (bf16[5,64,128]{2,1,0:T(8,128)(2,1)S(1)}, bf16[5,64,128]{2,1,0:T(8,128)(2,1)S(1)}, u32[]{:S(2)}, u32[]{:S(2)}) collective-permute-start(bf16[5,64,128]{2,1,0:T(8,128)(2,1)S(1)} %get-tuple-element.107), channel_id=1, source_target_pairs={{0,8},{4,12},{8,0},{12,4},{16,24},{20,28},{24,16},{28,20},{1,9},{5... | collective-permute-start | bytes 245768 | tf_op jit(solution)/shard_map/ppermute | solution.py:586
  343.5 12.1 %input_back.1 = (bf16[16,64,128]{2,1,0:T(8,128)(2,1)S(1)}, bf16[16,64,128]{2,1,0:T(8,128)(2,1)S(1)}, bf16[16,64,128]{2,1,0:T(8,128)(2,1)S(1)}, bf16[16,64,128]{2,1,0:T(8,128)(2,1)S(1)}) custom-call(s32[4]{0:T(128)S(1)} %pad_add_fusion.idx, bf16[2,2,10,10,16,256]{5,4,3,2,1,0:T(8,128)(2,1)S(1)} %copy-done.2, bf16[16,256,512]{2,1,0:T(8,128)(2,1)} %widener_taps.1.w), custom_call_target="tpu_custom_call" | custom-call | flops 6000000000 | bytes 8519696 | tf_op jit(solution)/shard_map/input_back/pallas_call | solution.py:32
  365.0 3.8 collective-permute-start.71
  370.4 9.1 %collective-permute-start.69 = (bf16[9,64,128]{2,1,0:T(8,128)(2,1)S(1)}, bf16[9,64,128]{2,1,0:T(8,128)(2,1)S(1)}, u32[]{:S(2)}, u32[]{:S(2)}) collective-permute-start(bf16[9,64,128]{2,1,0:T(8,128)(2,1)S(1)} %get-tuple-element.97), channel_id=1, source_target_pairs={{0,8},{4,12},{8,0},{12,4},{16,24},{20,28},{24,16},{28,20},{1,9},{5... | collective-permute-start | bytes 442376 | tf_op jit(solution)/shard_map/ppermute | solution.py:586
  389.8 79.1 %reduce-scatter.9.cloned.1.call-done = f32[16,64,128]{2,1,0:T(8,128)} async-done(((f32[16,64,1024]{2,1,0:T(8,128)}), f32[16,64,128]{2,1,0:T(8,128)}) %reduce-scatter.9.cloned.1.call-update) | async-done | bytes 524304 | tf_op jit(solution)/shard_map/reduce_scatter | solution.py:867
  (264 shorter events, 128.1 us)
Async XLA Ops:
  7.2 134.1 %all-gather.4.cloned.1.call-start = ((), (), s32[]{:S(2)}) async-start(), calls=%async_computation.4 | async-start | bytes 1310720 | tf_op jit(solution)/shard_map/all_gather | solution.py:708
  7.9 143.4 %all-gather.6.cloned.1.call-start = ((), (), s32[]{:S(2)}) async-start(), calls=%async_computation.5 | async-start | bytes 2359296 | tf_op jit(solution)/shard_map/all_gather | solution.py:709
  8.7 223.4 %reduce-scatter.13.cloned.1.call-start = ((), (), s32[]{:S(2)}) async-start(), calls=%async_computation.9 | async-start | bytes 81920
  18.0 18.0 %collective-permute-start.8 = (bf16[9,64,128]{2,1,0:T(8,128)(2,1)S(1)}, bf16[9,64,128]{2,1,0:T(8,128)(2,1)S(1)}, u32[]{:S(2)}, u32[]{:S(2)}) collective-permute-start(bf16[9,64,128]{2,1,0:T(8,128)(2,1)S(1)} %get-tuple-element.38.refs_0_), channel_id=1, source_target_pairs={{0,24},{4,28},{8,16},{12,20},{16,8},{20,12},{24,0},{28,4},{1,25},{... | collective-permute-start | bytes 442376 | tf_op jit(solution)/shard_map/ppermute | solution.py:586
  18.2 22.8 %collective-permute-start.7 = (bf16[9,64,128]{2,1,0:T(8,128)(2,1)S(1)}, bf16[9,64,128]{2,1,0:T(8,128)(2,1)S(1)}, u32[]{:S(2)}, u32[]{:S(2)}) collective-permute-start(bf16[9,64,128]{2,1,0:T(8,128)(2,1)S(1)} %get-tuple-element.38.refs_0_), channel_id=1, source_target_pairs={{0,20},{4,16},{8,28},{12,24},{16,4},{20,0},{24,12},{28,8},{1,21},{... | collective-permute-start | bytes 442376 | tf_op jit(solution)/shard_map/ppermute | solution.py:586
  18.9 27.5 %collective-permute-start.6 = (bf16[9,64,128]{2,1,0:T(8,128)(2,1)S(1)}, bf16[9,64,128]{2,1,0:T(8,128)(2,1)S(1)}, u32[]{:S(2)}, u32[]{:S(2)}) collective-permute-start(bf16[9,64,128]{2,1,0:T(8,128)(2,1)S(1)} %get-tuple-element.38.refs_0_), channel_id=1, source_target_pairs={{0,16},{4,20},{8,24},{12,28},{16,0},{20,4},{24,8},{28,12},{1,17},{... | collective-permute-start | bytes 442376 | tf_op jit(solution)/shard_map/ppermute | solution.py:586
  21.7 24.7 %collective-permute-start.5 = (bf16[9,64,128]{2,1,0:T(8,128)(2,1)S(1)}, bf16[9,64,128]{2,1,0:T(8,128)(2,1)S(1)}, u32[]{:S(2)}, u32[]{:S(2)}) collective-permute-start(bf16[9,64,128]{2,1,0:T(8,128)(2,1)S(1)} %get-tuple-element.38.refs_0_), channel_id=1, source_target_pairs={{0,12},{4,8},{8,4},{12,0},{16,28},{20,24},{24,20},{28,16},{1,13},{... | collective-permute-start | bytes 442376 | tf_op jit(solution)/shard_map/ppermute | solution.py:586
  25.1 23.1 %collective-permute-start.4 = (bf16[9,64,128]{2,1,0:T(8,128)(2,1)S(1)}, bf16[9,64,128]{2,1,0:T(8,128)(2,1)S(1)}, u32[]{:S(2)}, u32[]{:S(2)}) collective-permute-start(bf16[9,64,128]{2,1,0:T(8,128)(2,1)S(1)} %get-tuple-element.38.refs_0_), channel_id=1, source_target_pairs={{0,8},{4,12},{8,0},{12,4},{16,24},{20,28},{24,16},{28,20},{1,9},{5... | collective-permute-start | bytes 442376 | tf_op jit(solution)/shard_map/ppermute | solution.py:586
  56.7 18.2 %collective-permute-start.35 = (bf16[5,64,128]{2,1,0:T(8,128)(2,1)}, bf16[5,64,128]{2,1,0:T(8,128)(2,1)S(1)}, u32[]{:S(2)}, u32[]{:S(2)}) collective-permute-start(bf16[5,64,128]{2,1,0:T(8,128)(2,1)} %copy-done.8), channel_id=1, source_target_pairs={{0,1},{1,0},{2,3},{3,2},{4,5},{5,4},{6,7},{7,6},{8,9},{9,8},{10,11... | collective-permute-start | bytes 245768 | tf_op jit(solution)/shard_map/ppermute | solution.py:586
  57.2 18.9 %collective-permute-start.34 = (bf16[5,64,128]{2,1,0:T(8,128)(2,1)}, bf16[5,64,128]{2,1,0:T(8,128)(2,1)S(1)}, u32[]{:S(2)}, u32[]{:S(2)}) collective-permute-start(bf16[5,64,128]{2,1,0:T(8,128)(2,1)} %copy-done.8), channel_id=1, source_target_pairs={{0,28},{4,24},{8,20},{12,16},{16,12},{20,8},{24,4},{28,0},{1,29},{... | collective-permute-start | bytes 245768 | tf_op jit(solution)/shard_map/ppermute | solution.py:586
  67.1 19.8 %collective-permute-start.33 = (bf16[5,64,128]{2,1,0:T(8,128)(2,1)S(1)}, bf16[5,64,128]{2,1,0:T(8,128)(2,1)S(1)}, u32[]{:S(2)}, u32[]{:S(2)}) collective-permute-start(bf16[5,64,128]{2,1,0:T(8,128)(2,1)S(1)} %copy-done.9), channel_id=1, source_target_pairs={{0,24},{4,28},{8,16},{12,20},{16,8},{20,12},{24,0},{28,4},{1,25},{... | collective-permute-start | bytes 245768 | tf_op jit(solution)/shard_map/ppermute | solution.py:586
  68.5 49.2 %collective-permute-start.32 = (bf16[5,64,128]{2,1,0:T(8,128)(2,1)S(1)}, bf16[5,64,128]{2,1,0:T(8,128)(2,1)S(1)}, u32[]{:S(2)}, u32[]{:S(2)}) collective-permute-start(bf16[5,64,128]{2,1,0:T(8,128)(2,1)S(1)} %copy-done.9), channel_id=1, source_target_pairs={{0,20},{4,16},{8,28},{12,24},{16,4},{20,0},{24,12},{28,8},{1,21},{... | collective-permute-start | bytes 245768 | tf_op jit(solution)/shard_map/ppermute | solution.py:586
  72.1 45.6 %collective-permute-start.31 = (bf16[5,64,128]{2,1,0:T(8,128)(2,1)S(1)}, bf16[5,64,128]{2,1,0:T(8,128)(2,1)S(1)}, u32[]{:S(2)}, u32[]{:S(2)}) collective-permute-start(bf16[5,64,128]{2,1,0:T(8,128)(2,1)S(1)} %copy-done.9), channel_id=1, source_target_pairs={{0,16},{4,20},{8,24},{12,28},{16,0},{20,4},{24,8},{28,12},{1,17},{... | collective-permute-start | bytes 245768 | tf_op jit(solution)/shard_map/ppermute | solution.py:586
  74.9 42.9 %collective-permute-start.30 = (bf16[5,64,128]{2,1,0:T(8,128)(2,1)S(1)}, bf16[5,64,128]{2,1,0:T(8,128)(2,1)S(1)}, u32[]{:S(2)}, u32[]{:S(2)}) collective-permute-start(bf16[5,64,128]{2,1,0:T(8,128)(2,1)S(1)} %copy-done.9), channel_id=1, source_target_pairs={{0,12},{4,8},{8,4},{12,0},{16,28},{20,24},{24,20},{28,16},{1,13},{... | collective-permute-start | bytes 245768 | tf_op jit(solution)/shard_map/ppermute | solution.py:586
  76.0 42.2 %collective-permute-start.29 = (bf16[5,64,128]{2,1,0:T(8,128)(2,1)S(1)}, bf16[5,64,128]{2,1,0:T(8,128)(2,1)S(1)}, u32[]{:S(2)}, u32[]{:S(2)}) collective-permute-start(bf16[5,64,128]{2,1,0:T(8,128)(2,1)S(1)} %copy-done.9), channel_id=1, source_target_pairs={{0,8},{4,12},{8,0},{12,4},{16,24},{20,28},{24,16},{28,20},{1,9},{5... | collective-permute-start | bytes 245768 | tf_op jit(solution)/shard_map/ppermute | solution.py:586
  86.9 31.4 %collective-permute-start.19 = (f32[16,128]{1,0:T(8,128)S(1)}, f32[16,128]{1,0:T(8,128)S(1)}, u32[]{:S(2)}, u32[]{:S(2)}) collective-permute-start(f32[16,128]{1,0:T(8,128)S(1)} %get-tuple-element.40), channel_id=1, source_target_pairs={{0,1},{1,0},{2,3},{3,2},{4,5},{5,4},{6,7},{7,6},{8,9},{9,8},{10,11... | collective-permute-start | bytes 24584 | tf_op jit(solution)/shard_map/ppermute | solution.py:586
  137.8 29.3 %collective-permute-start.43 = (bf16[16,64,256]{2,1,0:T(8,128)(2,1)}, bf16[16,64,256]{2,1,0:T(8,128)(2,1)}, u32[]{:S(2)}, u32[]{:S(2)}) collective-permute-start(bf16[16,64,256]{2,1,0:T(8,128)(2,1)} %get-tuple-element.100), channel_id=1, source_target_pairs={{0,1},{1,0},{2,3},{3,2},{4,5},{5,4},{6,7},{7,6},{8,9},{9,8},{10,11... | collective-permute-start | bytes 1572872 | tf_op jit(solution)/shard_map/ppermute | solution.py:586
  139.2 35.2 %collective-permute-start.27 = (bf16[16,16,16,128]{3,2,1,0:T(8,128)(2,1)}, bf16[16,16,16,128]{3,2,1,0:T(8,128)(2,1)}, u32[]{:S(2)}, u32[]{:S(2)}) collective-permute-start(bf16[16,16,16,128]{3,2,1,0:T(8,128)(2,1)} %bitcast.10.own), channel_id=1, source_target_pairs={{0,2},{1,3},{2,0},{3,1},{4,6},{5,7},{6,4},{7,5},{8,10},{9,11},{10,... | collective-permute-start | bytes 3145736 | tf_op jit(solution)/shard_map/ppermute | solution.py:586
  213.2 169.5 %reduce-scatter.7.cloned.1.call-start = ((), (), s32[]{:S(2)}) async-start(), calls=%async_computation.6 | async-start | bytes 5242880 | tf_op jit(solution)/shard_map/reduce_scatter | solution.py:864
  241.8 148.0 %reduce-scatter.11.cloned.1.call-start = ((), (), s32[]{:S(2)}) async-start(), calls=%async_computation.8 | async-start | bytes 147456 | tf_op jit(solution)/shard_map/reduce_scatter | solution.py:868
  242.7 226.2 %reduce-scatter.9.cloned.1.call-start = ((), (), s32[]{:S(2)}) async-start(), calls=%async_computation.7 | async-start | bytes 4718592 | tf_op jit(solution)/shard_map/reduce_scatter | solution.py:867
  247.0 35.4 %collective-permute-start.54 = (bf16[16,16,16,128]{3,2,1,0:T(8,128)(2,1)}, bf16[16,16,16,128]{3,2,1,0:T(8,128)(2,1)S(1)}, u32[]{:S(2)}, u32[]{:S(2)}) collective-permute-start(bf16[16,16,16,128]{3,2,1,0:T(8,128)(2,1)} %copy-done.3), channel_id=1, source_target_pairs={{0,2},{1,3},{2,0},{3,1},{4,6},{5,7},{6,4},{7,5},{8,10},{9,11},{10,... | collective-permute-start | bytes 3145736 | tf_op jit(solution)/shard_map/ppermute | solution.py:586
  260.1 38.2 %collective-permute-start.75 = (bf16[8,5,64,128]{3,2,1,0:T(8,128)(2,1)S(1)}, bf16[8,5,64,128]{3,2,1,0:T(8,128)(2,1)S(1)}, u32[]{:S(2)}, u32[]{:S(2)}) collective-permute-start(bf16[8,5,64,128]{3,2,1,0:T(8,128)(2,1)S(1)} %get-tuple-element.66), channel_id=1, source_target_pairs={{0,1},{1,0},{2,3},{3,2},{4,5},{5,4},{6,7},{7,6},{8,9},{9,8},{10,11... | collective-permute-start | bytes 1966088 | tf_op jit(solution)/shard_map/ppermute | solution.py:586
  284.3 15.9 %collective-permute-start.62 = (f32[2,8,128]{2,1,0:T(8,128)S(1)}, f32[2,8,128]{2,1,0:T(8,128)S(1)}, u32[]{:S(2)}, u32[]{:S(2)}) collective-permute-start(f32[2,8,128]{2,1,0:T(8,128)S(1)} %pad_maximum_fusion.3.refs_0_), channel_id=1, source_target_pairs={{0,28},{4,24},{8,20},{12,16},{16,12},{20,8},{24,4},{28,0},{1,29},{... | collective-permute-start | bytes 24584 | tf_op jit(solution)/shard_map/ppermute | solution.py:586
  302.1 21.4 %collective-permute-start.53 = (bf16[16,64,256]{2,1,0:T(8,128)(2,1)S(1)}, bf16[16,64,256]{2,1,0:T(8,128)(2,1)S(1)}, u32[]{:S(2)}, u32[]{:S(2)}) collective-permute-start(bf16[16,64,256]{2,1,0:T(8,128)(2,1)S(1)} %get-tuple-element.50), channel_id=1, source_target_pairs={{0,1},{1,0},{2,3},{3,2},{4,5},{5,4},{6,7},{7,6},{8,9},{9,8},{10,11... | collective-permute-start | bytes 1572872 | tf_op jit(solution)/shard_map/ppermute | solution.py:586
  318.4 40.0 %collective-permute-start.67 = (bf16[8,9,64,128]{3,2,1,0:T(8,128)(2,1)S(1)}, bf16[8,9,64,128]{3,2,1,0:T(8,128)(2,1)}, u32[]{:S(2)}, u32[]{:S(2)}) collective-permute-start(bf16[8,9,64,128]{3,2,1,0:T(8,128)(2,1)S(1)} %get-tuple-element.62), channel_id=1, source_target_pairs={{0,1},{1,0},{2,3},{3,2},{4,5},{5,4},{6,7},{7,6},{8,9},{9,8},{10,11... | collective-permute-start | bytes 3538952 | tf_op jit(solution)/shard_map/ppermute | solution.py:586
  323.5 14.3 %collective-permute-start.79 = (bf16[5,64,128]{2,1,0:T(8,128)(2,1)S(1)}, bf16[5,64,128]{2,1,0:T(8,128)(2,1)S(1)}, u32[]{:S(2)}, u32[]{:S(2)}) collective-permute-start(bf16[5,64,128]{2,1,0:T(8,128)(2,1)S(1)} %get-tuple-element.105), channel_id=1, source_target_pairs={{0,16},{4,20},{8,24},{12,28},{16,0},{20,4},{24,8},{28,12},{1,17},{... | collective-permute-start | bytes 245768 | tf_op jit(solution)/shard_map/ppermute | solution.py:586
  363.4 16.1 %collective-permute-start.73 = (bf16[9,64,128]{2,1,0:T(8,128)(2,1)S(1)}, bf16[9,64,128]{2,1,0:T(8,128)(2,1)S(1)}, u32[]{:S(2)}, u32[]{:S(2)}) collective-permute-start(bf16[9,64,128]{2,1,0:T(8,128)(2,1)S(1)} %get-tuple-element.93), channel_id=1, source_target_pairs={{0,24},{4,28},{8,16},{12,20},{16,8},{20,12},{24,0},{28,4},{1,25},{... | collective-permute-start | bytes 442376 | tf_op jit(solution)/shard_map/ppermute | solution.py:586
  365.0 20.9 %collective-permute-start.72 = (bf16[9,64,128]{2,1,0:T(8,128)(2,1)}, bf16[9,64,128]{2,1,0:T(8,128)(2,1)S(1)}, u32[]{:S(2)}, u32[]{:S(2)}) collective-permute-start(bf16[9,64,128]{2,1,0:T(8,128)(2,1)} %get-tuple-element.94), channel_id=1, source_target_pairs={{0,20},{4,16},{8,28},{12,24},{16,4},{20,0},{24,12},{28,8},{1,21},{... | collective-permute-start | bytes 442376 | tf_op jit(solution)/shard_map/ppermute | solution.py:586
  365.0 23.1 %collective-permute-start.71 = (bf16[9,64,128]{2,1,0:T(8,128)(2,1)}, bf16[9,64,128]{2,1,0:T(8,128)(2,1)S(1)}, u32[]{:S(2)}, u32[]{:S(2)}) collective-permute-start(bf16[9,64,128]{2,1,0:T(8,128)(2,1)} %get-tuple-element.95), channel_id=1, source_target_pairs={{0,16},{4,20},{8,24},{12,28},{16,0},{20,4},{24,8},{28,12},{1,17},{... | collective-permute-start | bytes 442376 | tf_op jit(solution)/shard_map/ppermute | solution.py:586
  368.8 19.3 %collective-permute-start.70 = (bf16[9,64,128]{2,1,0:T(8,128)(2,1)}, bf16[9,64,128]{2,1,0:T(8,128)(2,1)S(1)}, u32[]{:S(2)}, u32[]{:S(2)}) collective-permute-start(bf16[9,64,128]{2,1,0:T(8,128)(2,1)} %get-tuple-element.96), channel_id=1, source_target_pairs={{0,12},{4,8},{8,4},{12,0},{16,28},{20,24},{24,20},{28,16},{1,13},{... | collective-permute-start | bytes 442376 | tf_op jit(solution)/shard_map/ppermute | solution.py:586
  370.4 18.4 %collective-permute-start.69 = (bf16[9,64,128]{2,1,0:T(8,128)(2,1)S(1)}, bf16[9,64,128]{2,1,0:T(8,128)(2,1)S(1)}, u32[]{:S(2)}, u32[]{:S(2)}) collective-permute-start(bf16[9,64,128]{2,1,0:T(8,128)(2,1)S(1)} %get-tuple-element.97), channel_id=1, source_target_pairs={{0,8},{4,12},{8,0},{12,4},{16,24},{20,28},{24,16},{28,20},{1,9},{5... | collective-permute-start | bytes 442376 | tf_op jit(solution)/shard_map/ppermute | solution.py:586
  (79 other events, 690.5 us)
Sparse Core Ops, SparseCore 0:
  9.6 19.4 all-gather.3
  31.1 63.5 all-gather.5
  213.4 18.6 reduce-scatter.12
  241.9 53.7 reduce-scatter.6
  299.4 65.9 reduce-scatter.10
  369.5 99.3 reduce-scatter.8

commit v2 on v1

v2 whole, which is shorter than its diff:
```python
import jax
import jax.numpy as jnp
from jax import lax
from jax.experimental import pallas as pl
from jax.experimental.pallas import tpu as pltpu
from jax.sharding import PartitionSpec as P

MB = 4
epsilon = 1e-05
f32 = jnp.float32
bf16 = jnp.bfloat16
MIB = 2**20

NT = (((1,), (1,)), ((), ()))
TN = (((0,), (0,)), ((), ()))


def dot(a, b, dims=None):
    if dims is None:
        return jnp.dot(a, b, preferred_element_type=f32)
    return lax.dot_general(a, b, dims, preferred_element_type=f32)


class Traffic:
    def __init__(self, ins, outs, in_sems, out_sems, late):
        self.ins = [
            pltpu.make_async_copy(src, dst, in_sems.at[k]) for k, (src, dst) in enumerate(ins)
        ]
        self.outs, self.out_sems = outs, out_sems
        self.sent = {}
        for k, copy in enumerate(self.ins):
            copy.start()
        for k, copy in enumerate(self.ins):
            if k not in late:
                copy.wait()

    def need(self, *which):
        for k in which:
            self.ins[k].wait()

    def part(self, k, n, count):
        src, dst = self.outs[k]
        rows = src.shape[0] // count
        cut = pl.ds(n * rows, rows)
        return pltpu.make_async_copy(src.at[cut], dst.at[cut], self.out_sems.at[k, n])

    def send(self, k, n=0, count=1):
        self.sent[k] = count
        self.part(k, n, count).start()

    def finish(self):
        for k in range(len(self.outs)):
            if k not in self.sent:
                self.send(k)
        for k, count in self.sent.items():
            for n in range(count):
                self.part(k, n, count).wait()


def call(body, outs, args, name, scratch=(), smem=1, deps=(), late=(), plain=False):
    outs = [jax.ShapeDtypeStruct(shape, dtype) for shape, dtype in outs]
    args, deps = list(args), list(deps)
    big = len(args) - smem
    count = len(outs)
    anywhere, inside = pl.BlockSpec(memory_space=pl.ANY), pl.BlockSpec(memory_space=pltpu.VMEM)

    def kernel(*refs):
        refs = list(refs)
        scalars, refs = refs[:smem], refs[smem:]
        ins, refs = refs[:big], refs[big + len(deps) :]
        results, refs = refs[:count], refs[count:]
        if plain:
            body(*scalars, *ins, *results, *refs)
            return
        held, refs = refs[:big], refs[big:]
        made, refs = refs[:count], refs[count:]
        in_sems, out_sems = refs[0], refs[1]
        traffic = Traffic(
            list(zip(ins, held)), list(zip(made, results)), in_sems, out_sems, late
        )
        extra = (traffic,) if late else ()
        body(*extra, *scalars, *held, *made, *refs[2:])
        traffic.finish()

    own = []
    if not plain:
        own = [pltpu.VMEM(a.shape, a.dtype) for a in args[smem:]]
        own += [pltpu.VMEM(o.shape, o.dtype) for o in outs]
        own += [pltpu.SemaphoreType.DMA((big,)), pltpu.SemaphoreType.DMA((count, 8))]
    return pl.pallas_call(
        kernel,
        out_shape=outs,
        in_specs=[pl.BlockSpec(memory_space=pltpu.SMEM)] * smem
        + [inside if plain else anywhere] * big
        + [anywhere] * len(deps),
        out_specs=[inside if plain else anywhere] * count,
        scratch_shapes=own + list(scratch),
        compiler_params=pltpu.CompilerParams(
            vmem_limit_bytes=(16 if plain else 56) * MIB
        ),
        cost_estimate=pl.CostEstimate(flops=0, bytes_accessed=0, transcendentals=0),
        name=name,
    )(*args, *deps)


def after(value, *deps):
    return pl.pallas_call(
        lambda *refs: None,
        out_shape=jax.ShapeDtypeStruct(value.shape, value.dtype),
        in_specs=[pl.BlockSpec(memory_space=pl.ANY)] * (1 + len(deps)),
        out_specs=pl.BlockSpec(memory_space=pl.ANY),
        input_output_aliases={0: 0},
        name="after",
    )(value, *deps)


def iota(shape, dim):
    return lax.broadcasted_iota(jnp.int32, shape, dim)


def onehot(cond):
    return jnp.where(cond, 1.0, 0.0).astype(f32).astype(bf16)


def eye(n):
    return onehot(iota((n, n), 0) == iota((n, n), 1))


def sixteen_swap():
    r, q = iota((256, 256), 0), iota((256, 256), 1)
    return onehot(((r % 16) == (q // 16)) & ((r // 16) == (q % 16)))


def tree(parts):
    parts = list(parts)
    while len(parts) > 1:
        parts = [parts[n] + parts[n + 1] for n in range(0, len(parts), 2)]
    return parts[0]


def sigmoid(v):
    return 1.0 / (1.0 + jnp.exp(-v))


def pack_wide_body(w, out):
    packed = jnp.concatenate([w[:, 0], w[:, 1]], axis=-1)
    for k in range(8):
        out[k] = packed


def pack_fine_body(r, e, out):
    slots = [r[q // 2, q % 2] for q in range(18)] + [e[...], jnp.zeros_like(e[...])]
    for row in range(5):
        out[row] = jnp.concatenate(slots[4 * row : 4 * row + 4], axis=-1)
    out[5:] = jnp.zeros((3, 64, 128), bf16)


def fill_taps(core, own, other, out):
    for blocks, side in ((own, core), (other, 1 - core)):
        for half in range(2):
            rows = pl.ds(pl.multiple_of(half * 128 + side * 64, 64), 64)
            lanes = slice(half * 64, half * 64 + 64)
            for group in range(4):
                w = [
                    jnp.concatenate(
                        [blocks[2 * group][t][:, lanes], blocks[2 * group + 1][t][:, lanes]],
                        axis=-1,
                    ).astype(f32)
                    for t in range(9)
                ]
                down = {
                    (0, 0): w[0:3],
                    (0, 1): [w[3 + s] + w[6 + s] for s in range(3)],
                    (1, 0): [w[s] + w[3 + s] for s in range(3)],
                    (1, 1): w[6:9],
                }
                for a in range(2):
                    for u in range(2):
                        d = down[(a, u)]
                        across = {
                            (0, 0): d[0],
                            (0, 1): d[1] + d[2],
                            (1, 0): d[0] + d[1],
                            (1, 1): d[2],
                        }
                        for b in range(2):
                            for v in range(2):
                                out[
                                    a * 8 + b * 4 + u * 2 + v,
                                    rows,
                                    group * 128 : group * 128 + 128,
                                ] = across[(b, v)].astype(bf16)


def refiner_select(chip):
    r, q = iota((1024, 1024), 0), iota((1024, 1024), 1)
    channel = (r // 128) * 32 + r % 32
    return onehot((((r // 32) % 4) == (q // 256)) & ((channel ^ (chip * 128)) == (q % 256)))


def refiner_body(idx, own, other, out, ex):
    core, chip = idx[1], idx[2]
    select = refiner_select(chip)
    for blocks, side in ((own, core), (other, 1 - core)):
        rows = pl.multiple_of(side * 64, 64)
        raw = jnp.concatenate([blocks[k, :5].reshape(320, 128) for k in range(8)], axis=-1)
        got = dot(raw, select).astype(bf16)
        for q in range(18):
            piece = got[(q // 4) * 64 : (q // 4) * 64 + 64, (q % 4) * 256 : (q % 4) * 256 + 256]
            out[q // 2, pl.ds(rows + (q % 2) * 128, 64), :] = piece
        ex[pl.ds(rows, 64), :] = got[256:320, 512:768]


def feature_select(place):
    r, q = iota((512, 512), 0), iota((512, 512), 1)
    kept = r % 256
    return onehot((((kept // 64) ^ place) * 64 + kept % 64) * 2 + r // 256 == q)


def feature_body(idx, b0, b1, b2, b3, out, turned):
    ident = eye(128)

    def turn(s, carry):
        x = jnp.concatenate([b0[s], b1[s], b2[s], b3[s]], axis=0)
        t = dot(ident, x, NT).astype(bf16)
        turned[s] = jnp.concatenate([t[:64], t[64:]], axis=-1)
        return carry

    lax.fori_loop(0, 16, turn, 0, unroll=4)
    swap = sixteen_swap()
    select = feature_select(idx[0])
    zero = jnp.zeros((10, 16, 512), bf16)
    out[0] = zero
    out[9] = zero
    out[:, 0] = zero
    out[:, 9] = zero
    for block in range(4):
        a = turned[:, block * 16 : block * 16 + 16, :].reshape(256, 512)
        c = dot(dot(swap, a).astype(bf16), select).astype(bf16)
        out[1 + 2 * block : 3 + 2 * block, 1:9] = c.reshape(2, 8, 16, 512)


def input_back_body(io, idx, d, w, b0, b1, b2, b3, turned):
    swap = sixteen_swap()
    select = feature_select(idx[0])

    io.need(1)
    acc = None
    for a in range(2):
        for b in range(2):
            lhs = jnp.concatenate(
                [
                    d[a, b, 2 - u - a : 10 - u - a, 2 - v - b : 10 - v - b].reshape(1024, 256)
                    for u in range(2)
                    for v in range(2)
                ],
                axis=-1,
            )
            first = a * 8 + b * 4
            term = dot(lhs, w[first : first + 4].reshape(1024, 512))
            acc = term if acc is None else acc + term
    x = dot(acc.astype(bf16), select, NT).astype(bf16)
    for block in range(4):
        t = dot(swap, x[block * 256 : block * 256 + 256]).astype(bf16)
        turned[:, block * 16 : block * 16 + 16, :] = t.reshape(16, 16, 512)
    ident = eye(256)

    def turn(s, carry):
        t = turned[s]
        t = jnp.concatenate([t[:, :256], t[:, 256:]], axis=0)
        o = dot(ident, t, NT).astype(bf16)
        b0[s] = o[0:64]
        b1[s] = o[64:128]
        b2[s] = o[128:192]
        b3[s] = o[192:256]
        return carry

    lax.fori_loop(0, 16, turn, 0, unroll=4)


def upstream_body(idx, own, other, out, turned):
    first = idx[1] == 0
    ident = eye(256)

    def turn(s, carry):
        p, q = own[s], other[s]
        lo = jnp.where(first, p, q)
        hi = jnp.where(first, q, p)
        turned[s] = dot(ident, jnp.concatenate([lo, hi], axis=0), NT).astype(bf16)
        return carry

    lax.fori_loop(0, 16, turn, 0, unroll=4)
    swap = sixteen_swap()

    def mix(y, carry):
        a = turned[:, pl.ds(pl.multiple_of(y * 16, 16), 16), :].reshape(256, 128)
        out[y] = dot(swap, a).astype(bf16).reshape(16, 16, 128)
        return carry

    lax.fori_loop(0, 16, mix, 0, unroll=4)


def over_samples(mask, values):
    return jnp.concatenate(
        [jnp.sum(mask[m] * values, axis=0, keepdims=True) for m in range(MB)], axis=0
    )


def per_sample(mask, rows):
    return sum(mask[m] * rows[m : m + 1] for m in range(MB))


def local_stats(mask, mean_s, squares_s):
    ones = jnp.ones_like(mean_s)
    n = over_samples(mask, ones) * 256.0
    mean = over_samples(mask, mean_s) * 256.0 / jnp.maximum(n, 1.0)
    gap = mean_s - per_sample(mask, mean)
    squares = over_samples(mask, squares_s + 256.0 * gap * gap)
    return n, mean, squares


def total_stats(messages, entries):
    parts = [(g[0:4], g[4:8], g[8:12]) for g in messages]
    mean = tree([n * m for n, m, _ in parts]) / entries
    squares = tree([q + n * (m - mean) * (m - mean) for n, m, q in parts])
    inverse = lax.rsqrt(squares / entries + epsilon)
    return mean, inverse


def message_list(refs):
    return [ref[c] for ref in refs for c in range(ref.shape[0])]


def conv_one_body(io, idx, own, other, x, mask, gap, logit, base, msg, w, glu):
    fill_taps(idx[1], own, other, w)
    io.send(4)
    io.need(2, 3)
    total = jnp.zeros((16, 128), f32)
    for a in range(2):
        for b in range(2):
            kept = []
            for u in range(2):
                for v in range(2):
                    kept.append(x[u + a : u + a + 8, v + b : v + b + 8].reshape(1024, 512))
            first = a * 8 + b * 4
            rhs = jnp.concatenate([w[first + n] for n in range(4)], axis=-1)
            c = dot(jnp.concatenate(kept, axis=-1), rhs, NT)
            g = (c[:, :128] * sigmoid(c[:, 128:])).reshape(8, 8, 16, 128)
            logit[:, a, :, b] = c[:, 128:].reshape(8, 8, 16, 128).astype(bf16)
            glu[a, b] = g
            total = total + jnp.sum(g, axis=(0, 1))
    io.send(1)
    mean_s = total * (1.0 / 256.0)
    base[...] = mean_s
    io.send(2)

    def spread(i, acc):
        for a in range(2):
            for b in range(2):
                d = glu[a, b, i] - mean_s[None]
                gap[i, a, :, b] = d.astype(bf16)
                acc = acc + jnp.sum(d * d, axis=0)
        io.send(0, i, 8)
        return acc

    squares = lax.fori_loop(0, 8, spread, jnp.zeros((16, 128), f32))
    n, mean, squares = local_stats(mask[...], mean_s, squares)
    msg[0:4] = n
    msg[4:8] = mean
    msg[8:12] = squares
    msg[12:16] = jnp.zeros((4, 128), f32)


def make_scale_body(entries):
    def body(mask, gains, base, messages, line, stat):
        mean, inverse = total_stats(message_list([messages]), entries)
        m = mask[...]
        mean_s, inverse_s = per_sample(m, mean), per_sample(m, inverse)
        stat[0] = base[...] - mean_s
        stat[1] = inverse_s
        scale = inverse_s * gains[0:1]
        line[0] = scale
        line[1] = (base[...] - mean_s) * scale + gains[1:2]

    return body


def conv_two_body(io, own, other, line, line_other, w, up, held, glu, logit, sums):
    zero = jnp.zeros((18, 16, 256), bf16)
    held[0] = zero
    held[17] = zero
    held[:, 0] = zero
    held[:, 17] = zero

    def fill(y, carry):
        for gap, scale, lanes in ((own, line, 0), (other, line_other, 128)):
            h = gap[y].astype(f32) * scale[0] + scale[1]
            held[y + 1, 1:17, :, lanes : lanes + 128] = h.astype(bf16)
        return carry

    lax.fori_loop(0, 16, fill, 0)
    io.send(0)
    io.need(4)

    def rows(step, total):
        y = step * 4
        lhs = jnp.concatenate(
            [
                held[pl.ds(y + t // 3, 4), t % 3 : t % 3 + 16].reshape(1024, 256)
                for t in range(9)
            ],
            axis=-1,
        )
        rhs = jnp.concatenate([w[t] for t in range(9)], axis=-1)
        c = dot(lhs, rhs, NT)
        g = (c[:, :128] * sigmoid(c[:, 128:])).reshape(4, 16, 16, 128)
        logit[pl.ds(y, 4)] = c[:, 128:].reshape(4, 16, 16, 128).astype(bf16)
        glu[pl.ds(y, 4)] = g
        io.send(1, step, 4)
        io.send(2, step, 4)
        return total + jnp.sum(g, axis=(0, 1))

    total = lax.fori_loop(0, 4, rows, jnp.zeros((16, 128), f32))
    mean_s = total * (1.0 / 256.0)

    io.need(5)

    def spread(y, acc):
        gap = glu[y] - mean_s[None]
        u = up[y].astype(f32)
        return (
            acc[0] + jnp.sum(gap * gap, axis=0),
            acc[1] + jnp.sum(u, axis=0),
            acc[2] + jnp.sum(u * gap, axis=0),
        )

    none = jnp.zeros((16, 128), f32)
    squares, plain, cross = lax.fori_loop(0, 16, spread, (none, none, none))
    sums[0] = mean_s
    sums[1] = plain
    sums[2] = cross
    sums[3] = squares


def make_back_two_body(entries):
    def body(io, glu, logit, up, mask, pull, gains, sums, w, gap, gap_other, messages, *outs):
        grad, own, other, small, stat, mine = outs
        messages = message_list([messages])
        mean, inverse = total_stats(messages, entries)
        plain = tree([g[12:16] for g in messages])
        cross = inverse * tree([g[16:20] + g[12:16] * (g[4:8] - mean) for g in messages])
        m = mask[...]
        mean_s, inverse_s = per_sample(m, mean), per_sample(m, inverse)
        gain, shift = gains[2:3], gains[3:4]
        stat[0] = mean_s
        stat[1] = inverse_s
        weight, gate = pull[0], pull[1]
        centred = sums[2] + sums[1] * (sums[0] - mean_s)
        small[2] = weight * (gain * inverse_s * centred + shift * sums[1])
        mine[2, 0:1] = jnp.sum(cross, axis=0, keepdims=True)
        mine[2, 1:2] = jnp.sum(plain, axis=0, keepdims=True)
        mine[2, 2:] = jnp.zeros((14, 128), f32)
        plain_s = per_sample(m, plain) * (1.0 / entries)
        cross_s = per_sample(m, cross) * (1.0 / entries)
        scale = inverse_s * gain
        factor = weight * gate
        io.need(0, 1, 2)
        zero = jnp.zeros((18, 16, 256), bf16)
        grad[0] = zero
        grad[17] = zero
        grad[:, 0] = zero
        grad[:, 17] = zero

        def step(y, carry):
            g = glu[y]
            s = sigmoid(logit[y].astype(f32))
            hat = (g - mean_s) * inverse_s
            d = scale * (up[y].astype(f32) * factor - plain_s - hat * cross_s)
            grad[y + 1, 1:17, :, 0:128] = (d * s).astype(bf16)
            grad[y + 1, 1:17, :, 128:256] = (d * g * (1.0 - s)).astype(bf16)
            return carry

        lax.fori_loop(0, 16, step, 0)
        io.send(0)
        io.need(7, 8, 9)

        def rows(step, acc):
            y = step * 4
            lhs = jnp.concatenate(
                [
                    grad[pl.ds(y + 2 - t // 3, 4), 2 - t % 3 : 18 - t % 3].reshape(1024, 256)
                    for t in range(9)
                ],
                axis=-1,
            )
            c = dot(lhs, w[...].reshape(2304, 256)).astype(bf16)
            out = []
            for ref, at, lanes in ((own, gap, 0), (other, gap_other, 128)):
                d = c[:, lanes : lanes + 128].reshape(4, 16, 16, 128)
                ref[pl.ds(y, 4)] = d
                io.send(1 if lanes == 0 else 2, step, 4)
                d = d.astype(f32)
                out.append(jnp.sum(d, axis=(0, 1)))
                out.append(jnp.sum(d * at[pl.ds(y, 4)].astype(f32), axis=(0, 1)))
            return tuple(p + q for p, q in zip(acc, out))

        none = jnp.zeros((16, 128), f32)
        mine[0], mine[1], small[0], small[1] = lax.fori_loop(0, 4, rows, (none,) * 4)

    return body


def output_part(idx, glu, stat, pull, gains, own, other, turned):
    swap = sixteen_swap()
    mean_s, inverse_s = stat[0], stat[1]
    gain, shift = gains[2:3], gains[3:4]
    gate = pull[1]

    def step(y, carry):
        o = (((glu[y] - mean_s) * inverse_s) * gain + shift) * gate
        o = dot(swap, o.astype(bf16).reshape(256, 128)).astype(bf16)
        turned[:, pl.ds(pl.multiple_of(y * 16, 16), 16), :] = o.reshape(16, 16, 128)
        return carry

    lax.fori_loop(0, 16, step, 0, unroll=4)
    ident = eye(128)
    first = idx[1] == 0

    def turn(s, carry):
        t = dot(ident, turned[s], NT).astype(bf16)
        own[s] = jnp.where(first, t[:64], t[64:])
        other[s] = jnp.where(first, t[64:], t[:64])
        return carry

    lax.fori_loop(0, 16, turn, 0, unroll=4)


def refiner_grad_body(
    io, idx, grad, held, glu, stat, pull, gains, own, other, out_own, out_other, work, turned
):
    core, chip = idx[1], idx[2]

    def tap(t, carry):
        d = grad[1:17, 1:17].reshape(4096, 256)
        h = held[pl.ds(t // 3, 16), pl.ds(t % 3, 16)].reshape(4096, 256)
        work[t] = dot(d, h, TN).astype(bf16)
        return carry

    lax.fori_loop(0, 9, tap, 0)
    select = refiner_select(chip)
    for out, side in ((own, core), (other, 1 - core)):
        start = pl.multiple_of(side * 64, 64)
        rows = []
        for row in range(5):
            pieces = []
            for q in range(4 * row, 4 * row + 4):
                if q < 18:
                    pieces.append(work[q // 2, pl.ds(start + (q % 2) * 128, 64), :])
                else:
                    pieces.append(jnp.zeros((64, 256), bf16))
            rows.append(jnp.concatenate(pieces, axis=-1))
        got = dot(jnp.concatenate(rows, axis=0), select, NT).astype(bf16)
        for k in range(8):
            out[k] = got[:, k * 128 : k * 128 + 128].reshape(5, 64, 128)
    io.send(0)
    io.send(1)
    io.need(2, 3, 4, 5)
    output_part(idx, glu, stat, pull, gains, out_own, out_other, turned)


def refiner_sum_body(parts, out):
    total = tree([parts[k, :320].astype(f32) for k in range(8)])
    for q in range(18):
        rows = slice((q // 4) * 64, (q // 4) * 64 + 64)
        out[q // 2, q % 2] = total[rows, (q % 4) * 32 : (q % 4) * 32 + 32]


def first_sums_body(mine, theirs, mask, stat, msg):
    m = mask[...]
    plain = mine[0] + theirs[0]
    cross = mine[1] + theirs[1] + stat[0] * plain
    msg[0:4] = over_samples(m, plain)
    msg[4:8] = over_samples(m, cross * stat[1])


def make_back_one_body(entries):
    def body(
        io,
        idx,
        gap,
        logit,
        base,
        own,
        other,
        mask,
        stat,
        gains,
        messages,
        x,
        grad,
        small,
        keep,
        send,
        work,
    ):
        messages = message_list([messages])
        plain = tree([g[0:4] for g in messages])
        cross = tree([g[4:8] for g in messages])
        small[0:1] = jnp.sum(cross, axis=0, keepdims=True)
        small[1:2] = jnp.sum(plain, axis=0, keepdims=True)
        small[2:8] = jnp.zeros((6, 128), f32)
        io.send(1)
        m = mask[...]
        plain_s = per_sample(m, plain) * (1.0 / entries)
        cross_s = per_sample(m, cross) * (1.0 / entries)
        shift_s, inverse_s = stat[0], stat[1]
        mean = base[...]
        scale = inverse_s * gains[0:1]
        zero = jnp.zeros((10, 16, 256), bf16)
        for a in range(2):
            for b in range(2):
                grad[a, b, 0] = zero
                grad[a, b, 9] = zero
                grad[a, b, :, 0] = zero
                grad[a, b, :, 9] = zero

        def step(i, carry):
            for a in range(2):
                for b in range(2):
                    g = gap[i, a, :, b].astype(f32)
                    s = sigmoid(logit[i, a, :, b].astype(f32))
                    hat = (g + shift_s) * inverse_s
                    g = g + mean
                    d = own[i, a, :, b].astype(f32) + other[i, a, :, b].astype(f32)
                    d = scale * (d - plain_s - hat * cross_s)
                    grad[a, b, i + 1, 1:9, :, 0:128] = (d * s).astype(bf16)
                    grad[a, b, i + 1, 1:9, :, 128:256] = (d * g * (1.0 - s)).astype(bf16)
            return carry

        lax.fori_loop(0, 8, step, 0)
        io.send(0)
        io.need(9)
        widener_grad(idx[1], grad, x, keep, send, work)

    return body


def widener_grad(core, grad, x, own, other, work):
    def phase(n, carry):
        a, b = n // 2, n % 2
        d = grad[a, b, 1:9, 1:9].reshape(1024, 256)
        for u in range(2):
            for v in range(2):
                f = x[pl.ds(u + a, 8), pl.ds(v + b, 8)].reshape(1024, 512)
                work[n, 2 * u + v] = dot(d, f, TN)
        return carry

    lax.fori_loop(0, 4, phase, 0)
    source = {0: (0, 0), 1: (1, 0), 2: (1, 1)}
    for out, side in ((own, core), (other, 1 - core)):
        start = pl.multiple_of(side * 64, 64)
        for pair in range(4):
            lanes = slice(pair * 128, pair * 128 + 128)
            for r in range(3):
                for s in range(3):
                    both = []
                    for half in range(2):
                        rows = pl.ds(start + half * 128, 64)
                        both.append(
                            sum(
                                work[2 * a + b, 2 * source[r][a] + source[s][b], rows, lanes]
                                for a in range(2)
                                for b in range(2)
                            )
                        )
                    first, second = both
                    out[2 * pair, 3 * r + s] = jnp.concatenate(
                        [first[:, :64], second[:, :64]], axis=-1
                    ).astype(bf16)
                    out[2 * pair + 1, 3 * r + s] = jnp.concatenate(
                        [first[:, 64:], second[:, 64:]], axis=-1
                    ).astype(bf16)


def pair_sum_body(own, other, out):
    out[...] = (own[...].astype(f32) + other[...].astype(f32)).astype(bf16)


def widener_sum_body(parts, out):
    for t in range(9):
        total = tree([parts[k, t].astype(f32) for k in range(8)])
        out[t, 0] = total[:, :64]
        out[t, 1] = total[:, 64:]


def skip_quarter_body(idx, skip, out):
    rows = pl.ds(pl.multiple_of(idx[0] * 8, 8), 8)
    for i in range(8):
        out[i] = skip[rows, i * 16 : i * 16 + 16, :]


def squeeze_body(skip, kernels, msg, kept, out, rows):
    rows[...] = skip[...].astype(f32).reshape(1024, 128)
    for k in range(16):
        kept[:, k * 128 : k * 128 + 128] = rows[pl.ds(k, 64, stride=16), :].astype(bf16)
    part = dot(kept[...], kernels[...], NT)
    for i in range(8):
        for c in range(2):
            out[2 * i + c, 0:16] = msg[...]
            out[2 * i + c, 16:24] = part[i * 8 : i * 8 + 8, :128]
            out[2 * i + c, 24:32] = part[i * 8 : i * 8 + 8, 128:]


def part_sum_body(idx, parts, out):
    core = idx[1]
    out[:, :128] = tree([parts[2 * k + core, 16:24] for k in range(8)])
    out[:, 128:] = tree([parts[2 * k + core, 24:32] for k in range(8)])


def own_first(v, chip):
    return jnp.where(chip == 0, v, jnp.concatenate([v[:, 128:], v[:, :128]], axis=-1))


def gate_body(idx, s0, s1, s2, s3, ex, weight, out, squeezed):
    j, core, chip = idx[0], idx[1], idx[2]
    for n, part in enumerate((s0, s1, s2, s3)):
        squeezed[pl.ds(pl.multiple_of((j ^ n) * 8, 8), 8), :] = part[...]
    mine = squeezed[pl.ds(pl.multiple_of(core * 16, 16), 16), :]
    excited = dot(own_first(mine * sigmoid(mine), chip).astype(bf16), ex[...], NT)
    out[0] = weight[...]
    out[1] = sigmoid(excited)


def message_two_body(mask, pull, sums, msg):
    mean_s, plain, cross = sums[0], sums[1], sums[2]
    m = mask[...]
    n, mean, squares = local_stats(m, mean_s, sums[3])
    factor = pull[0] * pull[1]
    msg[0:4] = n
    msg[4:8] = mean
    msg[8:12] = squares
    msg[12:16] = over_samples(m, factor * plain)
    msg[16:20] = over_samples(m, factor * (cross + plain * (mean_s - per_sample(m, mean))))
    msg[20:24] = jnp.zeros((4, 128), f32)


def excite_back_body(idx, g0, g1, squeezed, ex_own, ex_other, fine, recv, vectors, out):
    chip = idx[2]
    s = squeezed[...]
    sigm = sigmoid(s)
    swish = (s * sigm).astype(bf16)
    mine = own_first(ex_own[...].astype(f32), chip)
    theirs = own_first(ex_other[...].astype(f32), 1 - chip)
    ex = jnp.where(
        chip == 0, jnp.concatenate([mine, theirs], axis=0), jnp.concatenate([theirs, mine], axis=0)
    ).astype(bf16)
    gate = sigmoid(dot(swish, ex, NT))
    core = idx[1]
    rows = []
    for half in range(2):
        own = jnp.where(core == half, g0[0], g1[0])
        other = jnp.where(core == half, g0[1], g1[1])
        lo, hi = jnp.where(chip == 0, own, other), jnp.where(chip == 0, other, own)
        rows.append(jnp.concatenate([lo, hi], axis=-1))
    grad_gate = jnp.concatenate(rows, axis=0)
    d_excited = (grad_gate * gate * (1.0 - gate)).astype(bf16)
    d_swish = dot(d_excited, ex)
    d_squeezed = d_swish * (sigm * (1.0 + s * (1.0 - sigm)))
    j = idx[0]
    pick_out = onehot(iota((256, 64), 0) == iota((256, 64), 1) + j * 64)
    both = jnp.concatenate(
        [dot(d_squeezed.astype(bf16), pick_out), dot(d_excited, pick_out)], axis=-1
    ).astype(bf16)
    vectors[...] = both
    pick_in = onehot((iota((256, 1024), 0) // 32 == iota((256, 1024), 1) // 128)
                     & (iota((256, 1024), 0) % 32 == iota((256, 1024), 1) % 128))
    picked = dot(swish, pick_in).astype(bf16)
    total = (fine[...].astype(f32) + recv[...].astype(f32)).astype(bf16)
    out[:, :320] = total.reshape(8, 320, 128)
    for k in range(8):
        out[k, 320:352] = both
        out[k, 352:384] = picked[:, k * 128 : k * 128 + 128]


def quarters_first(v):
    v = v.astype(f32)
    return jnp.concatenate(
        [v[i * 32 + q * 8 : i * 32 + q * 8 + 8] for q in range(4) for i in range(8)], axis=0
    )


def squeeze_back_body(parts, skips, ex_grad, sq_grad):
    vectors = jnp.concatenate([parts[k, 320:352] for k in range(8)], axis=0)
    swish = jnp.concatenate([parts[k, 352:384] for k in range(8)], axis=0)
    ex_grad[...] = dot(vectors, swish, TN)[64:, :32]
    sq_grad[...] = dot(quarters_first(vectors).astype(bf16), skips[...], TN)[:64]


def skip_back_body(idx, vectors, kernels, keep, send, rows):
    d = vectors[:, :64]
    for i in range(8):
        pooled = dot(d, kernels[i * 64 : i * 64 + 64, :])
        for k in range(16):
            rows[:, i * 16 + k, :] = pooled[:, k * 128 : k * 128 + 128]
    at = idx[2] * 64
    keep[...] = rows[:, pl.ds(pl.multiple_of(at, 64), 64), :].astype(bf16)
    send[...] = rows[:, pl.ds(pl.multiple_of(64 - at, 64), 64), :].astype(bf16)


def skip_add_body(idx, own, other, keep, send):
    first = idx[1] == 0
    total = own[...].astype(f32) + other[...].astype(f32)
    lo, hi = total[:, :32], total[:, 32:]
    keep[...] = jnp.where(first, lo, hi)
    send[...] = jnp.where(first, hi, lo).astype(bf16)


def skip_last_body(own, other, out):
    out[...] = own[...] + other[...].astype(f32)


def swap_with(v, axis, k):
    return lax.ppermute(v, axis, [(n, n ^ k) for n in range(lax.axis_size(axis))])


def on_device(
    features,
    skip_feature,
    section_ids,
    micro_ids,
    widener,
    refiner,
    squeezer,
    exciter,
    gain_one,
    bias_one,
    gain_two,
    bias_two,
    upstream,
):
    nb = lax.axis_size("batch")
    eight = nb == 8
    samples = features.shape[0]
    entries = float(samples * nb // MB * 256)
    i = lax.axis_index("batch")
    j = lax.axis_index("chan")
    core, chip = j % 2, j // 2
    idx = jnp.stack([j, core, chip, i]).astype(jnp.int32)

    def half(v, which):
        return lax.dynamic_slice_in_dim(v, which * 16, 16, axis=0)

    def natural(own, other, axis):
        return jnp.where(
            core == 0,
            jnp.concatenate([own, other], axis=axis),
            jnp.concatenate([other, own], axis=axis),
        )

    def over_batch(v):
        return lax.all_to_all(v, "batch", 0, 0, tiled=True)

    f_keep, f_send = half(features, core), half(features, 1 - core)
    f_blocks = [f_keep] + [
        swap_with(f_send if k % 2 else f_keep, "chan", k) for k in range(1, 4)
    ]
    if eight:
        (wide,) = call(
            pack_wide_body, [((8, 9, 64, 128), bf16)], (widener,), "pack_wide", smem=0, plain=True
        )
        wide_own = over_batch(wide)
    else:
        w_all = lax.all_gather(widener, "batch", axis=3, tiled=True)
        wide_own = w_all.reshape(9, 2, 64, 8, 64).transpose(3, 0, 2, 1, 4).reshape(8, 9, 64, 128)

    gains = jnp.stack([gain_one, bias_one, gain_two, bias_two], axis=0)
    gains = natural(gains, swap_with(gains, "chan", 1), 1)
    ids = half(micro_ids, core)
    mask = jnp.broadcast_to(
        (ids[None, :, None] == jnp.arange(MB, dtype=jnp.int32)[:, None, None]).astype(f32),
        (MB, 16, 128),
    )
    weight_of = jnp.where(section_ids == 0, 1.0, jnp.where(section_ids == 1, 2.0, 4.0)).astype(f32)
    weight = jnp.broadcast_to(half(weight_of, core)[:, None], (16, 128))

    groups = [[n * 4 + 2 * x + c for n in range(nb) for c in range(2)] for x in range(2)]

    def exchange(copies):
        return lax.all_to_all(
            copies, ("batch", "chan"), 0, 0, tiled=True, axis_index_groups=groups
        )

    def share(msg):
        if eight:
            return exchange(jnp.broadcast_to(msg, (16,) + msg.shape))
        pair = jnp.stack([msg, swap_with(msg, "chan", 1)], axis=0)
        return lax.all_gather(pair, "batch").reshape((-1,) + msg.shape)

    u_keep = half(upstream, core)
    u_other = swap_with(half(upstream, 1 - core), "chan", 1)
    (up,) = call(
        upstream_body,
        [((16, 16, 16, 128), bf16)],
        (idx, u_keep, u_other),
        "upstream_turned",
        scratch=[pltpu.VMEM((16, 256, 128), bf16)],
    )
    (field,) = call(
        feature_body,
        [((10, 10, 16, 512), bf16)],
        (idx, *f_blocks),
        "features_turned",
        scratch=[pltpu.VMEM((16, 64, 512), bf16)],
        deps=(up,),
    )
    if eight:
        skip_full = lax.all_gather(skip_feature, "chan", axis=1, tiled=True)
        flat = squeezer.reshape(16, 64, 16, 8).transpose(1, 2, 3, 0).reshape(64, 2048)
        squeezer_whole = lax.all_gather(flat, "chan", axis=0, tiled=True)
        wide_own = after(wide_own, field, skip_full)

        (quarter,) = call(
            skip_quarter_body,
            [((8, 8, 16, 128), bf16)],
            (idx, skip_full),
            "skip_quarter", plain=True,
            deps=(wide_own,),
        )
        quarter = over_batch(quarter)
        (fine,) = call(
            pack_fine_body,
            [((8, 64, 128), bf16)],
            (refiner, exciter),
            "pack_fine",
            smem=0, plain=True,
            deps=(wide_own,),
        )
        fine_own = lax.all_gather(fine, "batch")
    else:
        r_all = lax.all_gather(refiner, "batch", axis=3, tiled=True)
        e_all = lax.all_gather(exciter, "batch", axis=1, tiled=True)
        r_all = jnp.concatenate(
            [r_all.reshape(18, 64, 256), e_all[None], jnp.zeros((1, 64, 256), bf16)], axis=0
        )
        r_all = r_all.reshape(5, 4, 64, 8, 32).transpose(3, 0, 2, 1, 4).reshape(8, 5, 64, 128)
        fine_own = jnp.pad(r_all, ((0, 0), (0, 3), (0, 0), (0, 0)))

    wide_other = swap_with(wide_own, "chan", 1)
    gap, logit_one, base, msg_one, wide_w = call(
        conv_one_body,
        [
            ((8, 2, 8, 2, 16, 128), bf16),
            ((8, 2, 8, 2, 16, 128), bf16),
            ((16, 128), f32),
            ((16, 128), f32),
            ((16, 256, 512), bf16),
        ],
        (idx, wide_own, wide_other, field, mask),
        "conv_one",
        scratch=[pltpu.VMEM((2, 2, 8, 8, 16, 128), f32)],
        late=(2, 3),
    )
    flat_field = (16, 16, 16, 128)
    gap_other = swap_with(gap, "chan", 2).reshape(flat_field)

    if eight:
        skips, payload = call(
            squeeze_body,
            [((64, 2048), bf16), ((16, 32, 128), f32)],
            (quarter, squeezer_whole, msg_one),
            "squeeze",
            scratch=[pltpu.VMEM((1024, 128), f32)],
            smem=0,
            plain=True,
        )
        shared_one = exchange(payload)
    else:
        shared_one = share(msg_one)
    shared_one = after(shared_one, gap_other)
    if eight:
        (part,) = call(
            part_sum_body, [((8, 256), f32)], (idx, shared_one), "part_sum", plain=True
        )
    line, stat_one = call(
        make_scale_body(entries),
        [((2, 16, 128), f32), ((2, 16, 128), f32)],
        (mask, gains, base, shared_one),
        "scale", plain=True,
        smem=0,
    )
    fine_own = after(fine_own, shared_one)
    fine_other = swap_with(fine_own, "chan", 1)
    fine_w, exciter_own = call(
        refiner_body,
        [((9, 256, 256), bf16), ((128, 256), bf16)],
        (idx, fine_own, fine_other),
        "refiner_taps", plain=True,
    )
    if eight:
        line_other, part_other = swap_with(line, "chan", 2), swap_with(part, "chan", 2)
        squeezed = (part, swap_with(part, "chan", 1), part_other, swap_with(part_other, "chan", 1))
    else:
        line_other = swap_with(line, "chan", 2)

    held, glu_two, logit_two, sums_two = call(
        conv_two_body,
        [
            ((18, 18, 16, 256), bf16),
            ((16, 16, 16, 128), f32),
            ((16, 16, 16, 128), bf16),
            ((4, 16, 128), f32),
        ],
        (gap.reshape(flat_field), gap_other, line, line_other, fine_w, up),
        "conv_two",
        smem=0,
        late=(4, 5),
    )
    if eight:
        pull, squeezed = call(
            gate_body,
            [((2, 16, 128), f32), ((32, 256), f32)],
            (idx, *squeezed, exciter_own, weight),
            "gate", plain=True,
        )
    else:
        skip_full = lax.all_gather(skip_feature, "chan", axis=1, tiled=True)
        squeezer_full = lax.all_gather(squeezer, "batch", axis=2, tiled=True)
        pooled = skip_full.reshape(samples, -1, 16)
        squeezed = jnp.einsum("toc,bct->bo", squeezer_full, pooled, preferred_element_type=f32)
        squeeze_sig = jax.nn.sigmoid(squeezed)
        swish = (squeezed * squeeze_sig).astype(bf16)
        swish_full = lax.all_gather(swish, "chan", axis=1, tiled=True)
        exciter_full = lax.all_gather(exciter, "batch", axis=1, tiled=True)
        excited = jnp.einsum("oc,bc->bo", exciter_full, swish_full, preferred_element_type=f32)
        gate = jax.nn.sigmoid(excited)
        gate_mine = natural(half(gate, core), swap_with(half(gate, 1 - core), "chan", 1), 1)
        pull = jnp.stack([weight, gate_mine], axis=0)
    (msg_two,) = call(
        message_two_body, [((24, 128), f32)], (mask, pull, sums_two), "message_two", plain=True, smem=0
    )
    shared_two = share(msg_two)
    if eight:
        flats = lax.all_gather(after(flat, shared_two), "batch", axis=0, tiled=True)
    grad_two, dh_own, dh_send, small, stat_two, mine = call(
        make_back_two_body(entries),
        [
            ((18, 18, 16, 256), bf16),
            ((16, 16, 16, 128), bf16),
            ((16, 16, 16, 128), bf16),
            ((3, 16, 128), f32),
            ((2, 16, 128), f32),
            ((3, 16, 128), f32),
        ],
        (
            glu_two,
            logit_two,
            up,
            mask,
            pull,
            gains,
            sums_two,
            fine_w,
            gap.reshape(flat_field),
            gap_other,
            shared_two,
        ),
        "back_two",
        smem=0,
        late=(0, 1, 2, 7, 8, 9),
    )
    theirs = swap_with(small, "chan", 2)
    dh_other = swap_with(after(dh_send, theirs), "chan", 2)
    (msg_three,) = call(
        first_sums_body, [((8, 128), f32)], (mine, theirs, mask, stat_one), "first_sums", plain=True, smem=0
    )
    shared_three = share(msg_three)
    fine_keep, fine_send, out_own, out_send = call(
        refiner_grad_body,
        [
            ((8, 5, 64, 128), bf16),
            ((8, 5, 64, 128), bf16),
            ((16, 64, 256), bf16),
            ((16, 64, 256), bf16),
        ],
        (idx, grad_two, held, glu_two, stat_two, pull, gains),
        "refiner_grad",
        scratch=[pltpu.VMEM((9, 256, 256), bf16), pltpu.VMEM((16, 256, 128), bf16)],
        late=(2, 3, 4, 5),
    )
    output = natural(out_own, swap_with(out_send, "chan", 1), 0)
    fine_recv = swap_with(after(fine_send, shared_three), "chan", 1)

    def pair(keep, recv, name):
        return call(pair_sum_body, [(keep.shape, bf16)], (keep, recv), name, smem=0)[0]

    if eight:
        both = jnp.stack([small[2], theirs[2]], axis=0)
        vectors, combined = call(
            excite_back_body,
            [((32, 128), bf16), ((8, 384, 128), bf16)],
            (
                idx,
                both,
                swap_with(both, "chan", 1),
                squeezed,
                exciter_own,
                swap_with(exciter_own, "chan", 2),
                fine_keep,
                fine_recv,
            ),
            "excite_back",
            deps=(shared_three,),
        )
        parts = over_batch(combined)
        ready = (combined, out_own)
    else:
        refiner_pair = pair(fine_keep, fine_recv, "refiner_pair")
        ready = (refiner_pair, out_own)
        v = refiner_pair.reshape(8, 5, 64, 4, 32).transpose(1, 3, 2, 0, 4).reshape(20, 64, 256)
        v = v[:18].reshape(9, 2, 64, 256).astype(f32)
        refiner_sum = lax.psum_scatter(v, "batch", scatter_dimension=3, tiled=True)

    by_phase = (8, 2, 8, 2, 16, 128)
    grad_one, small_one, wide_keep, wide_send = call(
        make_back_one_body(entries),
        [
            ((2, 2, 10, 10, 16, 256), bf16),
            ((8, 128), f32),
            ((8, 9, 64, 128), bf16),
            ((8, 9, 64, 128), bf16),
        ],
        (
            idx,
            gap,
            logit_one,
            base,
            dh_own.reshape(by_phase),
            dh_other.reshape(by_phase),
            mask,
            stat_one,
            gains,
            shared_three,
            field,
        ),
        "back_one",
        scratch=[pltpu.VMEM((4, 4, 256, 512), f32)],
        deps=ready,
        late=(9,),
    )
    widener_pair = pair(wide_keep, swap_with(wide_send, "chan", 1), "widener_pair")
    if eight:
        widener_pair = after(widener_pair, parts)
        widener_parts = over_batch(widener_pair)
    else:
        v = widener_pair.reshape(8, 9, 64, 2, 64).transpose(1, 3, 2, 0, 4).reshape(9, 2, 64, 512)
        widener_sum = lax.psum_scatter(v.astype(f32), "batch", scatter_dimension=3, tiled=True)
    if eight:
        skip_keep, skip_send = call(
            skip_back_body,
            [((32, 64, 128), bf16), ((32, 64, 128), bf16)],
            (idx, vectors, flats),
            "skip_back",
            scratch=[pltpu.VMEM((32, 128, 128), f32)],
            deps=(widener_pair,),
        )
    blocks = call(
        input_back_body,
        [((16, 64, 128), bf16)] * 4,
        (idx, grad_one, wide_w),
        "input_back",
        scratch=[pltpu.VMEM((16, 64, 512), bf16)],
        deps=(skip_send,) if eight else (widener_pair,),
        late=(1,),
    )
    got = [blocks[0]] + [swap_with(blocks[k], "chan", k) for k in range(1, 4)]
    input_grad = natural(
        got[0].astype(f32) + got[2].astype(f32), got[1].astype(f32) + got[3].astype(f32), 0
    )

    if eight:
        (refiner_sum,) = call(
            refiner_sum_body,
            [(refiner.shape, f32)],
            (parts,),
            "refiner_sum",
            smem=0, plain=True,
            deps=(widener_pair,),
        )
        skips = lax.all_gather(after(skips, dh_other), "chan", axis=0, tiled=True)
        exciter_sum, squeezer_sum = call(
            squeeze_back_body,
            [((64, 32), f32), ((64, 2048), f32)],
            (parts, skips),
            "squeeze_back",
            smem=0,
            plain=True,
            deps=(widener_pair,),
        )
        squeezer_sum = (
            squeezer_sum.reshape(64, 16, 8, 16).transpose(3, 0, 1, 2).reshape(16, 64, 128)
        )
        skip_own, skip_other = call(
            skip_add_body,
            [((32, 32, 128), f32), ((32, 32, 128), bf16)],
            (idx, skip_keep, swap_with(skip_send, "chan", 2)),
            "skip_add", plain=True,
        )
        (skip_grad,) = call(
            skip_last_body,
            [((32, 32, 128), f32)],
            (skip_own, swap_with(skip_other, "chan", 1)),
            "skip_last", plain=True,
            smem=0,
        )
        (widener_sum,) = call(
            widener_sum_body,
            [(widener.shape, f32)],
            (widener_parts,),
            "widener_sum",
            smem=0, plain=True,
            deps=(input_grad, skip_grad, output, squeezer_sum, refiner_sum),
        )
    else:
        lo, hi = small[2, :, :64], small[2, :, 64:]
        keep, send = jnp.where(core == 0, lo, hi), jnp.where(core == 0, hi, lo)
        grad_gate = natural(keep, swap_with(send, "chan", 1), 0)
        grad_excited = (grad_gate * gate * (1.0 - gate)).astype(bf16)
        exciter_grad = jnp.einsum(
            "bo,bc->oc", grad_excited, swish_full, preferred_element_type=f32
        )
        partial_swish = jnp.einsum(
            "bo,oc->bc", grad_excited, exciter_full, preferred_element_type=f32
        )
        grad_swish = lax.psum_scatter(
            partial_swish.astype(bf16), "chan", scatter_dimension=1, tiled=True
        ).astype(f32)
        grad_squeezed = grad_swish * squeeze_sig * (1.0 + squeezed * (1.0 - squeeze_sig))
        grad_squeezed = grad_squeezed.astype(bf16)
        squeezer_grad = jnp.einsum(
            "bo,bct->toc", grad_squeezed, pooled, preferred_element_type=f32
        )
        partial_pooled = jnp.einsum(
            "bo,toc->bct", grad_squeezed, squeezer_full, preferred_element_type=f32
        ).reshape(samples, -1, 128)
        skip_grad = lax.psum_scatter(
            partial_pooled.astype(bf16), "chan", scatter_dimension=1, tiled=True
        ).astype(f32)
        squeezer_sum = lax.psum_scatter(squeezer_grad, "batch", scatter_dimension=2, tiled=True)
        exciter_sum = lax.psum_scatter(exciter_grad, "batch", scatter_dimension=1, tiled=True)

    norms = jnp.concatenate([small_one[0:2], mine[2, 0:2]], axis=0)
    norm_grads = jnp.where(core == 0, norms[:, :64], norms[:, 64:])
    return (
        output,
        input_grad,
        skip_grad,
        widener_sum,
        refiner_sum,
        squeezer_sum,
        exciter_sum,
        norm_grads,
    )


def solution(mesh):
    placed = (
        P("batch", "chan", None),
        P("batch", "chan", None),
        P("batch"),
        P("batch"),
        P(None, None, "chan", "batch"),
        P(None, None, "chan", "batch"),
        P(None, "chan", "batch"),
        P("chan", "batch"),
        P("chan"),
        P("chan"),
        P("chan"),
        P("chan"),
        P("batch", "chan", None),
    )
    return jax.shard_map(
        on_device,
        mesh=mesh,
        in_specs=placed,
        out_specs=(
            P("batch", "chan", None),
            P("batch", "chan", None),
            P("batch", "chan", None),
            P(None, None, "chan", "batch"),
            P(None, None, "chan", "batch"),
            P(None, "chan", "batch"),
            P("chan", "batch"),
            P(None, "chan"),
        ),
        check_vma=False,
    )
```

time: 477 us -> 267 us (0.56)
  waiting for transfers between devices: 156 us -> 36.6 us
  starting transfers between devices: 113 us -> 39.9 us
  Pallas kernels: 93.3 us -> 107 us
  blocking collectives: 43.3 us -> 29.7 us
  matrix products: 10.8 us -> 0 us
  local copies, waits for them, and re-layouts: 39.1 us -> 32.6 us
    ppermute x83 -> x24, starting transfers between devices: 113 us -> 13.3 us  [swap_with(): lax.ppermute(v, axis, [(n, n ^ k) for n in range(lax.axis_size(axis))])]
    reduce_scatter x3 -> x0, waiting for transfers between devices: 79.1 us -> none  [the longest x1 79.1 us: on_device(): lax.psum_scatter(squeezer_grad, 'batch', scatter_dimension=2, tiled=True)]
    all_gather x2 -> x0, blocking collectives: 43.3 us -> none  [the longest x1 30.8 us: on_device(): exciter_full = lax.all_gather(exciter, 'batch', axis=1, tiled=True)]
    ppermute x83 -> x24, waiting for transfers between devices: 57 us -> 22.7 us  [swap_with(): lax.ppermute(v, axis, [(n, n ^ k) for n in range(lax.axis_size(axis))])]
    all_to_all x0 -> x2, blocking collectives: none -> 29.7 us  [exchange(): lax.all_to_all(copies, ('batch', 'chan'), 0, 0, tiled=True, axis_index_gr...]
    all_to_all x0 -> x5, starting transfers between devices: none -> 26.2 us  [the longest x4 22.7 us: over_batch(): return lax.all_to_all(v, 'batch', 0, 0, tiled=True)]
    unnamed x7 -> x5, waiting for transfers between devices: 20.3 us -> 0.75 us
    pallas_call x17 -> x34, Pallas kernels: 93.3 us -> 107 us  [the longest x26 107 us: call(): pl.pallas_call(kernel, out_shape=outs, in_specs=[pl.BlockSpec(memory_spac...]
  transfers between devices with their start and end apart: 89 -> 34, of which waited for: 24 -> 13; matrix products, arithmetic and copies ran while one was open for 7% -> 6% of each run, Pallas kernels for 15% -> 39%
where the time goes in v2:
time: 267 us; the launch traced here: 265 us
  Pallas kernels  107 us (40%)
  starting transfers between devices  39.9 us (15%)
  waiting for transfers between devices  36.6 us (14%)
  local copies, waits for them, and re-layouts  32.6 us (12%)
  blocking collectives  29.7 us (11%)
  between operations  14.6 us (5%)
  other arithmetic  4.7 us (2%)
    pallas_call x26, Pallas kernels, call(): pl.pallas_call(kernel, out_shape=outs, in_specs=[pl.BlockSpec(memory_spac...  107 us
    all_to_all x2, blocking collectives, exchange(): lax.all_to_all(copies, ('batch', 'chan'), 0, 0, tiled=True, axis_index_gr...  29.7 us
    unnamed x132, local copies, waits for them, and re-layouts  24.1 us
    all_to_all x4, starting transfers between devices, over_batch(): return lax.all_to_all(v, 'batch', 0, 0, tiled=True)  22.7 us
    ppermute x24, waiting for transfers between devices, swap_with(): lax.ppermute(v, axis, [(n, n ^ k) for n in range(lax.axis_size(axis))])  22.7 us
    ppermute x24, starting transfers between devices, swap_with(): lax.ppermute(v, axis, [(n, n ^ k) for n in range(lax.axis_size(axis))])  13.3 us
    all_to_all x4, waiting for transfers between devices, over_batch(): return lax.all_to_all(v, 'batch', 0, 0, tiled=True)  11.9 us
  transfers between devices with their start and end apart: 34, of which 13 were waited for; matrix products, arithmetic and copies ran while one was open for 6% of the time, Pallas kernels for 39%

profile of v2, /device:TPU:0, one launch (start us, length us, event | category | flops | bytes accessed | tf_op | source)
XLA Modules:
  0.0 264.8 jit_solution(17473228903129235854)
XLA Ops:
  10.1 7.4 %all-to-all-start = ((bf16[8,9,64,128]{3,2,1,0:T(8,128)(2,1)}), bf16[8,9,64,128]{3,2,1,0:T(8,128)(2,1)S(1)}, u32[]{:S(2)}, u32[]{:S(2)}) async-start(bf16[8,9,64,128]{3,2,1,0:T(8,128)(2,1)} %pack_wide.1), calls=%async_computation | async-start | bytes 2359296 | tf_op jit(solution)/shard_map/all_to_all | solution.py:861
  23.7 5.3 %upstream_turned.1.refs_5_.refs_2_ = bf16[16,16,16,128]{3,2,1,0:T(8,128)(2,1)} custom-call(s32[4]{0:T(128)} %pad_add_fusion.refs_0_, bf16[16,64,256]{2,1,0:T(8,128)(2,1)} %get-tuple-element.119.refs_1_, bf16[16,64,256]{2,1,0:T(8,128)(2,1)} %copy-done.44), custom_call_target="tpu_custom_call" | custom-call | tf_op jit(solution)/shard_map/upstream_turned/pallas_call | solution.py:90
  29.0 4.4 %collective-permute-done.1.refs_3_ = bf16[16,64,128]{2,1,0:T(8,128)(2,1)S(1)} collective-permute-done((bf16[16,64,128]{2,1,0:T(8,128)(2,1)S(1)}, bf16[16,64,128]{2,1,0:T(8,128)(2,1)S(1)}, u32[]{:S(2)}, u32[]{:S(2)}) %collective-permute-start.1) | collective-permute-done | bytes 262176 | tf_op jit(solution)/shard_map/ppermute | solution.py:823
  33.5 4.9 %collective-permute-done.2.refs_4_ = bf16[16,64,128]{2,1,0:T(8,128)(2,1)S(1)} collective-permute-done((bf16[16,64,128]{2,1,0:T(8,128)(2,1)S(1)}, bf16[16,64,128]{2,1,0:T(8,128)(2,1)S(1)}, u32[]{:S(2)}, u32[]{:S(2)}) %collective-permute-start.2) | collective-permute-done | bytes 262176 | tf_op jit(solution)/shard_map/ppermute | solution.py:823
  39.1 5.4 %features_turned.1.refs_1_.refs_3_.refs_10_ = bf16[10,10,16,512]{3,2,1,0:T(8,128)(2,1)} custom-call(s32[4]{0:T(128)} %pad_add_fusion.refs_0_, bf16[16,64,128]{2,1,0:T(8,128)(2,1)} %copy-done.41, bf16[16,64,128]{2,1,0:T(8,128)(2,1)} %copy-done.47, bf16[16,64,128]{2,1,0:T(8,128)(2,1)} %copy-done.48, bf16[16,64,128]{2,1,0:T(8,128)(2,1)} %copy-done.49, ...), custom_call_target="tpu_custom_call" | custom-call | tf_op jit(solution)/shard_map/features_turned/pallas_call | solution.py:90
  51.3 9.6 %conv_one.1 = (bf16[8,2,8,2,16,128]{5,4,3,2,1,0:T(8,128)(2,1)}, bf16[8,2,8,2,16,128]{5,4,3,2,1,0:T(8,128)(2,1)}, f32[16,128]{1,0:T(8,128)}, f32[16,128]{1,0:T(8,128)}, bf16[16,256,512]{2,1,0:T(8,128)(2,1)}) custom-call(s32[4]{0:T(128)} %pad_add_fusion.refs_0_, bf16[8,9,64,128]{3,2,1,0:T(8,128)(2,1)} %after.8.refs_1_.refs_2_, ...), custom_call_target="tpu_custom_call" | custom-call | tf_op jit(solution)/shard_map/conv_one/pallas_call | solution.py:90
  60.9 1.6 collective-permute-start.5
  63.7 3.6 %all-to-all-start.1 = ((bf16[8,8,16,128]{3,2,1,0:T(8,128)(2,1)}), bf16[8,8,16,128]{3,2,1,0:T(8,128)(2,1)S(1)}, u32[]{:S(2)}, u32[]{:S(2)}) async-start(bf16[8,8,16,128]{3,2,1,0:T(8,128)(2,1)} %skip_quarter.1), calls=%async_computation.1 | async-start | bytes 524288 | tf_op jit(solution)/shard_map/all_to_all | solution.py:861
  67.4 10.4 %all-to-all-done.1.refs_0_ = bf16[8,8,16,128]{3,2,1,0:T(8,128)(2,1)S(1)} async-done(((bf16[8,8,16,128]{3,2,1,0:T(8,128)(2,1)}), bf16[8,8,16,128]{3,2,1,0:T(8,128)(2,1)S(1)}, u32[]{:S(2)}, u32[]{:S(2)}) %all-to-all-start.1) | async-done | bytes 262176 | tf_op jit(solution)/shard_map/all_to_all | solution.py:861
  80.3 16.8 %all_to_all.35.refs_0_ = f32[16,32,128]{2,1,0:T(8,128)} all-to-all(f32[16,32,128]{2,1,0:T(8,128)S(1)} %get-tuple-element.54), channel_id=1, replica_groups={{0,1,4,5,8,9,12,13,16,17,20,21,24,25,28,29},{2,3,6,7,10,11,14,15,18,19,..., dimensions={0} | all-to-all | bytes 524288 | tf_op jit(solution)/shard_map/all_to_all | solution.py:889
  100.8 1.5 collective-permute-start.10
  105.9 2.1 refiner_taps.1
  109.7 9.5 %conv_two.1 = (bf16[18,18,16,256]{3,2,1,0:T(8,128)(2,1)}, f32[16,16,16,128]{3,2,1,0:T(8,128)}, bf16[16,16,16,128]{3,2,1,0:T(8,128)(2,1)}, f32[4,16,128]{2,1,0:T(8,128)}) custom-call(bf16[16,16,16,128]{3,2,1,0:T(8,128)(2,1)} %bitcast.26, bf16[16,16,16,128]{3,2,1,0:T(8,128)(2,1)} %bitcast.29, f32[2,16,128]{2,1,0:T(8,128)} %copy-done.33, ...), custom_call_target="tpu_custom_call" | custom-call | tf_op jit(solution)/shard_map/conv_two/pallas_call | solution.py:90
  121.4 12.9 %all_to_all.36.refs_10_.refs_1_ = f32[16,24,128]{2,1,0:T(8,128)} all-to-all(f32[16,24,128]{2,1,0:T(8,128)S(1)} %broadcast_in_dim.36), channel_id=1, replica_groups={{0,1,4,5,8,9,12,13,16,17,20,21,24,25,28,29},{2,3,6,7,10,11,14,15,18,19,..., dimensions={0} | all-to-all | bytes 393216 | tf_op jit(solution)/shard_map/all_to_all | solution.py:889
  134.3 11.7 %back_two.1 = (bf16[18,18,16,256]{3,2,1,0:T(8,128)(2,1)}, bf16[16,16,16,128]{3,2,1,0:T(8,128)(2,1)}, bf16[16,16,16,128]{3,2,1,0:T(8,128)(2,1)}, f32[3,16,128]{2,...) custom-call(f32[16,16,16,128]{3,2,1,0:T(8,128)} %get-tuple-element.57.refs_0_.refs_3_, ...), custom_call_target="tpu_custom_call" | custom-call | tf_op jit(solution)/shard_map/back_two/pallas_call | solution.py:90
  146.1 1.5 collective-permute-start.13
  147.6 2.6 collective-permute-done.13.refs_1_
  153.7 3.5 %all-to-all-start.4 = ((f32[16,8,128]{2,1,0:T(8,128)}), f32[16,8,128]{2,1,0:T(8,128)S(1)}, u32[]{:S(2)}, u32[]{:S(2)}) async-start(f32[16,8,128]{2,1,0:T(8,128)} %broadcast_in_dim.37), calls=%async_computation.4 | async-start | bytes 131072 | tf_op jit(solution)/shard_map/all_to_all | solution.py:889
  157.2 15.8 %refiner_grad.1 = (bf16[8,5,64,128]{3,2,1,0:T(8,128)(2,1)}, bf16[8,5,64,128]{3,2,1,0:T(8,128)(2,1)}, bf16[16,64,256]{2,1,0:T(8,128)(2,1)}, bf16[16,64,256]{2,1,0:T(8,128)(2,1)}) custom-call(s32[4]{0:T(128)} %pad_add_fusion.refs_0_, bf16[18,18,16,256]{3,2,1,0:T(8,128)(2,1)} %get-tuple-element.62.refs_1_, bf16[18,18,16,256]{3,2,1,0:T(8,128)(2,1)} %get-tuple-element.63.refs_2_, ...), custom_call_target="tpu_custom_call" | custom-call | tf_op jit(solution)/shard_map/refiner_grad/pallas_call | solution.py:90
  175.1 3.2 %collective-permute-done.16.refs_5_ = bf16[128,256]{1,0:T(8,128)(2,1)S(1)} collective-permute-done((bf16[128,256]{1,0:T(8,128)(2,1)S(1)}, bf16[128,256]{1,0:T(8,128)(2,1)S(1)}, u32[]{:S(2)}, u32[]{:S(2)}) %collective-permute-start.16) | collective-permute-done | bytes 65568 | tf_op jit(solution)/shard_map/ppermute | solution.py:823
  179.1 4.0 %excite_back.1 = (bf16[32,128]{1,0:T(8,128)(2,1)}, bf16[8,384,128]{2,1,0:T(8,128)(2,1)}) custom-call(s32[4]{0:T(128)} %pad_add_fusion.refs_0_, f32[2,16,128]{2,1,0:T(8,128)} %copy-done.52, f32[2,16,128]{2,1,0:T(8,128)} %copy-done.55, f32[32,256]{1,0:T(8,128)} %copy-done.31, bf16[128,256]{1,0:T(8,128)(2,1)} %copy-done.21, bf16[128,256]{1,0:T(8,128)(2,1)} %copy-done.53, ...), custom_call_target="tpu_custom_call" | custom-call | tf_op jit(solution)/shard_map/excite_back/pallas_call | solution.py:90
  183.1 5.8 %all-to-all-start.5 = ((bf16[8,384,128]{2,1,0:T(8,128)(2,1)}), bf16[8,384,128]{2,1,0:T(8,128)(2,1)S(1)}, u32[]{:S(2)}, u32[]{:S(2)}) async-start(bf16[8,384,128]{2,1,0:T(8,128)(2,1)} %get-tuple-element.76.refs_11_), calls=%async_computation.5 | async-start | bytes 1572864 | tf_op jit(solution)/shard_map/all_to_all | solution.py:861
  190.2 13.7 %back_one.1 = (bf16[2,2,10,10,16,256]{5,4,3,2,1,0:T(8,128)(2,1)}, f32[8,128]{1,0:T(8,128)}, bf16[8,9,64,128]{3,2,1,0:T(8,128)(2,1)}, bf16[8,9,64,128]{3,2,1,0:T(8,128)(2,1)}) custom-call(s32[4]{0:T(128)} %pad_add_fusion.refs_0_, bf16[8,2,8,2,16,128]{5,4,3,2,1,0:T(8,128)(2,1)} %get-tuple-element.51.refs_1_, ...), custom_call_target="tpu_custom_call" | custom-call | tf_op jit(solution)/shard_map/back_one/pallas_call | solution.py:90
  204.0 3.0 %collective-permute-done.18.refs_1_ = bf16[8,9,64,128]{3,2,1,0:T(8,128)(2,1)S(1)} collective-permute-done((bf16[8,9,64,128]{3,2,1,0:T(8,128)(2,1)}, bf16[8,9,64,128]{3,2,1,0:T(8,128)(2,1)S(1)}, u32[]{:S(2)}, u32[]{:S(2)}) %collective-permute-start.18) | collective-permute-done | bytes 1179680 | tf_op jit(solution)/shard_map/ppermute | solution.py:823
  208.1 3.0 %widener_pair.1.refs_0_ = bf16[8,9,64,128]{3,2,1,0:T(8,128)(2,1)} custom-call(bf16[8,9,64,128]{3,2,1,0:T(8,128)(2,1)} %get-tuple-element.80.refs_0_, bf16[8,9,64,128]{3,2,1,0:T(8,128)(2,1)} %copy-done.38), custom_call_target="tpu_custom_call" | custom-call | tf_op jit(solution)/shard_map/widener_pair/pallas_call | solution.py:90
  212.0 5.8 %all-to-all-start.6 = ((bf16[8,9,64,128]{3,2,1,0:T(8,128)(2,1)}), bf16[8,9,64,128]{3,2,1,0:T(8,128)(2,1)}, u32[]{:S(2)}, u32[]{:S(2)}) async-start(bf16[8,9,64,128]{3,2,1,0:T(8,128)(2,1)} %after.14.refs_3_.refs_2_.refs_1_), calls=%async_computation.6 | async-start | bytes 2359296 | tf_op jit(solution)/shard_map/all_to_all | solution.py:861
  217.9 1.9 collective-permute-done.12
  221.6 4.9 %skip_back.1 = (bf16[32,64,128]{2,1,0:T(8,128)(2,1)}, bf16[32,64,128]{2,1,0:T(8,128)(2,1)}) custom-call(s32[4]{0:T(128)} %pad_add_fusion.refs_0_, bf16[32,128]{1,0:T(8,128)(2,1)} %get-tuple-element.79.refs_1_, bf16[512,2048]{1,0:T(8,128)(2,1)} %all-gather.11.cloned.1.call-done.refs_2_, bf16[8,9,64,128]{3,2,1,0:T(8,128)(2,1)} %after.14.refs_3_.refs_2_.refs_1_), custom_call_target="tpu_custom_call" | custom-call | tf_op jit(solution)/shard_map/skip_back/pallas_call | solution.py:90
  227.1 11.7 %input_back.1 = (bf16[16,64,128]{2,1,0:T(8,128)(2,1)}, bf16[16,64,128]{2,1,0:T(8,128)(2,1)}, bf16[16,64,128]{2,1,0:T(8,128)(2,1)}, bf16[16,64,128]{2,1,0:T(8,128)(2,1)}) custom-call(s32[4]{0:T(128)} %pad_add_fusion.refs_0_, bf16[2,2,10,10,16,256]{5,4,3,2,1,0:T(8,128)(2,1)} %get-tuple-element.77.refs_1_, bf16[16,256,512]{2,1,0:T(8,128)(2,1)} %get-tuple-element.78.refs_2_, ...), custom_call_target="tpu_custom_call" | custom-call | tf_op jit(solution)/shard_map/input_back/pallas_call | solution.py:90
  238.9 1.6 collective-permute-start.19
  245.7 1.7 copy.55.refs_4_
  256.0 2.3 widener_sum.1
  (238 shorter events, 56.9 us)
Async XLA Ops:
  7.2 37.5 %all-gather.7.cloned.1.call-start = ((), (), s32[]{:S(2)}) async-start(), calls=%async_computation.7 | async-start | bytes 1310720 | tf_op jit(solution)/shard_map/all_gather | solution.py:917
  10.1 36.0 %all-to-all-start = ((bf16[8,9,64,128]{3,2,1,0:T(8,128)(2,1)}), bf16[8,9,64,128]{3,2,1,0:T(8,128)(2,1)S(1)}, u32[]{:S(2)}, u32[]{:S(2)}) async-start(bf16[8,9,64,128]{3,2,1,0:T(8,128)(2,1)} %pack_wide.1), calls=%async_computation | async-start | bytes 2359296 | tf_op jit(solution)/shard_map/all_to_all | solution.py:861
  17.5 49.9 %all-gather.9.cloned.1.call-start = ((), (), s32[]{:S(2)}) async-start(), calls=%async_computation.8 | async-start | bytes 1310720 | tf_op jit(solution)/shard_map/all_gather | solution.py:919
  19.0 80.3 %all-gather.15.cloned.1.call-start = ((), (), s32[]{:S(2)}) async-start(), calls=%async_computation.11 | async-start | bytes 1179648 | tf_op jit(solution)/shard_map/all_gather | solution.py:938
  20.1 2.8 %collective-permute-start.3 = (bf16[16,64,256]{2,1,0:T(8,128)(2,1)}, bf16[16,64,256]{2,1,0:T(8,128)(2,1)S(1)}, u32[]{:S(2)}, u32[]{:S(2)}) collective-permute-start(bf16[16,64,256]{2,1,0:T(8,128)(2,1)} %get-tuple-element.118), channel_id=1, source_target_pairs={{0,1},{1,0},{2,3},{3,2},{4,5},{5,4},{6,7},{7,6},{8,9},{9,8},{10,11... | collective-permute-start | bytes 1572872 | tf_op jit(solution)/shard_map/ppermute | solution.py:823
  20.2 8.9 %collective-permute-start = (bf16[16,64,128]{2,1,0:T(8,128)(2,1)S(1)}, bf16[16,64,128]{2,1,0:T(8,128)(2,1)S(1)}, u32[]{:S(2)}, u32[]{:S(2)}) collective-permute-start(bf16[16,64,128]{2,1,0:T(8,128)(2,1)S(1)} %get-tuple-element.120), channel_id=1, source_target_pairs={{0,1},{1,0},{2,3},{3,2},{4,5},{5,4},{6,7},{7,6},{8,9},{9,8},{10,11... | collective-permute-start | bytes 786440 | tf_op jit(solution)/shard_map/ppermute | solution.py:823
  20.7 12.8 %collective-permute-start.1 = (bf16[16,64,128]{2,1,0:T(8,128)(2,1)S(1)}, bf16[16,64,128]{2,1,0:T(8,128)(2,1)S(1)}, u32[]{:S(2)}, u32[]{:S(2)}) collective-permute-start(bf16[16,64,128]{2,1,0:T(8,128)(2,1)S(1)} %get-tuple-element.121.refs_1_), channel_id=1, source_target_pairs={{0,2},{1,3},{2,0},{3,1},{4,6},{5,7},{6,4},{7,5},{8,10},{9,11},{10,... | collective-permute-start | bytes 786440 | tf_op jit(solution)/shard_map/ppermute | solution.py:823
  22.2 16.2 %collective-permute-start.2 = (bf16[16,64,128]{2,1,0:T(8,128)(2,1)S(1)}, bf16[16,64,128]{2,1,0:T(8,128)(2,1)S(1)}, u32[]{:S(2)}, u32[]{:S(2)}) collective-permute-start(bf16[16,64,128]{2,1,0:T(8,128)(2,1)S(1)} %get-tuple-element.120), channel_id=1, source_target_pairs={{0,3},{1,2},{2,1},{3,0},{4,7},{5,6},{6,5},{7,4},{8,11},{9,10},{10,... | collective-permute-start | bytes 786440 | tf_op jit(solution)/shard_map/ppermute | solution.py:823
  47.2 3.1 %collective-permute-start.4 = (bf16[8,9,64,128]{3,2,1,0:T(8,128)(2,1)}, bf16[8,9,64,128]{3,2,1,0:T(8,128)(2,1)S(1)}, u32[]{:S(2)}, u32[]{:S(2)}) collective-permute-start(bf16[8,9,64,128]{3,2,1,0:T(8,128)(2,1)} %after.8.refs_1_.refs_2_), channel_id=1, source_target_pairs={{0,1},{1,0},{2,3},{3,2},{4,5},{5,4},{6,7},{7,6},{8,9},{9,8},{10,11... | collective-permute-start | bytes 3538952 | tf_op jit(solution)/shard_map/ppermute | solution.py:823
  60.9 36.1 %collective-permute-start.5 = (bf16[8,2,8,2,16,128]{5,4,3,2,1,0:T(8,128)(2,1)}, bf16[8,2,8,2,16,128]{5,4,3,2,1,0:T(8,128)(2,1)S(1)}, u32[]{:S(2)}, u32[]{:S(2)}) collective-permute-start(bf16[8,2,8,2,16,128]{5,4,3,2,1,0:T(8,128)(2,1)} %get-tuple-element.51.refs_1_), channel_id=1, source_target_pairs={{0,2},{1,3},{2,0},{3,1},{4,6},{5,7},{6,4},{7,5},{8,10},{9,11},{10,... | collective-permute-start | bytes 3145736 | tf_op jit(solution)/shard_map/ppermute | solution.py:823
  63.7 14.1 %all-to-all-start.1 = ((bf16[8,8,16,128]{3,2,1,0:T(8,128)(2,1)}), bf16[8,8,16,128]{3,2,1,0:T(8,128)(2,1)S(1)}, u32[]{:S(2)}, u32[]{:S(2)}) async-start(bf16[8,8,16,128]{3,2,1,0:T(8,128)(2,1)} %skip_quarter.1), calls=%async_computation.1 | async-start | bytes 524288 | tf_op jit(solution)/shard_map/all_to_all | solution.py:861
  67.3 154.3 %all-gather.11.cloned.1.call-start = ((), (), s32[]{:S(2)}) async-start(), calls=%async_computation.9 | async-start | bytes 2359296 | tf_op jit(solution)/shard_map/all_gather | solution.py:1043
  99.3 5.3 %collective-permute-start.8 = (bf16[8,8,64,128]{3,2,1,0:T(8,128)(2,1)}, bf16[8,8,64,128]{3,2,1,0:T(8,128)(2,1)S(1)}, u32[]{:S(2)}, u32[]{:S(2)}) collective-permute-start(bf16[8,8,64,128]{3,2,1,0:T(8,128)(2,1)} %after.10.refs_1_), channel_id=1, source_target_pairs={{0,1},{1,0},{2,3},{3,2},{4,5},{5,4},{6,7},{7,6},{8,9},{9,8},{10,11... | collective-permute-start | bytes 3145736 | tf_op jit(solution)/shard_map/ppermute | solution.py:823
  100.8 3.7 %collective-permute-start.10 = (f32[8,256]{1,0:T(8,128)S(1)}, f32[8,256]{1,0:T(8,128)S(1)}, u32[]{:S(2)}, u32[]{:S(2)}) collective-permute-start(f32[8,256]{1,0:T(8,128)S(1)} %part_sum.1.refs_1_), channel_id=1, source_target_pairs={{0,2},{1,3},{2,0},{3,1},{4,6},{5,7},{6,4},{7,5},{8,10},{9,11},{10,... | collective-permute-start | bytes 24584 | tf_op jit(solution)/shard_map/ppermute | solution.py:823
  102.4 16.8 %collective-permute-start.9 = (f32[8,256]{1,0:T(8,128)S(1)}, f32[8,256]{1,0:T(8,128)S(1)}, u32[]{:S(2)}, u32[]{:S(2)}) collective-permute-start(f32[8,256]{1,0:T(8,128)S(1)} %part_sum.1.refs_1_), channel_id=1, source_target_pairs={{0,1},{1,0},{2,3},{3,2},{4,5},{5,4},{6,7},{7,6},{8,9},{9,8},{10,11... | collective-permute-start | bytes 24584 | tf_op jit(solution)/shard_map/ppermute | solution.py:823
  102.5 6.5 %collective-permute-start.7 = (f32[2,16,128]{2,1,0:T(8,128)S(1)}, f32[2,16,128]{2,1,0:T(8,128)S(1)}, u32[]{:S(2)}, u32[]{:S(2)}) collective-permute-start(f32[2,16,128]{2,1,0:T(8,128)S(1)} %get-tuple-element.55.refs_2_), channel_id=1, source_target_pairs={{0,2},{1,3},{2,0},{3,1},{4,6},{5,7},{6,4},{7,5},{8,10},{9,11},{10,... | collective-permute-start | bytes 49160 | tf_op jit(solution)/shard_map/ppermute | solution.py:823
  104.5 14.6 %collective-permute-start.11 = (f32[8,256]{1,0:T(8,128)S(1)}, f32[8,256]{1,0:T(8,128)S(1)}, u32[]{:S(2)}, u32[]{:S(2)}) collective-permute-start(f32[8,256]{1,0:T(8,128)S(1)} %collective-permute-done.10.refs_3_), channel_id=1, source_target_pairs={{0,1},{1,0},{2,3},{3,2},{4,5},{5,4},{6,7},{7,6},{8,9},{9,8},{10,11... | collective-permute-start | bytes 24584 | tf_op jit(solution)/shard_map/ppermute | solution.py:823
  146.1 4.1 %collective-permute-start.13 = (f32[3,16,128]{2,1,0:T(8,128)}, f32[3,16,128]{2,1,0:T(8,128)S(1)}, u32[]{:S(2)}, u32[]{:S(2)}) collective-permute-start(f32[3,16,128]{2,1,0:T(8,128)} %get-tuple-element.70), channel_id=1, source_target_pairs={{0,2},{1,3},{2,0},{3,1},{4,6},{5,7},{6,4},{7,5},{8,10},{9,11},{10,... | collective-permute-start | bytes 73736 | tf_op jit(solution)/shard_map/ppermute | solution.py:823
  150.8 38.4 %collective-permute-start.14 = (bf16[16,16,16,128]{3,2,1,0:T(8,128)(2,1)}, bf16[16,16,16,128]{3,2,1,0:T(8,128)(2,1)S(1)}, u32[]{:S(2)}, u32[]{:S(2)}) collective-permute-start(bf16[16,16,16,128]{3,2,1,0:T(8,128)(2,1)} %after.11), channel_id=1, source_target_pairs={{0,2},{1,3},{2,0},{3,1},{4,6},{5,7},{6,4},{7,5},{8,10},{9,11},{10,... | collective-permute-start | bytes 3145736 | tf_op jit(solution)/shard_map/ppermute | solution.py:823
  153.7 19.4 %all-to-all-start.4 = ((f32[16,8,128]{2,1,0:T(8,128)}), f32[16,8,128]{2,1,0:T(8,128)S(1)}, u32[]{:S(2)}, u32[]{:S(2)}) async-start(f32[16,8,128]{2,1,0:T(8,128)} %broadcast_in_dim.37), calls=%async_computation.4 | async-start | bytes 131072 | tf_op jit(solution)/shard_map/all_to_all | solution.py:889
  173.7 4.6 %collective-permute-start.17 = (bf16[8,5,64,128]{3,2,1,0:T(8,128)(2,1)}, bf16[8,5,64,128]{3,2,1,0:T(8,128)(2,1)S(1)}, u32[]{:S(2)}, u32[]{:S(2)}) collective-permute-start(bf16[8,5,64,128]{3,2,1,0:T(8,128)(2,1)} %after.12), channel_id=1, source_target_pairs={{0,1},{1,0},{2,3},{3,2},{4,5},{5,4},{6,7},{7,6},{8,9},{9,8},{10,11... | collective-permute-start | bytes 1966088 | tf_op jit(solution)/shard_map/ppermute | solution.py:823
  174.0 4.3 %collective-permute-start.16 = (bf16[128,256]{1,0:T(8,128)(2,1)S(1)}, bf16[128,256]{1,0:T(8,128)(2,1)S(1)}, u32[]{:S(2)}, u32[]{:S(2)}) collective-permute-start(bf16[128,256]{1,0:T(8,128)(2,1)S(1)} %get-tuple-element.59.refs_5_.refs_4_), channel_id=1, source_target_pairs={{0,2},{1,3},{2,0},{3,1},{4,6},{5,7},{6,4},{7,5},{8,10},{9,11},{10,... | collective-permute-start | bytes 196616 | tf_op jit(solution)/shard_map/ppermute | solution.py:823
  175.0 3.2 %collective-permute-start.15 = (f32[2,16,128]{2,1,0:T(8,128)S(1)}, f32[2,16,128]{2,1,0:T(8,128)S(1)}, u32[]{:S(2)}, u32[]{:S(2)}) collective-permute-start(f32[2,16,128]{2,1,0:T(8,128)S(1)} %pad_maximum_fusion.refs_1_), channel_id=1, source_target_pairs={{0,1},{1,0},{2,3},{3,2},{4,5},{5,4},{6,7},{7,6},{8,9},{9,8},{10,11... | collective-permute-start | bytes 49160 | tf_op jit(solution)/shard_map/ppermute | solution.py:823
  183.1 28.0 %all-to-all-start.5 = ((bf16[8,384,128]{2,1,0:T(8,128)(2,1)}), bf16[8,384,128]{2,1,0:T(8,128)(2,1)S(1)}, u32[]{:S(2)}, u32[]{:S(2)}) async-start(bf16[8,384,128]{2,1,0:T(8,128)(2,1)} %get-tuple-element.76.refs_11_), calls=%async_computation.5 | async-start | bytes 1572864 | tf_op jit(solution)/shard_map/all_to_all | solution.py:861
  188.9 53.9 %all-gather.13.cloned.1.call-start = ((), (), s32[]{:S(2)}) async-start(), calls=%async_computation.10 | async-start | bytes 1310720 | tf_op jit(solution)/shard_map/all_gather | solution.py:1189
  203.9 3.1 %collective-permute-start.18 = (bf16[8,9,64,128]{3,2,1,0:T(8,128)(2,1)}, bf16[8,9,64,128]{3,2,1,0:T(8,128)(2,1)S(1)}, u32[]{:S(2)}, u32[]{:S(2)}) collective-permute-start(bf16[8,9,64,128]{3,2,1,0:T(8,128)(2,1)} %get-tuple-element.81), channel_id=1, source_target_pairs={{0,1},{1,0},{2,3},{3,2},{4,5},{5,4},{6,7},{7,6},{8,9},{9,8},{10,11... | collective-permute-start | bytes 3538952 | tf_op jit(solution)/shard_map/ppermute | solution.py:823
  212.0 42.0 %all-to-all-start.6 = ((bf16[8,9,64,128]{3,2,1,0:T(8,128)(2,1)}), bf16[8,9,64,128]{3,2,1,0:T(8,128)(2,1)}, u32[]{:S(2)}, u32[]{:S(2)}) async-start(bf16[8,9,64,128]{3,2,1,0:T(8,128)(2,1)} %after.14.refs_3_.refs_2_.refs_1_), calls=%async_computation.6 | async-start | bytes 2359296 | tf_op jit(solution)/shard_map/all_to_all | solution.py:861
  226.6 22.9 %collective-permute-start.22 = (bf16[32,64,128]{2,1,0:T(8,128)(2,1)}, bf16[32,64,128]{2,1,0:T(8,128)(2,1)}, u32[]{:S(2)}, u32[]{:S(2)}) collective-permute-start(bf16[32,64,128]{2,1,0:T(8,128)(2,1)} %get-tuple-element.82.refs_3_), channel_id=1, source_target_pairs={{0,2},{1,3},{2,0},{3,1},{4,6},{5,7},{6,4},{7,5},{8,10},{9,11},{10,... | collective-permute-start | bytes 1572872 | tf_op jit(solution)/shard_map/ppermute | solution.py:823
  238.9 9.6 %collective-permute-start.19 = (bf16[16,64,128]{2,1,0:T(8,128)(2,1)}, bf16[16,64,128]{2,1,0:T(8,128)(2,1)}, u32[]{:S(2)}, u32[]{:S(2)}) collective-permute-start(bf16[16,64,128]{2,1,0:T(8,128)(2,1)} %get-tuple-element.84), channel_id=1, source_target_pairs={{0,2},{1,3},{2,0},{3,1},{4,6},{5,7},{6,4},{7,5},{8,10},{9,11},{10,... | collective-permute-start | bytes 786440 | tf_op jit(solution)/shard_map/ppermute | solution.py:823
  240.5 10.3 %collective-permute-start.20 = (bf16[16,64,128]{2,1,0:T(8,128)(2,1)}, bf16[16,64,128]{2,1,0:T(8,128)(2,1)S(1)}, u32[]{:S(2)}, u32[]{:S(2)}) collective-permute-start(bf16[16,64,128]{2,1,0:T(8,128)(2,1)} %get-tuple-element.85), channel_id=1, source_target_pairs={{0,1},{1,0},{2,3},{3,2},{4,5},{5,4},{6,7},{7,6},{8,9},{9,8},{10,11... | collective-permute-start | bytes 786440 | tf_op jit(solution)/shard_map/ppermute | solution.py:823
  240.5 11.5 %collective-permute-start.21 = (bf16[16,64,128]{2,1,0:T(8,128)(2,1)}, bf16[16,64,128]{2,1,0:T(8,128)(2,1)}, u32[]{:S(2)}, u32[]{:S(2)}) collective-permute-start(bf16[16,64,128]{2,1,0:T(8,128)(2,1)} %get-tuple-element.86), channel_id=1, source_target_pairs={{0,3},{1,2},{2,1},{3,0},{4,7},{5,6},{6,5},{7,4},{8,11},{9,10},{10,... | collective-permute-start | bytes 786440 | tf_op jit(solution)/shard_map/ppermute | solution.py:823
  250.7 2.4 collective-permute-start.23
  (67 other events, 367.7 us)
Sparse Core Ops, SparseCore 0:
  9.6 23.6 all-gather.6
  34.8 16.2 all-gather.8
  53.8 45.4 all-gather.14
  134.5 47.5 all-gather.10
  204.1 17.0 all-gather.12

commit v3 on v2

--- a/solution.py
+++ b/solution.py
@@ -10,6 +10,7 @@
 f32 = jnp.float32
 bf16 = jnp.bfloat16
 MIB = 2**20
+LIMIT = 58
 
 NT = (((1,), (1,)), ((), ()))
 TN = (((0,), (0,)), ((), ()))
@@ -22,27 +23,46 @@
 
 
 class Traffic:
-    def __init__(self, ins, outs, in_sems, out_sems, late):
-        self.ins = [
-            pltpu.make_async_copy(src, dst, in_sems.at[k]) for k, (src, dst) in enumerate(ins)
-        ]
-        self.outs, self.out_sems = outs, out_sems
+    def __init__(self, ins, outs, in_sems, out_sems, late, cuts):
+        self.ins, self.outs, self.out_sems = [], outs, out_sems
         self.sent = {}
-        for k, copy in enumerate(self.ins):
-            copy.start()
-        for k, copy in enumerate(self.ins):
-            if k not in late:
-                copy.wait()
+        count = 0
+        for k, (pieces, held) in enumerate(ins):
+            copies, at = [], 0
+            parts = cuts.get(k, 1)
+            for piece in pieces:
+                rows = piece.shape[0] // parts
+                for n in range(parts):
+                    src = piece.at[pl.ds(n * rows, rows)]
+                    dst = held.at[pl.ds(at, rows)]
+                    copies.append(pltpu.make_async_copy(src, dst, in_sems.at[count]))
+                    count += 1
+                    at += rows
+            self.ins.append(copies)
+        for copies in self.ins:
+            for copy in copies:
+                copy.start()
+        self.need(*[k for k in range(len(ins)) if k not in late])
 
     def need(self, *which):
         for k in which:
-            self.ins[k].wait()
+            for copy in self.ins[k]:
+                copy.wait()
+
+    def need_part(self, k, n):
+        self.ins[k][n].wait()
 
     def part(self, k, n, count):
-        src, dst = self.outs[k]
-        rows = src.shape[0] // count
-        cut = pl.ds(n * rows, rows)
-        return pltpu.make_async_copy(src.at[cut], dst.at[cut], self.out_sems.at[k, n])
+        made, pieces = self.outs[k]
+        rows = made.shape[0] // count
+        if len(pieces) == 1:
+            dst = pieces[0].at[pl.ds(n * rows, rows)]
+        else:
+            each = pieces[0].shape[0]
+            dst = pieces[n * rows // each].at[pl.ds(n * rows % each, rows)]
+        return pltpu.make_async_copy(
+            made.at[pl.ds(n * rows, rows)], dst, self.out_sems.at[k, n]
+        )
 
     def send(self, k, n=0, count=1):
         self.sent[k] = count
@@ -51,56 +71,78 @@
     def finish(self):
         for k in range(len(self.outs)):
             if k not in self.sent:
-                self.send(k)
+                for n in range(len(self.outs[k][1])):
+                    self.send(k, n, len(self.outs[k][1]))
         for k, count in self.sent.items():
             for n in range(count):
                 self.part(k, n, count).wait()
 
 
-def call(body, outs, args, name, scratch=(), smem=1, deps=(), late=(), plain=False):
-    outs = [jax.ShapeDtypeStruct(shape, dtype) for shape, dtype in outs]
-    args, deps = list(args), list(deps)
-    big = len(args) - smem
-    count = len(outs)
+def grouped(refs, sizes):
+    out, at = [], 0
+    for size in sizes:
+        out.append(refs[at : at + size])
+        at += size
+    return out
+
+
+def call(body, outs, args, name, scratch=(), smem=1, deps=(), late=(), cuts={}, plain=False):
+    scalars, args, deps = list(args[:smem]), list(args[smem:]), list(deps)
+    args = [a if isinstance(a, tuple) else (a,) for a in args]
+    outs = [o if len(o) == 3 else (*o, 1) for o in outs]
+    in_sizes, out_sizes = [len(a) for a in args], [o[2] for o in outs]
+    n_in, n_out = sum(in_sizes), sum(out_sizes)
+    results = [
+        jax.ShapeDtypeStruct((shape[0] // count, *shape[1:]), dtype)
+        for shape, dtype, count in outs
+        for _ in range(count)
+    ]
     anywhere, inside = pl.BlockSpec(memory_space=pl.ANY), pl.BlockSpec(memory_space=pltpu.VMEM)
 
     def kernel(*refs):
         refs = list(refs)
-        scalars, refs = refs[:smem], refs[smem:]
-        ins, refs = refs[:big], refs[big + len(deps) :]
-        results, refs = refs[:count], refs[count:]
+        numbers, refs = refs[:smem], refs[smem:]
+        ins, refs = refs[:n_in], refs[n_in + len(deps) :]
+        made, refs = refs[:n_out], refs[n_out:]
         if plain:
-            body(*scalars, *ins, *results, *refs)
+            body(*numbers, *ins, *made, *refs)
             return
-        held, refs = refs[:big], refs[big:]
-        made, refs = refs[:count], refs[count:]
-        in_sems, out_sems = refs[0], refs[1]
+        held, refs = refs[: len(args)], refs[len(args) :]
+        work, refs = refs[: len(outs)], refs[len(outs) :]
         traffic = Traffic(
-            list(zip(ins, held)), list(zip(made, results)), in_sems, out_sems, late
+            list(zip(grouped(ins, in_sizes), held)),
+            list(zip(work, grouped(made, out_sizes))),
+            refs[0],
+            refs[1],
+            late,
+            cuts,
         )
         extra = (traffic,) if late else ()
-        body(*extra, *scalars, *held, *made, *refs[2:])
+        body(*extra, *numbers, *held, *work, *refs[2:])
         traffic.finish()
 
     own = []
     if not plain:
-        own = [pltpu.VMEM(a.shape, a.dtype) for a in args[smem:]]
-        own += [pltpu.VMEM(o.shape, o.dtype) for o in outs]
-        own += [pltpu.SemaphoreType.DMA((big,)), pltpu.SemaphoreType.DMA((count, 8))]
-    return pl.pallas_call(
+        own = [
+            pltpu.VMEM((sum(p.shape[0] for p in a), *a[0].shape[1:]), a[0].dtype) for a in args
+        ]
+        own += [pltpu.VMEM(shape, dtype) for shape, dtype, _ in outs]
+        own += [pltpu.SemaphoreType.DMA((n_in * max([1, *cuts.values()]),)), pltpu.SemaphoreType.DMA((len(outs), 8))]
+    got = pl.pallas_call(
         kernel,
-        out_shape=outs,
+        out_shape=results,
         in_specs=[pl.BlockSpec(memory_space=pltpu.SMEM)] * smem
-        + [inside if plain else anywhere] * big
+        + [inside if plain else anywhere] * n_in
         + [anywhere] * len(deps),
-        out_specs=[inside if plain else anywhere] * count,
+        out_specs=[inside if plain else anywhere] * n_out,
         scratch_shapes=own + list(scratch),
         compiler_params=pltpu.CompilerParams(
-            vmem_limit_bytes=(16 if plain else 56) * MIB
+            vmem_limit_bytes=(16 if plain else LIMIT) * MIB
         ),
         cost_estimate=pl.CostEstimate(flops=0, bytes_accessed=0, transcendentals=0),
         name=name,
-    )(*args, *deps)
+    )(*scalars, *[p for a in args for p in a], *deps)
+    return [p[0] if len(p) == 1 else tuple(p) for p in grouped(list(got), out_sizes)]
 
 
 def after(value, *deps):
@@ -148,8 +190,8 @@
         out[k] = packed
 
 
-def pack_fine_body(r, e, out):
-    slots = [r[q // 2, q % 2] for q in range(18)] + [e[...], jnp.zeros_like(e[...])]
+def pack_fine_body(r, e, e_other, out):
+    slots = [r[q // 2, q % 2] for q in range(18)] + [e[...], e_other[...]]
     for row in range(5):
         out[row] = jnp.concatenate(slots[4 * row : 4 * row + 4], axis=-1)
     out[5:] = jnp.zeros((3, 64, 128), bf16)
@@ -192,23 +234,17 @@
                                 ] = across[(b, v)].astype(bf16)
 
 
-def refiner_select(chip):
-    r, q = iota((1024, 1024), 0), iota((1024, 1024), 1)
-    channel = (r // 128) * 32 + r % 32
-    return onehot((((r // 32) % 4) == (q // 256)) & ((channel ^ (chip * 128)) == (q % 256)))
-
-
-def refiner_body(idx, own, other, out, ex):
-    core, chip = idx[1], idx[2]
-    select = refiner_select(chip)
+def refiner_body(idx, own, other, out, ex, ex_other):
+    core = idx[1]
     for blocks, side in ((own, core), (other, 1 - core)):
         rows = pl.multiple_of(side * 64, 64)
-        raw = jnp.concatenate([blocks[k, :5].reshape(320, 128) for k in range(8)], axis=-1)
-        got = dot(raw, select).astype(bf16)
-        for q in range(18):
-            piece = got[(q // 4) * 64 : (q // 4) * 64 + 64, (q % 4) * 256 : (q % 4) * 256 + 256]
-            out[q // 2, pl.ds(rows + (q % 2) * 128, 64), :] = piece
-        ex[pl.ds(rows, 64), :] = got[256:320, 512:768]
+        for q in range(20):
+            lanes = slice((q % 4) * 32, (q % 4) * 32 + 32)
+            piece = jnp.concatenate([blocks[k, q // 4][:, lanes] for k in range(8)], axis=-1)
+            if q < 18:
+                out[q // 2, pl.ds(rows + (q % 2) * 128, 64), :] = piece
+            else:
+                (ex, ex_other)[q - 18][pl.ds(rows, 64), :] = piece
 
 
 def feature_select(place):
@@ -244,10 +280,11 @@
     swap = sixteen_swap()
     select = feature_select(idx[0])
 
-    io.need(1)
     acc = None
     for a in range(2):
+        io.need_part(0, a)
         for b in range(2):
+            io.need_part(1, 2 * a + b)
             lhs = jnp.concatenate(
                 [
                     d[a, b, 2 - u - a : 10 - u - a, 2 - v - b : 10 - v - b].reshape(1024, 256)
@@ -276,6 +313,12 @@
         return carry
 
     lax.fori_loop(0, 16, turn, 0, unroll=4)
+
+
+def input_join_body(idx, b0, b1, b2, b3, out):
+    at = pl.multiple_of(idx[1] * 16, 16)
+    out[pl.ds(at, 16)] = b0[...].astype(f32) + b2[...].astype(f32)
+    out[pl.ds(16 - at, 16)] = b1[...].astype(f32) + b3[...].astype(f32)
 
 
 def upstream_body(idx, own, other, out, turned):
@@ -354,16 +397,14 @@
     base[...] = mean_s
     io.send(2)
 
-    def spread(i, acc):
+    squares = jnp.zeros((16, 128), f32)
+    for i in range(8):
         for a in range(2):
             for b in range(2):
                 d = glu[a, b, i] - mean_s[None]
                 gap[i, a, :, b] = d.astype(bf16)
-                acc = acc + jnp.sum(d * d, axis=0)
+                squares = squares + jnp.sum(d * d, axis=0)
         io.send(0, i, 8)
-        return acc
-
-    squares = lax.fori_loop(0, 8, spread, jnp.zeros((16, 128), f32))
     n, mean, squares = local_stats(mask[...], mean_s, squares)
     msg[0:4] = n
     msg[4:8] = mean
@@ -372,7 +413,7 @@
 
 
 def make_scale_body(entries):
-    def body(mask, gains, base, messages, line, stat):
+    def body(idx, mask, gains, base, messages, line, stat):
         mean, inverse = total_stats(message_list([messages]), entries)
         m = mask[...]
         mean_s, inverse_s = per_sample(m, mean), per_sample(m, inverse)
@@ -381,11 +422,17 @@
         scale = inverse_s * gains[0:1]
         line[0] = scale
         line[1] = (base[...] - mean_s) * scale + gains[1:2]
+        if messages.shape[0] == 16 and messages.shape[1] == 32:
+            core = idx[1]
+            line[2, 0:8] = tree([messages[2 * k + core, 16:24] for k in range(8)])
+            line[2, 8:16] = tree([messages[2 * k + core, 24:32] for k in range(8)])
+        else:
+            line[2] = jnp.zeros((16, 128), f32)
 
     return body
 
 
-def conv_two_body(io, own, other, line, line_other, w, up, held, glu, logit, sums):
+def conv_two_body(io, idx, own, other, line, line_other, w, up, held, glu, logit, sums):
     zero = jnp.zeros((18, 16, 256), bf16)
     held[0] = zero
     held[17] = zero
@@ -393,12 +440,13 @@
     held[:, 17] = zero
 
     def fill(y, carry):
-        for gap, scale, lanes in ((own, line, 0), (other, line_other, 128)):
+        for gap, scale, side in ((own, line, idx[2]), (other, line_other, 1 - idx[2])):
             h = gap[y].astype(f32) * scale[0] + scale[1]
-            held[y + 1, 1:17, :, lanes : lanes + 128] = h.astype(bf16)
+            lanes = pl.ds(pl.multiple_of(side * 128, 128), 128)
+            held[y + 1, 1:17, :, lanes] = h.astype(bf16)
         return carry
 
-    lax.fori_loop(0, 16, fill, 0)
+    lax.fori_loop(0, 16, fill, 0, unroll=2)
     io.send(0)
     io.need(4)
 
@@ -420,7 +468,7 @@
         io.send(2, step, 4)
         return total + jnp.sum(g, axis=(0, 1))
 
-    total = lax.fori_loop(0, 4, rows, jnp.zeros((16, 128), f32))
+    total = lax.fori_loop(0, 4, rows, jnp.zeros((16, 128), f32), unroll=True)
     mean_s = total * (1.0 / 256.0)
 
     io.need(5)
@@ -443,7 +491,7 @@
 
 
 def make_back_two_body(entries):
-    def body(io, glu, logit, up, mask, pull, gains, sums, w, gap, gap_other, messages, *outs):
+    def body(io, idx, glu, logit, up, mask, pull, gains, sums, w, gap, gap_other, messages, *outs):
         grad, own, other, small, stat, mine = outs
         messages = message_list([messages])
         mean, inverse = total_stats(messages, entries)
@@ -480,7 +528,7 @@
             grad[y + 1, 1:17, :, 128:256] = (d * g * (1.0 - s)).astype(bf16)
             return carry
 
-        lax.fori_loop(0, 16, step, 0)
+        lax.fori_loop(0, 16, step, 0, unroll=2)
         io.send(0)
         io.need(7, 8, 9)
 
@@ -495,17 +543,22 @@
             )
             c = dot(lhs, w[...].reshape(2304, 256)).astype(bf16)
             out = []
-            for ref, at, lanes in ((own, gap, 0), (other, gap_other, 128)):
-                d = c[:, lanes : lanes + 128].reshape(4, 16, 16, 128)
+            first = idx[2] == 0
+            mine_c = jnp.where(first, c[:, :128], c[:, 128:])
+            their_c = jnp.where(first, c[:, 128:], c[:, :128])
+            for k, ref, at, d in ((1, own, gap, mine_c), (2, other, gap_other, their_c)):
+                d = d.reshape(4, 16, 16, 128)
                 ref[pl.ds(y, 4)] = d
-                io.send(1 if lanes == 0 else 2, step, 4)
+                io.send(k, step, 4)
                 d = d.astype(f32)
                 out.append(jnp.sum(d, axis=(0, 1)))
                 out.append(jnp.sum(d * at[pl.ds(y, 4)].astype(f32), axis=(0, 1)))
             return tuple(p + q for p, q in zip(acc, out))
 
         none = jnp.zeros((16, 128), f32)
-        mine[0], mine[1], small[0], small[1] = lax.fori_loop(0, 4, rows, (none,) * 4)
+        mine[0], mine[1], small[0], small[1] = lax.fori_loop(
+            0, 4, rows, (none,) * 4, unroll=True
+        )
 
     return body
 
@@ -538,7 +591,7 @@
 def refiner_grad_body(
     io, idx, grad, held, glu, stat, pull, gains, own, other, out_own, out_other, work, turned
 ):
-    core, chip = idx[1], idx[2]
+    core = idx[1]
 
     def tap(t, carry):
         d = grad[1:17, 1:17].reshape(4096, 256)
@@ -546,22 +599,18 @@
         work[t] = dot(d, h, TN).astype(bf16)
         return carry
 
-    lax.fori_loop(0, 9, tap, 0)
-    select = refiner_select(chip)
+    lax.fori_loop(0, 9, tap, 0, unroll=3)
     for out, side in ((own, core), (other, 1 - core)):
         start = pl.multiple_of(side * 64, 64)
-        rows = []
         for row in range(5):
-            pieces = []
-            for q in range(4 * row, 4 * row + 4):
-                if q < 18:
-                    pieces.append(work[q // 2, pl.ds(start + (q % 2) * 128, 64), :])
-                else:
-                    pieces.append(jnp.zeros((64, 256), bf16))
-            rows.append(jnp.concatenate(pieces, axis=-1))
-        got = dot(jnp.concatenate(rows, axis=0), select, NT).astype(bf16)
-        for k in range(8):
-            out[k] = got[:, k * 128 : k * 128 + 128].reshape(5, 64, 128)
+            pieces = [
+                work[q // 2, pl.ds(start + (q % 2) * 128, 64), :]
+                for q in range(4 * row, min(4 * row + 4, 18))
+            ]
+            pieces += [jnp.zeros((64, 256), bf16)] * (4 - len(pieces))
+            for k in range(8):
+                lanes = slice(k * 32, k * 32 + 32)
+                out[k, row] = jnp.concatenate([p[:, lanes] for p in pieces], axis=-1)
     io.send(0)
     io.send(1)
     io.need(2, 3, 4, 5)
@@ -575,12 +624,13 @@
         out[q // 2, q % 2] = total[rows, (q % 4) * 32 : (q % 4) * 32 + 32]
 
 
-def first_sums_body(mine, theirs, mask, stat, msg):
+def first_sums_body(mine, theirs, mask, stat, payload):
     m = mask[...]
     plain = mine[0] + theirs[0]
     cross = mine[1] + theirs[1] + stat[0] * plain
-    msg[0:4] = over_samples(m, plain)
-    msg[4:8] = over_samples(m, cross * stat[1])
+    msg = jnp.concatenate([over_samples(m, plain), over_samples(m, cross * stat[1])], axis=0)
+    for k in range(payload.shape[0]):
+        payload[k] = msg
 
 
 def make_back_one_body(entries):
@@ -655,7 +705,7 @@
                 work[n, 2 * u + v] = dot(d, f, TN)
         return carry
 
-    lax.fori_loop(0, 4, phase, 0)
+    lax.fori_loop(0, 4, phase, 0, unroll=2)
     source = {0: (0, 0), 1: (1, 0), 2: (1, 1)}
     for out, side in ((own, core), (other, 1 - core)):
         start = pl.multiple_of(side * 64, 64)
@@ -682,8 +732,12 @@
                     ).astype(bf16)
 
 
-def pair_sum_body(own, other, out):
-    out[...] = (own[...].astype(f32) + other[...].astype(f32)).astype(bf16)
+def pair_sum_body(io, own, other, out):
+    for k in range(8):
+        io.need_part(0, k)
+        io.need_part(1, k)
+        out[k] = (own[k].astype(f32) + other[k].astype(f32)).astype(bf16)
+        io.send(0, k, 8)
 
 
 def widener_sum_body(parts, out):
@@ -711,37 +765,33 @@
             out[2 * i + c, 24:32] = part[i * 8 : i * 8 + 8, 128:]
 
 
-def part_sum_body(idx, parts, out):
-    core = idx[1]
-    out[:, :128] = tree([parts[2 * k + core, 16:24] for k in range(8)])
-    out[:, 128:] = tree([parts[2 * k + core, 24:32] for k in range(8)])
-
-
-def own_first(v, chip):
-    return jnp.where(chip == 0, v, jnp.concatenate([v[:, 128:], v[:, :128]], axis=-1))
-
-
 def gate_body(idx, s0, s1, s2, s3, ex, weight, out, squeezed):
-    j, core, chip = idx[0], idx[1], idx[2]
+    j, core = idx[0], idx[1]
     for n, part in enumerate((s0, s1, s2, s3)):
-        squeezed[pl.ds(pl.multiple_of((j ^ n) * 8, 8), 8), :] = part[...]
+        rows = pl.ds(pl.multiple_of((j ^ n) * 8, 8), 8)
+        squeezed[rows, :128] = part[2, 0:8]
+        squeezed[rows, 128:] = part[2, 8:16]
     mine = squeezed[pl.ds(pl.multiple_of(core * 16, 16), 16), :]
-    excited = dot(own_first(mine * sigmoid(mine), chip).astype(bf16), ex[...], NT)
+    excited = dot((mine * sigmoid(mine)).astype(bf16), ex[...], NT)
     out[0] = weight[...]
     out[1] = sigmoid(excited)
 
 
-def message_two_body(mask, pull, sums, msg):
+def gate_message_body(idx, s0, s1, s2, s3, ex, weight, mask, sums, out, squeezed, payload):
+    gate_body(idx, s0, s1, s2, s3, ex, weight, out, squeezed)
+    message_two_body(mask, out, sums, payload)
+
+
+def message_two_body(mask, pull, sums, payload):
     mean_s, plain, cross = sums[0], sums[1], sums[2]
     m = mask[...]
     n, mean, squares = local_stats(m, mean_s, sums[3])
     factor = pull[0] * pull[1]
-    msg[0:4] = n
-    msg[4:8] = mean
-    msg[8:12] = squares
-    msg[12:16] = over_samples(m, factor * plain)
-    msg[16:20] = over_samples(m, factor * (cross + plain * (mean_s - per_sample(m, mean))))
-    msg[20:24] = jnp.zeros((4, 128), f32)
+    spread = over_samples(m, factor * (cross + plain * (mean_s - per_sample(m, mean))))
+    rows = [n, mean, squares, over_samples(m, factor * plain), spread, jnp.zeros((4, 128), f32)]
+    msg = jnp.concatenate(rows, axis=0)
+    for k in range(payload.shape[0]):
+        payload[k] = msg
 
 
 def excite_back_body(idx, g0, g1, squeezed, ex_own, ex_other, fine, recv, vectors, out):
@@ -749,11 +799,10 @@
     s = squeezed[...]
     sigm = sigmoid(s)
     swish = (s * sigm).astype(bf16)
-    mine = own_first(ex_own[...].astype(f32), chip)
-    theirs = own_first(ex_other[...].astype(f32), 1 - chip)
+    mine, theirs = ex_own[...], ex_other[...]
     ex = jnp.where(
         chip == 0, jnp.concatenate([mine, theirs], axis=0), jnp.concatenate([theirs, mine], axis=0)
-    ).astype(bf16)
+    )
     gate = sigmoid(dot(swish, ex, NT))
     core = idx[1]
     rows = []
@@ -789,34 +838,46 @@
     )
 
 
-def squeeze_back_body(parts, skips, ex_grad, sq_grad):
+def squeeze_back_body(parts, skips, ex_grad, sq_grad, refiner_out):
+    refiner_sum_body(parts, refiner_out)
     vectors = jnp.concatenate([parts[k, 320:352] for k in range(8)], axis=0)
     swish = jnp.concatenate([parts[k, 352:384] for k in range(8)], axis=0)
     ex_grad[...] = dot(vectors, swish, TN)[64:, :32]
-    sq_grad[...] = dot(quarters_first(vectors).astype(bf16), skips[...], TN)[:64]
-
-
-def skip_back_body(idx, vectors, kernels, keep, send, rows):
+    grad = dot(quarters_first(vectors).astype(bf16), skips[...], TN)
+    for t in range(16):
+        sq_grad[t] = grad[:64, t * 128 : t * 128 + 128]
+
+
+def skip_back_body(io, idx, vectors, kernels, keep, send):
     d = vectors[:, :64]
     for i in range(8):
-        pooled = dot(d, kernels[i * 64 : i * 64 + 64, :])
-        for k in range(16):
-            rows[:, i * 16 + k, :] = pooled[:, k * 128 : k * 128 + 128]
-    at = idx[2] * 64
-    keep[...] = rows[:, pl.ds(pl.multiple_of(at, 64), 64), :].astype(bf16)
-    send[...] = rows[:, pl.ds(pl.multiple_of(64 - at, 64), 64), :].astype(bf16)
+        io.need_part(1, i)
+        pooled = dot(d, kernels[i * 64 : i * 64 + 64, :]).astype(bf16)
+        lanes = slice((i % 4) * 2048, (i % 4) * 2048 + 2048)
+        mine = idx[2] == i // 4
+
+        @pl.when(mine)
+        def _():
+            keep[:, lanes] = pooled
+
+        @pl.when(jnp.logical_not(mine))
+        def _():
+            send[:, lanes] = pooled
 
 
 def skip_add_body(idx, own, other, keep, send):
     first = idx[1] == 0
     total = own[...].astype(f32) + other[...].astype(f32)
-    lo, hi = total[:, :32], total[:, 32:]
+    lo, hi = total[:, :4096], total[:, 4096:]
     keep[...] = jnp.where(first, lo, hi)
     send[...] = jnp.where(first, hi, lo).astype(bf16)
 
 
-def skip_last_body(own, other, out):
-    out[...] = own[...] + other[...].astype(f32)
+def last_join_body(idx, b0, b1, b2, b3, own, other, out, skip):
+    input_join_body(idx, b0, b1, b2, b3, out)
+    for r in range(32):
+        lanes = slice(r * 128, r * 128 + 128)
+        skip[:, r, :] = own[:, lanes] + other[:, lanes].astype(f32)
 
 
 def swap_with(v, axis, k):
@@ -911,29 +972,31 @@
         (idx, *f_blocks),
         "features_turned",
         scratch=[pltpu.VMEM((16, 64, 512), bf16)],
-        deps=(up,),
+        deps=(up, gains),
     )
     if eight:
-        skip_full = lax.all_gather(skip_feature, "chan", axis=1, tiled=True)
+        by_tap = skip_feature.reshape(32, 2, 16, 8, 16).transpose(0, 1, 4, 2, 3)
+        skip_full = lax.all_gather(by_tap.reshape(32, 32, 128), "chan", axis=1, tiled=True)
         flat = squeezer.reshape(16, 64, 16, 8).transpose(1, 2, 3, 0).reshape(64, 2048)
-        squeezer_whole = lax.all_gather(flat, "chan", axis=0, tiled=True)
-        wide_own = after(wide_own, field, skip_full)
-
+        squeezer_whole = lax.all_gather(
+            squeezer.transpose(1, 0, 2).reshape(64, 2048), "chan", axis=0, tiled=True
+        )
         (quarter,) = call(
             skip_quarter_body,
             [((8, 8, 16, 128), bf16)],
             (idx, skip_full),
             "skip_quarter", plain=True,
-            deps=(wide_own,),
-        )
-        quarter = over_batch(quarter)
+        )
+        wide_own = after(wide_own, field, quarter)
+        quarter = over_batch(after(quarter, wide_own))
+
         (fine,) = call(
             pack_fine_body,
             [((8, 64, 128), bf16)],
-            (refiner, exciter),
+            (refiner, exciter, swap_with(exciter, "chan", 2)),
             "pack_fine",
             smem=0, plain=True,
-            deps=(wide_own,),
+            deps=(field,),
         )
         fine_own = lax.all_gather(fine, "batch")
     else:
@@ -949,7 +1012,7 @@
     gap, logit_one, base, msg_one, wide_w = call(
         conv_one_body,
         [
-            ((8, 2, 8, 2, 16, 128), bf16),
+            ((8, 2, 8, 2, 16, 128), bf16, 2),
             ((8, 2, 8, 2, 16, 128), bf16),
             ((16, 128), f32),
             ((16, 128), f32),
@@ -960,8 +1023,8 @@
         scratch=[pltpu.VMEM((2, 2, 8, 8, 16, 128), f32)],
         late=(2, 3),
     )
-    flat_field = (16, 16, 16, 128)
-    gap_other = swap_with(gap, "chan", 2).reshape(flat_field)
+    gap_other = tuple(swap_with(v, "chan", 2).reshape(8, 16, 16, 128) for v in gap)
+    gap_flat = tuple(v.reshape(8, 16, 16, 128) for v in gap)
 
     if eight:
         skips, payload = call(
@@ -971,36 +1034,30 @@
             "squeeze",
             scratch=[pltpu.VMEM((1024, 128), f32)],
             smem=0,
-            plain=True,
         )
         shared_one = exchange(payload)
     else:
         shared_one = share(msg_one)
-    shared_one = after(shared_one, gap_other)
-    if eight:
-        (part,) = call(
-            part_sum_body, [((8, 256), f32)], (idx, shared_one), "part_sum", plain=True
-        )
+    shared_one = after(shared_one, *gap_other)
     line, stat_one = call(
         make_scale_body(entries),
-        [((2, 16, 128), f32), ((2, 16, 128), f32)],
-        (mask, gains, base, shared_one),
-        "scale", plain=True,
-        smem=0,
+        [((3, 16, 128), f32), ((2, 16, 128), f32)],
+        (idx, mask, gains, base, shared_one),
+        "scale",
+        plain=True,
     )
     fine_own = after(fine_own, shared_one)
     fine_other = swap_with(fine_own, "chan", 1)
-    fine_w, exciter_own = call(
+    fine_w, exciter_own, exciter_other = call(
         refiner_body,
-        [((9, 256, 256), bf16), ((128, 256), bf16)],
+        [((9, 256, 256), bf16), ((128, 256), bf16), ((128, 256), bf16)],
         (idx, fine_own, fine_other),
         "refiner_taps", plain=True,
     )
+    line_other = swap_with(line, "chan", 2)
     if eight:
-        line_other, part_other = swap_with(line, "chan", 2), swap_with(part, "chan", 2)
-        squeezed = (part, swap_with(part, "chan", 1), part_other, swap_with(part_other, "chan", 1))
-    else:
-        line_other = swap_with(line, "chan", 2)
+        squeezed = (line, swap_with(line, "chan", 1), line_other, swap_with(line_other, "chan", 1))
+        skips_all = lax.all_gather(after(skips, line_other), "chan", axis=0, tiled=True)
 
     held, glu_two, logit_two, sums_two = call(
         conv_two_body,
@@ -1010,18 +1067,18 @@
             ((16, 16, 16, 128), bf16),
             ((4, 16, 128), f32),
         ],
-        (gap.reshape(flat_field), gap_other, line, line_other, fine_w, up),
+        (idx, gap_flat, gap_other, line, line_other, fine_w, up),
         "conv_two",
-        smem=0,
         late=(4, 5),
     )
     if eight:
-        pull, squeezed = call(
-            gate_body,
-            [((2, 16, 128), f32), ((32, 256), f32)],
-            (idx, *squeezed, exciter_own, weight),
-            "gate", plain=True,
-        )
+        pull, squeezed, payload_two = call(
+            gate_message_body,
+            [((2, 16, 128), f32), ((32, 256), f32), ((16, 24, 128), f32)],
+            (idx, *squeezed, exciter_own, weight, mask, sums_two),
+            "gate",
+        )
+        shared_two = exchange(payload_two)
     else:
         skip_full = lax.all_gather(skip_feature, "chan", axis=1, tiled=True)
         squeezer_full = lax.all_gather(squeezer, "batch", axis=2, tiled=True)
@@ -1035,10 +1092,10 @@
         gate = jax.nn.sigmoid(excited)
         gate_mine = natural(half(gate, core), swap_with(half(gate, 1 - core), "chan", 1), 1)
         pull = jnp.stack([weight, gate_mine], axis=0)
-    (msg_two,) = call(
-        message_two_body, [((24, 128), f32)], (mask, pull, sums_two), "message_two", plain=True, smem=0
-    )
-    shared_two = share(msg_two)
+        (msg_two,) = call(
+            message_two_body, [((1, 24, 128), f32)], (mask, pull, sums_two), "message", smem=0
+        )
+        shared_two = share(msg_two[0])
     if eight:
         flats = lax.all_gather(after(flat, shared_two), "batch", axis=0, tiled=True)
     grad_two, dh_own, dh_send, small, stat_two, mine = call(
@@ -1052,6 +1109,7 @@
             ((3, 16, 128), f32),
         ],
         (
+            idx,
             glu_two,
             logit_two,
             up,
@@ -1060,20 +1118,25 @@
             gains,
             sums_two,
             fine_w,
-            gap.reshape(flat_field),
+            gap_flat,
             gap_other,
             shared_two,
         ),
         "back_two",
-        smem=0,
+        deps=(skips_all,) if eight else (),
         late=(0, 1, 2, 7, 8, 9),
     )
     theirs = swap_with(small, "chan", 2)
     dh_other = swap_with(after(dh_send, theirs), "chan", 2)
-    (msg_three,) = call(
-        first_sums_body, [((8, 128), f32)], (mine, theirs, mask, stat_one), "first_sums", plain=True, smem=0
-    )
-    shared_three = share(msg_three)
+    (payload_three,) = call(
+        first_sums_body,
+        [((16 if eight else 1, 8, 128), f32)],
+        (mine, theirs, mask, stat_one),
+        "first_sums",
+        smem=0,
+        plain=True,
+    )
+    shared_three = exchange(payload_three) if eight else share(payload_three[0])
     fine_keep, fine_send, out_own, out_send = call(
         refiner_grad_body,
         [
@@ -1091,7 +1154,15 @@
     fine_recv = swap_with(after(fine_send, shared_three), "chan", 1)
 
     def pair(keep, recv, name):
-        return call(pair_sum_body, [(keep.shape, bf16)], (keep, recv), name, smem=0)[0]
+        return call(
+            pair_sum_body,
+            [(keep.shape, bf16)],
+            (keep, recv),
+            name,
+            smem=0,
+            late=(0, 1),
+            cuts={0: 8, 1: 8},
+        )[0]
 
     if eight:
         both = jnp.stack([small[2], theirs[2]], axis=0)
@@ -1104,7 +1175,7 @@
                 swap_with(both, "chan", 1),
                 squeezed,
                 exciter_own,
-                swap_with(exciter_own, "chan", 2),
+                exciter_other,
                 fine_keep,
                 fine_recv,
             ),
@@ -1157,11 +1228,12 @@
     if eight:
         skip_keep, skip_send = call(
             skip_back_body,
-            [((32, 64, 128), bf16), ((32, 64, 128), bf16)],
+            [((32, 8192), bf16), ((32, 8192), bf16)],
             (idx, vectors, flats),
             "skip_back",
-            scratch=[pltpu.VMEM((32, 128, 128), f32)],
             deps=(widener_pair,),
+            late=(1,),
+            cuts={1: 8},
         )
     blocks = call(
         input_back_body,
@@ -1170,57 +1242,43 @@
         "input_back",
         scratch=[pltpu.VMEM((16, 64, 512), bf16)],
         deps=(skip_send,) if eight else (widener_pair,),
-        late=(1,),
-    )
+        late=(0, 1),
+        cuts={0: 2, 1: 4},
+    )
+    if eight:
+        skip_own, skip_other = call(
+            skip_add_body,
+            [((32, 4096), f32), ((32, 4096), bf16)],
+            (idx, skip_keep, swap_with(skip_send, "chan", 2)),
+            "skip_add", plain=True,
+        )
+        blocks = [blocks[0]] + [after(b, skip_other) for b in blocks[1:]]
     got = [blocks[0]] + [swap_with(blocks[k], "chan", k) for k in range(1, 4)]
-    input_grad = natural(
-        got[0].astype(f32) + got[2].astype(f32), got[1].astype(f32) + got[3].astype(f32), 0
-    )
-
     if eight:
-        (refiner_sum,) = call(
-            refiner_sum_body,
-            [(refiner.shape, f32)],
-            (parts,),
-            "refiner_sum",
-            smem=0, plain=True,
-            deps=(widener_pair,),
-        )
-        skips = lax.all_gather(after(skips, dh_other), "chan", axis=0, tiled=True)
-        exciter_sum, squeezer_sum = call(
+        exciter_sum, squeezer_sum, refiner_sum = call(
             squeeze_back_body,
-            [((64, 32), f32), ((64, 2048), f32)],
-            (parts, skips),
+            [((64, 32), f32), ((16, 64, 128), f32), (refiner.shape, f32)],
+            (parts, skips_all),
             "squeeze_back",
             smem=0,
-            plain=True,
             deps=(widener_pair,),
-        )
-        squeezer_sum = (
-            squeezer_sum.reshape(64, 16, 8, 16).transpose(3, 0, 1, 2).reshape(16, 64, 128)
-        )
-        skip_own, skip_other = call(
-            skip_add_body,
-            [((32, 32, 128), f32), ((32, 32, 128), bf16)],
-            (idx, skip_keep, swap_with(skip_send, "chan", 2)),
-            "skip_add", plain=True,
-        )
-        (skip_grad,) = call(
-            skip_last_body,
-            [((32, 32, 128), f32)],
-            (skip_own, swap_with(skip_other, "chan", 1)),
-            "skip_last", plain=True,
-            smem=0,
         )
         (widener_sum,) = call(
             widener_sum_body,
             [(widener.shape, f32)],
             (widener_parts,),
             "widener_sum",
-            smem=0, plain=True,
-            deps=(input_grad, skip_grad, output, squeezer_sum, refiner_sum),
+            smem=0,
+        )
+        input_grad, skip_grad = call(
+            last_join_body,
+            [(features.shape, f32), (skip_feature.shape, f32)],
+            (idx, *got, skip_own, swap_with(skip_other, "chan", 1)),
+            "last_join",
+            deps=(widener_sum, squeezer_sum, output),
         )
     else:
+        (input_grad,) = call(input_join_body, [(features.shape, f32)], (idx, *got), "input_join")
         lo, hi = small[2, :, :64], small[2, :, 64:]
         keep, send = jnp.where(core == 0, lo, hi), jnp.where(core == 0, hi, lo)
         grad_gate = natural(keep, swap_with(send, "chan", 1), 0)

time: 267 us -> 264 us (0.989)
  blocking collectives: 29.7 us -> 19.9 us
  waiting for transfers between devices: 36.6 us -> 28.2 us
  starting transfers between devices: 39.9 us -> 47.8 us
  Pallas kernels: 107 us -> 112 us
  local copies, waits for them, and re-layouts: 32.6 us -> 36.6 us
    all_to_all x4, waiting for transfers between devices: 11.9 us -> 0.01 us  [over_batch(): return lax.all_to_all(v, 'batch', 0, 0, tiled=True)]
    all_to_all x2 -> x1, blocking collectives: 29.7 us -> 19.9 us  [exchange(): lax.all_to_all(copies, ('batch', 'chan'), 0, 0, tiled=True, axis_index_gr...]
    all_to_all x1 -> x2, waiting for transfers between devices: 0.01 us -> 7.61 us  [exchange(): lax.all_to_all(copies, ('batch', 'chan'), 0, 0, tiled=True, axis_index_gr...]
    all_to_all x1 -> x2, starting transfers between devices: 3.5 us -> 9.28 us  [exchange(): lax.all_to_all(copies, ('batch', 'chan'), 0, 0, tiled=True, axis_index_gr...]
    pallas_call x26 -> x23, Pallas kernels: 107 us -> 112 us  [call(): pl.pallas_call(kernel, out_shape=results, in_specs=[pl.BlockSpec(memory_s...]
    unnamed x132 -> x129, local copies, waits for them, and re-layouts: 24.1 us -> 27.9 us
  transfers between devices with their start and end apart: 34 -> 35, of which waited for: 13 -> 9; matrix products, arithmetic and copies ran while one was open for 6% -> 5% of each run, Pallas kernels for 39% -> 41%
where the time goes in v3:
time: 264 us; the launch traced here: 263 us
  Pallas kernels  112 us (42%)
  starting transfers between devices  47.8 us (18%)
  local copies, waits for them, and re-layouts  36.6 us (14%)
  waiting for transfers between devices  28.2 us (11%)
  blocking collectives  19.9 us (8%)
  between operations  14.6 us (6%)
  other arithmetic  3.14 us (1%)
    pallas_call x23, Pallas kernels, call(): pl.pallas_call(kernel, out_shape=results, in_specs=[pl.BlockSpec(memory_s...  112 us
    unnamed x129, local copies, waits for them, and re-layouts  27.9 us
    all_to_all x4, starting transfers between devices, over_batch(): return lax.all_to_all(v, 'batch', 0, 0, tiled=True)  25 us
    ppermute x24, waiting for transfers between devices, swap_with(): lax.ppermute(v, axis, [(n, n ^ k) for n in range(lax.axis_size(axis))])  20.4 us
    all_to_all x1, blocking collectives, exchange(): lax.all_to_all(copies, ('batch', 'chan'), 0, 0, tiled=True, axis_index_gr...  19.9 us
    ppermute x24, starting transfers between devices, swap_with(): lax.ppermute(v, axis, [(n, n ^ k) for n in range(lax.axis_size(axis))])  13.3 us
    all_to_all x2, starting transfers between devices, exchange(): lax.all_to_all(copies, ('batch', 'chan'), 0, 0, tiled=True, axis_index_gr...  9.28 us
    all_to_all x2, waiting for transfers between devices, exchange(): lax.all_to_all(copies, ('batch', 'chan'), 0, 0, tiled=True, axis_index_gr...  7.61 us
  transfers between devices with their start and end apart: 35, of which 9 were waited for; matrix products, arithmetic and copies ran while one was open for 5% of the time, Pallas kernels for 41%

profile of v3, /device:TPU:0, one launch (start us, length us, event | category | flops | bytes accessed | tf_op | source)
XLA Modules:
  0.0 262.7 jit_solution(12038095985027926722)
XLA Ops:
  11.5 7.4 %all-to-all-start = ((bf16[8,9,64,128]{3,2,1,0:T(8,128)(2,1)}), bf16[8,9,64,128]{3,2,1,0:T(8,128)(2,1)S(1)}, u32[]{:S(2)}, u32[]{:S(2)}) async-start(bf16[8,9,64,128]{3,2,1,0:T(8,128)(2,1)} %pack_wide.1), calls=%async_computation | async-start | bytes 2359296 | tf_op jit(solution)/shard_map/all_to_all | solution.py:922
  28.6 5.3 %upstream_turned.1.refs_5_.refs_8_.refs_3_ = bf16[16,16,16,128]{3,2,1,0:T(8,128)(2,1)} custom-call(s32[4]{0:T(128)} %pad_add_fusion.refs_0_, bf16[16,64,256]{2,1,0:T(8,128)(2,1)} %get-tuple-element.131.refs_1_, bf16[16,64,256]{2,1,0:T(8,128)(2,1)} %copy-done.40), custom_call_target="tpu_custom_call" | custom-call | tf_op jit(solution)/shard_map/upstream_turned/pallas_call | solution.py:131
  34.0 5.8 %collective-permute-done.1.refs_3_ = bf16[16,64,128]{2,1,0:T(8,128)(2,1)} collective-permute-done((bf16[16,64,128]{2,1,0:T(8,128)(2,1)S(1)}, bf16[16,64,128]{2,1,0:T(8,128)(2,1)}, u32[]{:S(2)}, u32[]{:S(2)}) %collective-permute-start.1) | collective-permute-done | bytes 262176 | tf_op jit(solution)/shard_map/ppermute | solution.py:884
  40.5 5.4 %features_turned.1.refs_1_.refs_3_.refs_11_ = bf16[10,10,16,512]{3,2,1,0:T(8,128)(2,1)} custom-call(s32[4]{0:T(128)} %pad_add_fusion.refs_0_, bf16[16,64,128]{2,1,0:T(8,128)(2,1)} %copy-done.35, bf16[16,64,128]{2,1,0:T(8,128)(2,1)} %copy-done.41, bf16[16,64,128]{2,1,0:T(8,128)(2,1)} %collective-permute-done.1.refs_3_, bf16[16,64,128]{2,1,0:T(8,128)(2,1)} %copy-done.42, ...), custom_call_target="tpu_custom_call" | custom-call | tf_op jit(solution)/shard_map/features_turned/pallas_call | solution.py:131
  51.8 5.7 %all-to-all-start.1 = ((bf16[8,8,16,128]{3,2,1,0:T(8,128)(2,1)}), bf16[8,8,16,128]{3,2,1,0:T(8,128)(2,1)S(1)}, u32[]{:S(2)}, u32[]{:S(2)}) async-start(bf16[8,8,16,128]{3,2,1,0:T(8,128)(2,1)} %after.13), calls=%async_computation.1 | async-start | bytes 524288 | tf_op jit(solution)/shard_map/all_to_all | solution.py:922
  58.8 9.6 %conv_one.1 = (bf16[4,2,8,2,16,128]{5,4,3,2,1,0:T(8,128)(2,1)}, bf16[4,2,8,2,16,128]{5,4,3,2,1,0:T(8,128)(2,1)}, bf16[8,2,8,2,16,128]{5,4,3,2,1,0:T(8,128)(2,1)}...) custom-call(s32[4]{0:T(128)} %pad_add_fusion.refs_0_, ...), custom_call_target="tpu_custom_call" | custom-call | tf_op jit(solution)/shard_map/conv_one/pallas_call | solution.py:131
  71.2 2.7 %squeeze.5 = (bf16[64,2048]{1,0:T(8,128)(2,1)}, f32[16,32,128]{2,1,0:T(8,128)}) custom-call(bf16[8,8,16,128]{3,2,1,0:T(8,128)(2,1)} %copy-done.37, bf16[256,2048]{1,0:T(8,128)(2,1)} %all-gather.9.cloned.1.call-done.refs_1_, f32[16,128]{1,0:T(8,128)} %get-tuple-element.60.refs_2_), custom_call_target="tpu_custom_call" | custom-call | tf_op jit(solution)/shard_map/squeeze/pallas_call | solution.py:131
  73.9 19.9 %all_to_all.35.refs_0_ = f32[16,32,128]{2,1,0:T(8,128)} all-to-all(f32[16,32,128]{2,1,0:T(8,128)} %get-tuple-element.61), channel_id=1, replica_groups={{0,1,4,5,8,9,12,13,16,17,20,21,24,25,28,29},{2,3,6,7,10,11,14,15,18,19,..., dimensions={0} | all-to-all | bytes 524288 | tf_op jit(solution)/shard_map/all_to_all | solution.py:950
  97.7 2.7 %collective-permute-done.8.refs_6_.refs_3_.refs_1_ = f32[3,16,128]{2,1,0:T(8,128)S(1)} collective-permute-done((f32[3,16,128]{2,1,0:T(8,128)S(1)}, f32[3,16,128]{2,1,0:T(8,128)S(1)}, u32[]{:S(2)}, u32[]{:S(2)}) %collective-permute-start.8) | collective-permute-done | bytes 24608 | tf_op jit(solution)/shard_map/ppermute | solution.py:884
  101.8 2.2 collective-permute-done.10.refs_2_
  109.1 9.6 %conv_two.1 = (bf16[18,18,16,256]{3,2,1,0:T(8,128)(2,1)}, f32[16,16,16,128]{3,2,1,0:T(8,128)}, bf16[16,16,16,128]{3,2,1,0:T(8,128)(2,1)}, f32[4,16,128]{2,1,0:T(8,128)}) custom-call(s32[4]{0:T(128)} %pad_add_fusion.refs_0_, bf16[8,16,16,128]{3,2,1,0:T(8,128)(2,1)} %bitcast.33, bf16[8,16,16,128]{3,2,1,0:T(8,128)(2,1)} %bitcast.35, ...), custom_call_target="tpu_custom_call" | custom-call | tf_op jit(solution)/shard_map/conv_two/pallas_call | solution.py:131
  119.4 2.7 %gate.1 = (f32[2,16,128]{2,1,0:T(8,128)}, f32[32,256]{1,0:T(8,128)}, f32[16,24,128]{2,1,0:T(8,128)}) custom-call(s32[4]{0:T(128)} %pad_add_fusion.refs_0_, f32[3,16,128]{2,1,0:T(8,128)} %copy-done.18, f32[3,16,128]{2,1,0:T(8,128)} %copy-done.51, f32[3,16,128]{2,1,0:T(8,128)} %copy-done.47, f32[3,16,128]{2,1,0:T(8,128)} %copy-done.52, ...), custom_call_target="tpu_custom_call" | custom-call | tf_op jit(solution)/shard_map/gate/pallas_call | solution.py:131
  122.2 5.6 %all-to-all-start.3 = ((f32[16,24,128]{2,1,0:T(8,128)}), f32[16,24,128]{2,1,0:T(8,128)S(1)}, u32[]{:S(2)}, u32[]{:S(2)}) async-start(f32[16,24,128]{2,1,0:T(8,128)} %get-tuple-element.69), calls=%async_computation.3 | async-start | bytes 393216 | tf_op jit(solution)/shard_map/all_to_all | solution.py:950
  129.1 7.6 %all-to-all-done.3.refs_13_.refs_1_ = f32[16,24,128]{2,1,0:T(8,128)S(1)} async-done(((f32[16,24,128]{2,1,0:T(8,128)}), f32[16,24,128]{2,1,0:T(8,128)S(1)}, u32[]{:S(2)}, u32[]{:S(2)}) %all-to-all-start.3) | async-done | bytes 196640 | tf_op jit(solution)/shard_map/all_to_all | solution.py:950
  137.5 12.2 %back_two.1 = (bf16[18,18,16,256]{3,2,1,0:T(8,128)(2,1)}, bf16[16,16,16,128]{3,2,1,0:T(8,128)(2,1)}, bf16[16,16,16,128]{3,2,1,0:T(8,128)(2,1)}, f32[3,16,128]{2,...) custom-call(s32[4]{0:T(128)} %pad_add_fusion.refs_0_, f32[16,16,16,128]{3,2,1,0:T(8,128)} %get-tuple-element.64.refs_1_.refs_3_, ...), custom_call_target="tpu_custom_call" | custom-call | tf_op jit(solution)/shard_map/back_two/pallas_call | solution.py:131
  150.2 3.6 %collective-permute-done.14.refs_1_ = f32[3,16,128]{2,1,0:T(8,128)S(1)} collective-permute-done((f32[3,16,128]{2,1,0:T(8,128)}, f32[3,16,128]{2,1,0:T(8,128)S(1)}, u32[]{:S(2)}, u32[]{:S(2)}) %collective-permute-start.14) | collective-permute-done | bytes 24608 | tf_op jit(solution)/shard_map/ppermute | solution.py:884
  156.2 3.7 %all-to-all-start.4 = ((f32[16,8,128]{2,1,0:T(8,128)}), f32[16,8,128]{2,1,0:T(8,128)S(1)}, u32[]{:S(2)}, u32[]{:S(2)}) async-start(f32[16,8,128]{2,1,0:T(8,128)} %first_sums.1), calls=%async_computation.4 | async-start | bytes 131072 | tf_op jit(solution)/shard_map/all_to_all | solution.py:950
  159.9 13.8 %refiner_grad.1 = (bf16[8,5,64,128]{3,2,1,0:T(8,128)(2,1)}, bf16[8,5,64,128]{3,2,1,0:T(8,128)(2,1)}, bf16[16,64,256]{2,1,0:T(8,128)(2,1)}, bf16[16,64,256]{2,1,0:T(8,128)(2,1)}) custom-call(s32[4]{0:T(128)} %pad_add_fusion.refs_0_, bf16[18,18,16,256]{3,2,1,0:T(8,128)(2,1)} %get-tuple-element.71.refs_1_, bf16[18,18,16,256]{3,2,1,0:T(8,128)(2,1)} %get-tuple-element.72.refs_2_, ...), custom_call_target="tpu_custom_call" | custom-call | tf_op jit(solution)/shard_map/refiner_grad/pallas_call | solution.py:131
  177.5 4.0 %excite_back.1 = (bf16[32,128]{1,0:T(8,128)(2,1)}, bf16[8,384,128]{2,1,0:T(8,128)(2,1)}) custom-call(s32[4]{0:T(128)} %pad_add_fusion.refs_0_, f32[2,16,128]{2,1,0:T(8,128)} %copy-done.50, f32[2,16,128]{2,1,0:T(8,128)} %copy-done.53, f32[32,256]{1,0:T(8,128)} %get-tuple-element.82.refs_3_, bf16[128,256]{1,0:T(8,128)(2,1)} %copy-done.12, ...), custom_call_target="tpu_custom_call" | custom-call | tf_op jit(solution)/shard_map/excite_back/pallas_call | solution.py:131
  181.5 5.7 %all-to-all-start.5 = ((bf16[8,384,128]{2,1,0:T(8,128)(2,1)}), bf16[8,384,128]{2,1,0:T(8,128)(2,1)S(1)}, u32[]{:S(2)}, u32[]{:S(2)}) async-start(bf16[8,384,128]{2,1,0:T(8,128)(2,1)} %get-tuple-element.86.refs_12_), calls=%async_computation.5 | async-start | bytes 1572864 | tf_op jit(solution)/shard_map/all_to_all | solution.py:922
  188.2 13.4 %back_one.1 = (bf16[2,2,10,10,16,256]{5,4,3,2,1,0:T(8,128)(2,1)}, f32[8,128]{1,0:T(8,128)}, bf16[8,9,64,128]{3,2,1,0:T(8,128)(2,1)}, bf16[8,9,64,128]{3,2,1,0:T(8,128)(2,1)}) custom-call(s32[4]{0:T(128)} %pad_add_fusion.refs_0_, bf16[4,2,8,2,16,128]{5,4,3,2,1,0:T(8,128)(2,1)} %get-tuple-element.57.refs_1_, ...), custom_call_target="tpu_custom_call" | custom-call | tf_op jit(solution)/shard_map/back_one/pallas_call | solution.py:131
  201.6 3.0 %collective-permute-done.18.refs_1_ = bf16[8,9,64,128]{3,2,1,0:T(8,128)(2,1)S(1)} collective-permute-done((bf16[8,9,64,128]{3,2,1,0:T(8,128)(2,1)}, bf16[8,9,64,128]{3,2,1,0:T(8,128)(2,1)S(1)}, u32[]{:S(2)}, u32[]{:S(2)}) %collective-permute-start.18) | collective-permute-done | bytes 1179680 | tf_op jit(solution)/shard_map/ppermute | solution.py:884
  205.7 2.6 %widener_pair.1.refs_0_ = bf16[8,9,64,128]{3,2,1,0:T(8,128)(2,1)} custom-call(bf16[8,9,64,128]{3,2,1,0:T(8,128)(2,1)} %get-tuple-element.90.refs_0_, bf16[8,9,64,128]{3,2,1,0:T(8,128)(2,1)} %copy-done.31), custom_call_target="tpu_custom_call" | custom-call | tf_op jit(solution)/shard_map/widener_pair/pallas_call | solution.py:131
  209.2 6.1 %all-to-all-start.6 = ((bf16[8,9,64,128]{3,2,1,0:T(8,128)(2,1)}), bf16[8,9,64,128]{3,2,1,0:T(8,128)(2,1)S(1)}, u32[]{:S(2)}, u32[]{:S(2)}) async-start(bf16[8,9,64,128]{3,2,1,0:T(8,128)(2,1)} %after.20.refs_3_.refs_2_), calls=%async_computation.6 | async-start | bytes 2359296 | tf_op jit(solution)/shard_map/all_to_all | solution.py:922
  215.5 4.7 %skip_back.1 = (bf16[32,8192]{1,0:T(8,128)(2,1)}, bf16[32,8192]{1,0:T(8,128)(2,1)}) custom-call(s32[4]{0:T(128)} %pad_add_fusion.refs_0_, bf16[32,128]{1,0:T(8,128)(2,1)} %get-tuple-element.89.refs_1_, bf16[512,2048]{1,0:T(8,128)(2,1)} %all-gather.13.cloned.1.call-done.refs_2_, bf16[8,9,64,128]{3,2,1,0:T(8,128)(2,1)} %after.20.refs_3_.refs_2_), custom_call_target="tpu_custom_call" | custom-call | tf_op jit(solution)/shard_map/skip_back/pallas_call | solution.py:131
  220.2 1.7 collective-permute-start.19
  223.7 11.2 %input_back.1 = (bf16[16,64,128]{2,1,0:T(8,128)(2,1)}, bf16[16,64,128]{2,1,0:T(8,128)(2,1)}, bf16[16,64,128]{2,1,0:T(8,128)(2,1)}, bf16[16,64,128]{2,1,0:T(8,128)(2,1)}) custom-call(s32[4]{0:T(128)} %pad_add_fusion.refs_0_, bf16[2,2,10,10,16,256]{5,4,3,2,1,0:T(8,128)(2,1)} %get-tuple-element.87.refs_1_, bf16[16,256,512]{2,1,0:T(8,128)(2,1)} %get-tuple-element.88.refs_2_, ...), custom_call_target="tpu_custom_call" | custom-call | tf_op jit(solution)/shard_map/input_back/pallas_call | solution.py:131
  239.7 3.0 %squeeze_back.1 = (f32[64,32]{1,0:T(8,128)}, f32[16,64,128]{2,1,0:T(8,128)}, f32[9,2,64,32]{3,2,1,0:T(8,128)}) custom-call(bf16[8,384,128]{2,1,0:T(8,128)(2,1)} %copy-done.25, bf16[256,2048]{1,0:T(8,128)(2,1)} %all-gather.11.cloned.1.call-done.refs_14_.refs_1_, bf16[8,9,64,128]{3,2,1,0:T(8,128)(2,1)} %after.20.refs_3_.refs_2_), custom_call_target="tpu_custom_call" | custom-call | tf_op jit(solution)/shard_map/squeeze_back/pallas_call | solution.py:131
  242.7 2.0 copy.63
  247.2 2.4 widener_sum.1.refs_7_
  249.6 2.0 collective-permute-done.21.refs_3_
  252.5 3.7 %last_join.1 = (f32[32,64,128]{2,1,0:T(8,128)}, f32[32,32,128]{2,1,0:T(8,128)}) custom-call(s32[4]{0:T(128)} %pad_add_fusion.refs_0_, bf16[16,64,128]{2,1,0:T(8,128)(2,1)} %get-tuple-element.93.refs_1_, bf16[16,64,128]{2,1,0:T(8,128)(2,1)} %copy-done.46, bf16[16,64,128]{2,1,0:T(8,128)(2,1)} %copy-done.45, bf16[16,64,128]{2,1,0:T(8,128)(2,1)} %copy-done.44, ...), custom_call_target="tpu_custom_call" | custom-call | tf_op jit(solution)/shard_map/last_join/pallas_call | solution.py:131
  (233 shorter events, 57.1 us)
Async XLA Ops:
  7.2 41.0 %all-gather.7.cloned.1.call-start = ((), (), s32[]{:S(2)}) async-start(), calls=%async_computation.7 | async-start | bytes 1310720 | tf_op jit(solution)/shard_map/all_gather | solution.py:979
  11.5 39.2 %all-to-all-start = ((bf16[8,9,64,128]{3,2,1,0:T(8,128)(2,1)}), bf16[8,9,64,128]{3,2,1,0:T(8,128)(2,1)S(1)}, u32[]{:S(2)}, u32[]{:S(2)}) async-start(bf16[8,9,64,128]{3,2,1,0:T(8,128)(2,1)} %pack_wide.1), calls=%async_computation | async-start | bytes 2359296 | tf_op jit(solution)/shard_map/all_to_all | solution.py:922
  18.9 51.6 %all-gather.9.cloned.1.call-start = ((), (), s32[]{:S(2)}) async-start(), calls=%async_computation.8 | async-start | bytes 1310720 | tf_op jit(solution)/shard_map/all_gather | solution.py:981
  19.7 81.2 %all-gather.15.cloned.1.call-start = ((), (), s32[]{:S(2)}) async-start(), calls=%async_computation.11 | async-start | bytes 1179648 | tf_op jit(solution)/shard_map/all_gather | solution.py:1001
  21.0 6.8 %collective-permute-start.3 = (bf16[16,64,256]{2,1,0:T(8,128)(2,1)}, bf16[16,64,256]{2,1,0:T(8,128)(2,1)S(1)}, u32[]{:S(2)}, u32[]{:S(2)}) collective-permute-start(bf16[16,64,256]{2,1,0:T(8,128)(2,1)} %get-tuple-element.130), channel_id=1, source_target_pairs={{0,1},{1,0},{2,3},{3,2},{4,5},{5,4},{6,7},{7,6},{8,9},{9,8},{10,11... | collective-permute-start | bytes 1572872 | tf_op jit(solution)/shard_map/ppermute | solution.py:884
  22.1 11.9 %collective-permute-start = (bf16[16,64,128]{2,1,0:T(8,128)(2,1)S(1)}, bf16[16,64,128]{2,1,0:T(8,128)(2,1)S(1)}, u32[]{:S(2)}, u32[]{:S(2)}) collective-permute-start(bf16[16,64,128]{2,1,0:T(8,128)(2,1)S(1)} %get-tuple-element.132), channel_id=1, source_target_pairs={{0,1},{1,0},{2,3},{3,2},{4,5},{5,4},{6,7},{7,6},{8,9},{9,8},{10,11... | collective-permute-start | bytes 786440 | tf_op jit(solution)/shard_map/ppermute | solution.py:884
  22.6 17.1 %collective-permute-start.2 = (bf16[16,64,128]{2,1,0:T(8,128)(2,1)S(1)}, bf16[16,64,128]{2,1,0:T(8,128)(2,1)S(1)}, u32[]{:S(2)}, u32[]{:S(2)}) collective-permute-start(bf16[16,64,128]{2,1,0:T(8,128)(2,1)S(1)} %get-tuple-element.132), channel_id=1, source_target_pairs={{0,3},{1,2},{2,1},{3,0},{4,7},{5,6},{6,5},{7,4},{8,11},{9,10},{10,... | collective-permute-start | bytes 786440 | tf_op jit(solution)/shard_map/ppermute | solution.py:884
  23.8 15.9 %collective-permute-start.1 = (bf16[16,64,128]{2,1,0:T(8,128)(2,1)S(1)}, bf16[16,64,128]{2,1,0:T(8,128)(2,1)}, u32[]{:S(2)}, u32[]{:S(2)}) collective-permute-start(bf16[16,64,128]{2,1,0:T(8,128)(2,1)S(1)} %get-tuple-element.133.refs_1_), channel_id=1, source_target_pairs={{0,2},{1,3},{2,0},{3,1},{4,6},{5,7},{6,4},{7,5},{8,10},{9,11},{10,... | collective-permute-start | bytes 786440 | tf_op jit(solution)/shard_map/ppermute | solution.py:884
  25.6 20.3 %collective-permute-start.9 = (bf16[64,32]{1,0:T(8,128)(2,1)S(1)}, bf16[64,32]{1,0:T(8,128)(2,1)S(1)}, u32[]{:S(2)}, u32[]{:S(2)}) collective-permute-start(bf16[64,32]{1,0:T(8,128)(2,1)S(1)} %copy.59.refs_1_), channel_id=1, source_target_pairs={{0,2},{1,3},{2,0},{3,1},{4,6},{5,7},{6,4},{7,5},{8,10},{9,11},{10,... | collective-permute-start | bytes 12296 | tf_op jit(solution)/shard_map/ppermute | solution.py:884
  51.8 5.9 %collective-permute-start.5 = (bf16[8,9,64,128]{3,2,1,0:T(8,128)(2,1)}, bf16[8,9,64,128]{3,2,1,0:T(8,128)(2,1)S(1)}, u32[]{:S(2)}, u32[]{:S(2)}) collective-permute-start(bf16[8,9,64,128]{3,2,1,0:T(8,128)(2,1)} %after.12.refs_1_), channel_id=1, source_target_pairs={{0,1},{1,0},{2,3},{3,2},{4,5},{5,4},{6,7},{7,6},{8,9},{9,8},{10,11... | collective-permute-start | bytes 3538952 | tf_op jit(solution)/shard_map/ppermute | solution.py:884
  51.8 18.7 %all-to-all-start.1 = ((bf16[8,8,16,128]{3,2,1,0:T(8,128)(2,1)}), bf16[8,8,16,128]{3,2,1,0:T(8,128)(2,1)S(1)}, u32[]{:S(2)}, u32[]{:S(2)}) async-start(bf16[8,8,16,128]{3,2,1,0:T(8,128)(2,1)} %after.13), calls=%async_computation.1 | async-start | bytes 524288 | tf_op jit(solution)/shard_map/all_to_all | solution.py:922
  57.6 79.9 %all-gather.11.cloned.1.call-start = ((), (), s32[]{:S(2)}) async-start(), calls=%async_computation.9 | async-start | bytes 1310720 | tf_op jit(solution)/shard_map/all_gather | solution.py:1060
  68.4 25.5 %collective-permute-start.6 = (bf16[4,2,8,2,16,128]{5,4,3,2,1,0:T(8,128)(2,1)}, bf16[4,2,8,2,16,128]{5,4,3,2,1,0:T(8,128)(2,1)S(1)}, u32[]{:S(2)}, u32[]{:S(2)}) collective-permute-start(bf16[4,2,8,2,16,128]{5,4,3,2,1,0:T(8,128)(2,1)} %get-tuple-element.57.refs_1_), channel_id=1, source_target_pairs={{0,2},{1,3},{2,0},{3,1},{4,6},{5,7},{6,4},{7,5},{8,10},{9,11},{10,... | collective-permute-start | bytes 1572872 | tf_op jit(solution)/shard_map/ppermute | solution.py:884
  68.9 25.0 %collective-permute-start.7 = (bf16[4,2,8,2,16,128]{5,4,3,2,1,0:T(8,128)(2,1)}, bf16[4,2,8,2,16,128]{5,4,3,2,1,0:T(8,128)(2,1)S(1)}, u32[]{:S(2)}, u32[]{:S(2)}) collective-permute-start(bf16[4,2,8,2,16,128]{5,4,3,2,1,0:T(8,128)(2,1)} %get-tuple-element.58.refs_2_), channel_id=1, source_target_pairs={{0,2},{1,3},{2,0},{3,1},{4,6},{5,7},{6,4},{7,5},{8,10},{9,11},{10,... | collective-permute-start | bytes 1572872 | tf_op jit(solution)/shard_map/ppermute | solution.py:884
  96.4 3.9 %collective-permute-start.8 = (f32[3,16,128]{2,1,0:T(8,128)S(1)}, f32[3,16,128]{2,1,0:T(8,128)S(1)}, u32[]{:S(2)}, u32[]{:S(2)}) collective-permute-start(f32[3,16,128]{2,1,0:T(8,128)S(1)} %get-tuple-element.62.refs_5_.refs_1_), channel_id=1, source_target_pairs={{0,2},{1,3},{2,0},{3,1},{4,6},{5,7},{6,4},{7,5},{8,10},{9,11},{10,... | collective-permute-start | bytes 73736 | tf_op jit(solution)/shard_map/ppermute | solution.py:884
  101.0 3.0 %collective-permute-start.10 = (bf16[8,8,64,128]{3,2,1,0:T(8,128)(2,1)}, bf16[8,8,64,128]{3,2,1,0:T(8,128)(2,1)S(1)}, u32[]{:S(2)}, u32[]{:S(2)}) collective-permute-start(bf16[8,8,64,128]{3,2,1,0:T(8,128)(2,1)} %after.15.refs_1_), channel_id=1, source_target_pairs={{0,1},{1,0},{2,3},{3,2},{4,5},{5,4},{6,7},{7,6},{8,9},{9,8},{10,11... | collective-permute-start | bytes 3145736 | tf_op jit(solution)/shard_map/ppermute | solution.py:884
  101.1 17.6 %collective-permute-start.11 = (f32[3,16,128]{2,1,0:T(8,128)S(1)}, f32[3,16,128]{2,1,0:T(8,128)S(1)}, u32[]{:S(2)}, u32[]{:S(2)}) collective-permute-start(f32[3,16,128]{2,1,0:T(8,128)S(1)} %get-tuple-element.62.refs_5_.refs_1_), channel_id=1, source_target_pairs={{0,1},{1,0},{2,3},{3,2},{4,5},{5,4},{6,7},{7,6},{8,9},{9,8},{10,11... | collective-permute-start | bytes 73736 | tf_op jit(solution)/shard_map/ppermute | solution.py:884
  101.7 17.0 %collective-permute-start.12 = (f32[3,16,128]{2,1,0:T(8,128)S(1)}, f32[3,16,128]{2,1,0:T(8,128)S(1)}, u32[]{:S(2)}, u32[]{:S(2)}) collective-permute-start(f32[3,16,128]{2,1,0:T(8,128)S(1)} %copy-done.48), channel_id=1, source_target_pairs={{0,1},{1,0},{2,3},{3,2},{4,5},{5,4},{6,7},{7,6},{8,9},{9,8},{10,11... | collective-permute-start | bytes 73736 | tf_op jit(solution)/shard_map/ppermute | solution.py:884
  122.2 14.6 %all-to-all-start.3 = ((f32[16,24,128]{2,1,0:T(8,128)}), f32[16,24,128]{2,1,0:T(8,128)S(1)}, u32[]{:S(2)}, u32[]{:S(2)}) async-start(f32[16,24,128]{2,1,0:T(8,128)} %get-tuple-element.69), calls=%async_computation.3 | async-start | bytes 393216 | tf_op jit(solution)/shard_map/all_to_all | solution.py:950
  127.7 87.7 %all-gather.13.cloned.1.call-start = ((), (), s32[]{:S(2)}) async-start(), calls=%async_computation.10 | async-start | bytes 2359296 | tf_op jit(solution)/shard_map/all_gather | solution.py:1100
  149.7 4.1 %collective-permute-start.14 = (f32[3,16,128]{2,1,0:T(8,128)}, f32[3,16,128]{2,1,0:T(8,128)S(1)}, u32[]{:S(2)}, u32[]{:S(2)}) collective-permute-start(f32[3,16,128]{2,1,0:T(8,128)} %get-tuple-element.79), channel_id=1, source_target_pairs={{0,2},{1,3},{2,0},{3,1},{4,6},{5,7},{6,4},{7,5},{8,10},{9,11},{10,... | collective-permute-start | bytes 73736 | tf_op jit(solution)/shard_map/ppermute | solution.py:884
  154.4 32.8 %collective-permute-start.15 = (bf16[16,16,16,128]{3,2,1,0:T(8,128)(2,1)}, bf16[16,16,16,128]{3,2,1,0:T(8,128)(2,1)S(1)}, u32[]{:S(2)}, u32[]{:S(2)}) collective-permute-start(bf16[16,16,16,128]{3,2,1,0:T(8,128)(2,1)} %after.17), channel_id=1, source_target_pairs={{0,2},{1,3},{2,0},{3,1},{4,6},{5,7},{6,4},{7,5},{8,10},{9,11},{10,... | collective-permute-start | bytes 3145736 | tf_op jit(solution)/shard_map/ppermute | solution.py:884
  156.2 17.6 %all-to-all-start.4 = ((f32[16,8,128]{2,1,0:T(8,128)}), f32[16,8,128]{2,1,0:T(8,128)S(1)}, u32[]{:S(2)}, u32[]{:S(2)}) async-start(f32[16,8,128]{2,1,0:T(8,128)} %first_sums.1), calls=%async_computation.4 | async-start | bytes 131072 | tf_op jit(solution)/shard_map/all_to_all | solution.py:950
  181.5 26.9 %all-to-all-start.5 = ((bf16[8,384,128]{2,1,0:T(8,128)(2,1)}), bf16[8,384,128]{2,1,0:T(8,128)(2,1)S(1)}, u32[]{:S(2)}, u32[]{:S(2)}) async-start(bf16[8,384,128]{2,1,0:T(8,128)(2,1)} %get-tuple-element.86.refs_12_), calls=%async_computation.5 | async-start | bytes 1572864 | tf_op jit(solution)/shard_map/all_to_all | solution.py:922
  201.5 3.1 %collective-permute-start.18 = (bf16[8,9,64,128]{3,2,1,0:T(8,128)(2,1)}, bf16[8,9,64,128]{3,2,1,0:T(8,128)(2,1)S(1)}, u32[]{:S(2)}, u32[]{:S(2)}) collective-permute-start(bf16[8,9,64,128]{3,2,1,0:T(8,128)(2,1)} %get-tuple-element.91), channel_id=1, source_target_pairs={{0,1},{1,0},{2,3},{3,2},{4,5},{5,4},{6,7},{7,6},{8,9},{9,8},{10,11... | collective-permute-start | bytes 3538952 | tf_op jit(solution)/shard_map/ppermute | solution.py:884
  209.2 36.9 %all-to-all-start.6 = ((bf16[8,9,64,128]{3,2,1,0:T(8,128)(2,1)}), bf16[8,9,64,128]{3,2,1,0:T(8,128)(2,1)S(1)}, u32[]{:S(2)}, u32[]{:S(2)}) async-start(bf16[8,9,64,128]{3,2,1,0:T(8,128)(2,1)} %after.20.refs_3_.refs_2_), calls=%async_computation.6 | async-start | bytes 2359296 | tf_op jit(solution)/shard_map/all_to_all | solution.py:922
  215.4 6.5 %collective-permute-start.13 = (bf16[16,64,256]{2,1,0:T(8,128)(2,1)S(1)}, bf16[16,64,256]{2,1,0:T(8,128)(2,1)S(1)}, u32[]{:S(2)}, u32[]{:S(2)}) collective-permute-start(bf16[16,64,256]{2,1,0:T(8,128)(2,1)S(1)} %copy-done.59), channel_id=1, source_target_pairs={{0,1},{1,0},{2,3},{3,2},{4,5},{5,4},{6,7},{7,6},{8,9},{9,8},{10,11... | collective-permute-start | bytes 1572872 | tf_op jit(solution)/shard_map/ppermute | solution.py:884
  220.2 14.7 %collective-permute-start.19 = (bf16[32,8192]{1,0:T(8,128)(2,1)}, bf16[32,8192]{1,0:T(8,128)(2,1)S(1)}, u32[]{:S(2)}, u32[]{:S(2)}) collective-permute-start(bf16[32,8192]{1,0:T(8,128)(2,1)} %get-tuple-element.92.refs_3_), channel_id=1, source_target_pairs={{0,2},{1,3},{2,0},{3,1},{4,6},{5,7},{6,4},{7,5},{8,10},{9,11},{10,... | collective-permute-start | bytes 1572872 | tf_op jit(solution)/shard_map/ppermute | solution.py:884
  236.4 15.1 %collective-permute-start.23 = (bf16[32,4096]{1,0:T(8,128)(2,1)S(1)}, bf16[32,4096]{1,0:T(8,128)(2,1)S(1)}, u32[]{:S(2)}, u32[]{:S(2)}) collective-permute-start(bf16[32,4096]{1,0:T(8,128)(2,1)S(1)} %get-tuple-element.96.refs_1_), channel_id=1, source_target_pairs={{0,1},{1,0},{2,3},{3,2},{4,5},{5,4},{6,7},{7,6},{8,9},{9,8},{10,11... | collective-permute-start | bytes 786440 | tf_op jit(solution)/shard_map/ppermute | solution.py:884
  237.1 12.4 %collective-permute-start.22 = (bf16[16,64,128]{2,1,0:T(8,128)(2,1)}, bf16[16,64,128]{2,1,0:T(8,128)(2,1)S(1)}, u32[]{:S(2)}, u32[]{:S(2)}) collective-permute-start(bf16[16,64,128]{2,1,0:T(8,128)(2,1)} %after.23), channel_id=1, source_target_pairs={{0,3},{1,2},{2,1},{3,0},{4,7},{5,6},{6,5},{7,4},{8,11},{9,10},{10,... | collective-permute-start | bytes 786440 | tf_op jit(solution)/shard_map/ppermute | solution.py:884
  238.0 13.6 %collective-permute-start.21 = (bf16[16,64,128]{2,1,0:T(8,128)(2,1)}, bf16[16,64,128]{2,1,0:T(8,128)(2,1)S(1)}, u32[]{:S(2)}, u32[]{:S(2)}) collective-permute-start(bf16[16,64,128]{2,1,0:T(8,128)(2,1)} %after.22), channel_id=1, source_target_pairs={{0,2},{1,3},{2,0},{3,1},{4,6},{5,7},{6,4},{7,5},{8,10},{9,11},{10,... | collective-permute-start | bytes 786440 | tf_op jit(solution)/shard_map/ppermute | solution.py:884
  239.0 12.6 %collective-permute-start.20 = (bf16[16,64,128]{2,1,0:T(8,128)(2,1)}, bf16[16,64,128]{2,1,0:T(8,128)(2,1)S(1)}, u32[]{:S(2)}, u32[]{:S(2)}) collective-permute-start(bf16[16,64,128]{2,1,0:T(8,128)(2,1)} %after.21), channel_id=1, source_target_pairs={{0,1},{1,0},{2,3},{3,2},{4,5},{5,4},{6,7},{7,6},{8,9},{9,8},{10,11... | collective-permute-start | bytes 786440 | tf_op jit(solution)/shard_map/ppermute | solution.py:884
  (66 other events, 301.6 us)
Sparse Core Ops, SparseCore 0:
  10.4 22.2 all-gather.6
  34.2 16.2 all-gather.8
  52.7 43.6 all-gather.14
  101.1 16.6 all-gather.10
  137.6 46.6 all-gather.12

commit v4 on v3

--- a/solution.py
+++ b/solution.py
@@ -619,9 +619,10 @@
 
 def refiner_sum_body(parts, out):
     total = tree([parts[k, :320].astype(f32) for k in range(8)])
-    for q in range(18):
-        rows = slice((q // 4) * 64, (q // 4) * 64 + 64)
-        out[q // 2, q % 2] = total[rows, (q % 4) * 32 : (q % 4) * 32 + 32]
+    for row in range(5):
+        turned = total[row * 64 : row * 64 + 64].T
+        for q in range(4 * row, min(4 * row + 4, 18)):
+            out[q // 2, q % 2] = turned[(q % 4) * 32 : (q % 4) * 32 + 32]
 
 
 def first_sums_body(mine, theirs, mask, stat, payload):
@@ -842,7 +843,7 @@
     refiner_sum_body(parts, refiner_out)
     vectors = jnp.concatenate([parts[k, 320:352] for k in range(8)], axis=0)
     swish = jnp.concatenate([parts[k, 352:384] for k in range(8)], axis=0)
-    ex_grad[...] = dot(vectors, swish, TN)[64:, :32]
+    ex_grad[...] = dot(swish, vectors, TN)[:32, 64:]
     grad = dot(quarters_first(vectors).astype(bf16), skips[...], TN)
     for t in range(16):
         sq_grad[t] = grad[:64, t * 128 : t * 128 + 128]
@@ -972,7 +973,7 @@
         (idx, *f_blocks),
         "features_turned",
         scratch=[pltpu.VMEM((16, 64, 512), bf16)],
-        deps=(up, gains),
+        deps=(up, gains, mask, weight),
     )
     if eight:
         by_tap = skip_feature.reshape(32, 2, 16, 8, 16).transpose(0, 1, 4, 2, 3)
@@ -1246,23 +1247,26 @@
         cuts={0: 2, 1: 4},
     )
     if eight:
+        skip_recv = swap_with(skip_send, "chan", 2)
         skip_own, skip_other = call(
             skip_add_body,
             [((32, 4096), f32), ((32, 4096), bf16)],
-            (idx, skip_keep, swap_with(skip_send, "chan", 2)),
+            (idx, skip_keep, skip_recv),
             "skip_add", plain=True,
         )
-        blocks = [blocks[0]] + [after(b, skip_other) for b in blocks[1:]]
+        blocks = [blocks[0]] + [after(b, skip_recv) for b in blocks[1:]]
     got = [blocks[0]] + [swap_with(blocks[k], "chan", k) for k in range(1, 4)]
     if eight:
         exciter_sum, squeezer_sum, refiner_sum = call(
             squeeze_back_body,
-            [((64, 32), f32), ((16, 64, 128), f32), (refiner.shape, f32)],
+            [((32, 64), f32), ((16, 64, 128), f32), ((9, 2, 32, 64), f32)],
             (parts, skips_all),
             "squeeze_back",
             smem=0,
             deps=(widener_pair,),
         )
+        exciter_sum = exciter_sum.T
+        refiner_sum = refiner_sum.transpose(0, 1, 3, 2)
         (widener_sum,) = call(
             widener_sum_body,
             [(widener.shape, f32)],

time: 264 us -> 264 us (level)
  waiting for transfers between devices: 28.2 us -> 31.2 us
  local copies, waits for them, and re-layouts: 36.6 us -> 33.9 us
    unnamed x129 -> x127, local copies, waits for them, and re-layouts: 27.9 us -> 24.5 us
  transfers between devices with their start and end apart: 35 -> 35, of which waited for: 9 -> 10; matrix products, arithmetic and copies ran while one was open for 5% -> 4% of each run, Pallas kernels for 41% -> 41%
where the time goes in v4:
time: 264 us; the launch traced here: 262 us
  Pallas kernels  112 us (42%)
  starting transfers between devices  46.9 us (18%)
  local copies, waits for them, and re-layouts  33.9 us (13%)
  waiting for transfers between devices  31.2 us (12%)
  blocking collectives  20.4 us (8%)
  between operations  14.6 us (6%)
  other arithmetic  3.14 us (1%)
    pallas_call x23, Pallas kernels, call(): pl.pallas_call(kernel, out_shape=results, in_specs=[pl.BlockSpec(memory_s...  112 us
    all_to_all x4, starting transfers between devices, over_batch(): return lax.all_to_all(v, 'batch', 0, 0, tiled=True)  24.8 us
    unnamed x127, local copies, waits for them, and re-layouts  24.5 us
    ppermute x24, waiting for transfers between devices, swap_with(): lax.ppermute(v, axis, [(n, n ^ k) for n in range(lax.axis_size(axis))])  21.2 us
    all_to_all x1, blocking collectives, exchange(): lax.all_to_all(copies, ('batch', 'chan'), 0, 0, tiled=True, axis_index_gr...  20.4 us
    ppermute x24, starting transfers between devices, swap_with(): lax.ppermute(v, axis, [(n, n ^ k) for n in range(lax.axis_size(axis))])  13 us
    all_to_all x2, starting transfers between devices, exchange(): lax.all_to_all(copies, ('batch', 'chan'), 0, 0, tiled=True, axis_index_gr...  8.93 us
    all_to_all x2, waiting for transfers between devices, exchange(): lax.all_to_all(copies, ('batch', 'chan'), 0, 0, tiled=True, axis_index_gr...  7.61 us
  transfers between devices with their start and end apart: 35, of which 10 were waited for; matrix products, arithmetic and copies ran while one was open for 4% of the time, Pallas kernels for 41%

profile of v4, /device:TPU:0, one launch (start us, length us, event | category | flops | bytes accessed | tf_op | source)
XLA Modules:
  0.0 262.4 jit_solution(15040284464025714078)
XLA Ops:
  11.5 7.4 %all-to-all-start = ((bf16[8,9,64,128]{3,2,1,0:T(8,128)(2,1)}), bf16[8,9,64,128]{3,2,1,0:T(8,128)(2,1)S(1)}, u32[]{:S(2)}, u32[]{:S(2)}) async-start(bf16[8,9,64,128]{3,2,1,0:T(8,128)(2,1)} %pack_wide.1), calls=%async_computation | async-start | bytes 2359296 | tf_op jit(solution)/shard_map/all_to_all | solution.py:923
  19.8 1.8 constant_dynamic-slice_fusion.2
  29.5 5.3 %upstream_turned.1.refs_5_.refs_8_.refs_3_ = bf16[16,16,16,128]{3,2,1,0:T(8,128)(2,1)} custom-call(s32[4]{0:T(128)} %pad_add_fusion.refs_0_, bf16[16,64,256]{2,1,0:T(8,128)(2,1)} %get-tuple-element.107.refs_1_, bf16[16,64,256]{2,1,0:T(8,128)(2,1)} %copy-done.40), custom_call_target="tpu_custom_call" | custom-call | tf_op jit(solution)/shard_map/upstream_turned/pallas_call | solution.py:131
  34.9 4.9 %collective-permute-done.1.refs_3_ = bf16[16,64,128]{2,1,0:T(8,128)(2,1)S(1)} collective-permute-done((bf16[16,64,128]{2,1,0:T(8,128)(2,1)S(1)}, bf16[16,64,128]{2,1,0:T(8,128)(2,1)S(1)}, u32[]{:S(2)}, u32[]{:S(2)}) %collective-permute-start.1) | collective-permute-done | bytes 262176 | tf_op jit(solution)/shard_map/ppermute | solution.py:885
  41.1 5.4 %features_turned.1.refs_1_.refs_3_.refs_11_ = bf16[10,10,16,512]{3,2,1,0:T(8,128)(2,1)} custom-call(s32[4]{0:T(128)} %pad_add_fusion.refs_0_, bf16[16,64,128]{2,1,0:T(8,128)(2,1)} %copy-done.35, bf16[16,64,128]{2,1,0:T(8,128)(2,1)} %copy-done.41, bf16[16,64,128]{2,1,0:T(8,128)(2,1)} %copy-done.42, bf16[16,64,128]{2,1,0:T(8,128)(2,1)} %collective-permute-done.2.refs_4_, ...), custom_call_target="tpu_custom_call" | custom-call | tf_op jit(solution)/shard_map/features_turned/pallas_call | solution.py:131
  52.4 5.5 %all-to-all-start.1 = ((bf16[8,8,16,128]{3,2,1,0:T(8,128)(2,1)}), bf16[8,8,16,128]{3,2,1,0:T(8,128)(2,1)S(1)}, u32[]{:S(2)}, u32[]{:S(2)}) async-start(bf16[8,8,16,128]{3,2,1,0:T(8,128)(2,1)} %after.13), calls=%async_computation.1 | async-start | bytes 524288 | tf_op jit(solution)/shard_map/all_to_all | solution.py:923
  59.0 9.6 %conv_one.1 = (bf16[4,2,8,2,16,128]{5,4,3,2,1,0:T(8,128)(2,1)}, bf16[4,2,8,2,16,128]{5,4,3,2,1,0:T(8,128)(2,1)}, bf16[8,2,8,2,16,128]{5,4,3,2,1,0:T(8,128)(2,1)}...) custom-call(s32[4]{0:T(128)} %pad_add_fusion.refs_0_, ...), custom_call_target="tpu_custom_call" | custom-call | tf_op jit(solution)/shard_map/conv_one/pallas_call | solution.py:131
  71.5 2.7 %squeeze.5 = (bf16[64,2048]{1,0:T(8,128)(2,1)}, f32[16,32,128]{2,1,0:T(8,128)}) custom-call(bf16[8,8,16,128]{3,2,1,0:T(8,128)(2,1)} %copy-done.37, bf16[256,2048]{1,0:T(8,128)(2,1)} %all-gather.9.cloned.1.call-done.refs_1_, f32[16,128]{1,0:T(8,128)} %get-tuple-element.60.refs_2_), custom_call_target="tpu_custom_call" | custom-call | tf_op jit(solution)/shard_map/squeeze/pallas_call | solution.py:131
  74.2 20.4 %all_to_all.35.refs_0_ = f32[16,32,128]{2,1,0:T(8,128)} all-to-all(f32[16,32,128]{2,1,0:T(8,128)} %get-tuple-element.61), channel_id=1, replica_groups={{0,1,4,5,8,9,12,13,16,17,20,21,24,25,28,29},{2,3,6,7,10,11,14,15,18,19,..., dimensions={0} | all-to-all | bytes 524288 | tf_op jit(solution)/shard_map/all_to_all | solution.py:951
  97.9 3.2 %collective-permute-done.8.refs_6_.refs_3_.refs_1_ = f32[3,16,128]{2,1,0:T(8,128)S(1)} collective-permute-done((f32[3,16,128]{2,1,0:T(8,128)S(1)}, f32[3,16,128]{2,1,0:T(8,128)S(1)}, u32[]{:S(2)}, u32[]{:S(2)}) %collective-permute-start.8) | collective-permute-done | bytes 24608 | tf_op jit(solution)/shard_map/ppermute | solution.py:885
  102.5 2.3 collective-permute-done.10.refs_2_
  109.9 9.6 %conv_two.1 = (bf16[18,18,16,256]{3,2,1,0:T(8,128)(2,1)}, f32[16,16,16,128]{3,2,1,0:T(8,128)}, bf16[16,16,16,128]{3,2,1,0:T(8,128)(2,1)}, f32[4,16,128]{2,1,0:T(8,128)}) custom-call(s32[4]{0:T(128)} %pad_add_fusion.refs_0_, bf16[8,16,16,128]{3,2,1,0:T(8,128)(2,1)} %bitcast.35, bf16[8,16,16,128]{3,2,1,0:T(8,128)(2,1)} %bitcast.37, ...), custom_call_target="tpu_custom_call" | custom-call | tf_op jit(solution)/shard_map/conv_two/pallas_call | solution.py:131
  120.1 2.7 %gate.1 = (f32[2,16,128]{2,1,0:T(8,128)}, f32[32,256]{1,0:T(8,128)}, f32[16,24,128]{2,1,0:T(8,128)}) custom-call(s32[4]{0:T(128)} %pad_add_fusion.refs_0_, f32[3,16,128]{2,1,0:T(8,128)} %copy-done.18, f32[3,16,128]{2,1,0:T(8,128)} %copy-done.51, f32[3,16,128]{2,1,0:T(8,128)} %copy-done.47, f32[3,16,128]{2,1,0:T(8,128)} %copy-done.52, ...), custom_call_target="tpu_custom_call" | custom-call | tf_op jit(solution)/shard_map/gate/pallas_call | solution.py:131
  122.8 5.2 %all-to-all-start.3 = ((f32[16,24,128]{2,1,0:T(8,128)}), f32[16,24,128]{2,1,0:T(8,128)S(1)}, u32[]{:S(2)}, u32[]{:S(2)}) async-start(f32[16,24,128]{2,1,0:T(8,128)} %get-tuple-element.69), calls=%async_computation.3 | async-start | bytes 393216 | tf_op jit(solution)/shard_map/all_to_all | solution.py:951
  129.4 7.6 %all-to-all-done.3.refs_13_.refs_1_ = f32[16,24,128]{2,1,0:T(8,128)S(1)} async-done(((f32[16,24,128]{2,1,0:T(8,128)}), f32[16,24,128]{2,1,0:T(8,128)S(1)}, u32[]{:S(2)}, u32[]{:S(2)}) %all-to-all-start.3) | async-done | bytes 196640 | tf_op jit(solution)/shard_map/all_to_all | solution.py:951
  137.8 12.2 %back_two.1 = (bf16[18,18,16,256]{3,2,1,0:T(8,128)(2,1)}, bf16[16,16,16,128]{3,2,1,0:T(8,128)(2,1)}, bf16[16,16,16,128]{3,2,1,0:T(8,128)(2,1)}, f32[3,16,128]{2,...) custom-call(s32[4]{0:T(128)} %pad_add_fusion.refs_0_, f32[16,16,16,128]{3,2,1,0:T(8,128)} %get-tuple-element.64.refs_1_.refs_3_, ...), custom_call_target="tpu_custom_call" | custom-call | tf_op jit(solution)/shard_map/back_two/pallas_call | solution.py:131
  150.6 3.5 %collective-permute-done.14.refs_1_ = f32[3,16,128]{2,1,0:T(8,128)S(1)} collective-permute-done((f32[3,16,128]{2,1,0:T(8,128)}, f32[3,16,128]{2,1,0:T(8,128)S(1)}, u32[]{:S(2)}, u32[]{:S(2)}) %collective-permute-start.14) | collective-permute-done | bytes 24608 | tf_op jit(solution)/shard_map/ppermute | solution.py:885
  156.6 3.7 %all-to-all-start.4 = ((f32[16,8,128]{2,1,0:T(8,128)}), f32[16,8,128]{2,1,0:T(8,128)S(1)}, u32[]{:S(2)}, u32[]{:S(2)}) async-start(f32[16,8,128]{2,1,0:T(8,128)} %first_sums.1), calls=%async_computation.4 | async-start | bytes 131072 | tf_op jit(solution)/shard_map/all_to_all | solution.py:951
  160.3 13.8 %refiner_grad.1 = (bf16[8,5,64,128]{3,2,1,0:T(8,128)(2,1)}, bf16[8,5,64,128]{3,2,1,0:T(8,128)(2,1)}, bf16[16,64,256]{2,1,0:T(8,128)(2,1)}, bf16[16,64,256]{2,1,0:T(8,128)(2,1)}) custom-call(s32[4]{0:T(128)} %pad_add_fusion.refs_0_, bf16[18,18,16,256]{3,2,1,0:T(8,128)(2,1)} %get-tuple-element.71.refs_1_, bf16[18,18,16,256]{3,2,1,0:T(8,128)(2,1)} %get-tuple-element.72.refs_2_, ...), custom_call_target="tpu_custom_call" | custom-call | tf_op jit(solution)/shard_map/refiner_grad/pallas_call | solution.py:131
  177.9 4.0 %excite_back.1 = (bf16[32,128]{1,0:T(8,128)(2,1)}, bf16[8,384,128]{2,1,0:T(8,128)(2,1)}) custom-call(s32[4]{0:T(128)} %pad_add_fusion.refs_0_, f32[2,16,128]{2,1,0:T(8,128)} %copy-done.50, f32[2,16,128]{2,1,0:T(8,128)} %copy-done.53, f32[32,256]{1,0:T(8,128)} %get-tuple-element.82.refs_3_, bf16[128,256]{1,0:T(8,128)(2,1)} %copy-done.12, ...), custom_call_target="tpu_custom_call" | custom-call | tf_op jit(solution)/shard_map/excite_back/pallas_call | solution.py:131
  181.8 5.8 %all-to-all-start.5 = ((bf16[8,384,128]{2,1,0:T(8,128)(2,1)}), bf16[8,384,128]{2,1,0:T(8,128)(2,1)S(1)}, u32[]{:S(2)}, u32[]{:S(2)}) async-start(bf16[8,384,128]{2,1,0:T(8,128)(2,1)} %get-tuple-element.86.refs_12_), calls=%async_computation.5 | async-start | bytes 1572864 | tf_op jit(solution)/shard_map/all_to_all | solution.py:923
  188.6 13.4 %back_one.1 = (bf16[2,2,10,10,16,256]{5,4,3,2,1,0:T(8,128)(2,1)}, f32[8,128]{1,0:T(8,128)}, bf16[8,9,64,128]{3,2,1,0:T(8,128)(2,1)}, bf16[8,9,64,128]{3,2,1,0:T(8,128)(2,1)}) custom-call(s32[4]{0:T(128)} %pad_add_fusion.refs_0_, bf16[4,2,8,2,16,128]{5,4,3,2,1,0:T(8,128)(2,1)} %get-tuple-element.57.refs_1_, ...), custom_call_target="tpu_custom_call" | custom-call | tf_op jit(solution)/shard_map/back_one/pallas_call | solution.py:131
  202.0 3.0 %collective-permute-done.18.refs_1_ = bf16[8,9,64,128]{3,2,1,0:T(8,128)(2,1)S(1)} collective-permute-done((bf16[8,9,64,128]{3,2,1,0:T(8,128)(2,1)}, bf16[8,9,64,128]{3,2,1,0:T(8,128)(2,1)S(1)}, u32[]{:S(2)}, u32[]{:S(2)}) %collective-permute-start.18) | collective-permute-done | bytes 1179680 | tf_op jit(solution)/shard_map/ppermute | solution.py:885
  206.1 2.6 %widener_pair.1.refs_0_ = bf16[8,9,64,128]{3,2,1,0:T(8,128)(2,1)} custom-call(bf16[8,9,64,128]{3,2,1,0:T(8,128)(2,1)} %get-tuple-element.90.refs_0_, bf16[8,9,64,128]{3,2,1,0:T(8,128)(2,1)} %copy-done.31), custom_call_target="tpu_custom_call" | custom-call | tf_op jit(solution)/shard_map/widener_pair/pallas_call | solution.py:131
  209.6 6.1 %all-to-all-start.6 = ((bf16[8,9,64,128]{3,2,1,0:T(8,128)(2,1)}), bf16[8,9,64,128]{3,2,1,0:T(8,128)(2,1)S(1)}, u32[]{:S(2)}, u32[]{:S(2)}) async-start(bf16[8,9,64,128]{3,2,1,0:T(8,128)(2,1)} %after.20.refs_3_.refs_2_), calls=%async_computation.6 | async-start | bytes 2359296 | tf_op jit(solution)/shard_map/all_to_all | solution.py:923
  215.9 4.7 %skip_back.1 = (bf16[32,8192]{1,0:T(8,128)(2,1)}, bf16[32,8192]{1,0:T(8,128)(2,1)}) custom-call(s32[4]{0:T(128)} %pad_add_fusion.refs_0_, bf16[32,128]{1,0:T(8,128)(2,1)} %get-tuple-element.89.refs_1_, bf16[512,2048]{1,0:T(8,128)(2,1)} %all-gather.13.cloned.1.call-done.refs_2_, bf16[8,9,64,128]{3,2,1,0:T(8,128)(2,1)} %after.20.refs_3_.refs_2_), custom_call_target="tpu_custom_call" | custom-call | tf_op jit(solution)/shard_map/skip_back/pallas_call | solution.py:131
  224.0 11.2 %input_back.1 = (bf16[16,64,128]{2,1,0:T(8,128)(2,1)}, bf16[16,64,128]{2,1,0:T(8,128)(2,1)}, bf16[16,64,128]{2,1,0:T(8,128)(2,1)}, bf16[16,64,128]{2,1,0:T(8,128)(2,1)}) custom-call(s32[4]{0:T(128)} %pad_add_fusion.refs_0_, bf16[2,2,10,10,16,256]{5,4,3,2,1,0:T(8,128)(2,1)} %get-tuple-element.87.refs_1_, bf16[16,256,512]{2,1,0:T(8,128)(2,1)} %get-tuple-element.88.refs_2_, ...), custom_call_target="tpu_custom_call" | custom-call | tf_op jit(solution)/shard_map/input_back/pallas_call | solution.py:131
  239.5 2.9 %squeeze_back.1 = (f32[32,64]{1,0:T(8,128)}, f32[16,64,128]{2,1,0:T(8,128)}, f32[9,2,32,64]{3,2,1,0:T(8,128)}) custom-call(bf16[8,384,128]{2,1,0:T(8,128)(2,1)} %copy-done.25, bf16[256,2048]{1,0:T(8,128)(2,1)} %all-gather.11.cloned.1.call-done.refs_14_.refs_1_, bf16[8,9,64,128]{3,2,1,0:T(8,128)(2,1)} %after.20.refs_3_.refs_2_), custom_call_target="tpu_custom_call" | custom-call | tf_op jit(solution)/shard_map/squeeze_back/pallas_call | solution.py:131
  242.5 2.2 all-to-all-done.6.refs_0_
  245.7 2.4 widener_sum.1.refs_7_
  248.1 3.3 %collective-permute-done.21.refs_3_ = bf16[16,64,128]{2,1,0:T(8,128)(2,1)S(1)} collective-permute-done((bf16[16,64,128]{2,1,0:T(8,128)(2,1)}, bf16[16,64,128]{2,1,0:T(8,128)(2,1)S(1)}, u32[]{:S(2)}, u32[]{:S(2)}) %collective-permute-start.21) | collective-permute-done | bytes 262176 | tf_op jit(solution)/shard_map/ppermute | solution.py:885
  252.2 3.7 %last_join.1 = (f32[32,64,128]{2,1,0:T(8,128)}, f32[32,32,128]{2,1,0:T(8,128)}) custom-call(s32[4]{0:T(128)} %pad_add_fusion.refs_0_, bf16[16,64,128]{2,1,0:T(8,128)(2,1)} %get-tuple-element.93.refs_1_, bf16[16,64,128]{2,1,0:T(8,128)(2,1)} %copy-done.46, bf16[16,64,128]{2,1,0:T(8,128)(2,1)} %copy-done.45, bf16[16,64,128]{2,1,0:T(8,128)(2,1)} %copy-done.44, ...), custom_call_target="tpu_custom_call" | custom-call | tf_op jit(solution)/shard_map/last_join/pallas_call | solution.py:131
  (231 shorter events, 55.8 us)
Async XLA Ops:
  7.2 41.6 %all-gather.7.cloned.1.call-start = ((), (), s32[]{:S(2)}) async-start(), calls=%async_computation.7 | async-start | bytes 1310720 | tf_op jit(solution)/shard_map/all_gather | solution.py:980
  11.5 39.8 %all-to-all-start = ((bf16[8,9,64,128]{3,2,1,0:T(8,128)(2,1)}), bf16[8,9,64,128]{3,2,1,0:T(8,128)(2,1)S(1)}, u32[]{:S(2)}, u32[]{:S(2)}) async-start(bf16[8,9,64,128]{3,2,1,0:T(8,128)(2,1)} %pack_wide.1), calls=%async_computation | async-start | bytes 2359296 | tf_op jit(solution)/shard_map/all_to_all | solution.py:923
  18.9 51.8 %all-gather.9.cloned.1.call-start = ((), (), s32[]{:S(2)}) async-start(), calls=%async_computation.8 | async-start | bytes 1310720 | tf_op jit(solution)/shard_map/all_gather | solution.py:982
  19.7 82.0 %all-gather.15.cloned.1.call-start = ((), (), s32[]{:S(2)}) async-start(), calls=%async_computation.11 | async-start | bytes 1179648 | tf_op jit(solution)/shard_map/all_gather | solution.py:1002
  21.7 13.2 %collective-permute-start = (bf16[16,64,128]{2,1,0:T(8,128)(2,1)}, bf16[16,64,128]{2,1,0:T(8,128)(2,1)S(1)}, u32[]{:S(2)}, u32[]{:S(2)}) collective-permute-start(bf16[16,64,128]{2,1,0:T(8,128)(2,1)} %get-tuple-element.108), channel_id=1, source_target_pairs={{0,1},{1,0},{2,3},{3,2},{4,5},{5,4},{6,7},{7,6},{8,9},{9,8},{10,11... | collective-permute-start | bytes 786440 | tf_op jit(solution)/shard_map/ppermute | solution.py:885
  21.8 18.0 %collective-permute-start.2 = (bf16[16,64,128]{2,1,0:T(8,128)(2,1)}, bf16[16,64,128]{2,1,0:T(8,128)(2,1)}, u32[]{:S(2)}, u32[]{:S(2)}) collective-permute-start(bf16[16,64,128]{2,1,0:T(8,128)(2,1)} %get-tuple-element.108), channel_id=1, source_target_pairs={{0,3},{1,2},{2,1},{3,0},{4,7},{5,6},{6,5},{7,4},{8,11},{9,10},{10,... | collective-permute-start | bytes 786440 | tf_op jit(solution)/shard_map/ppermute | solution.py:885
  24.4 4.3 %collective-permute-start.3 = (bf16[16,64,256]{2,1,0:T(8,128)(2,1)}, bf16[16,64,256]{2,1,0:T(8,128)(2,1)S(1)}, u32[]{:S(2)}, u32[]{:S(2)}) collective-permute-start(bf16[16,64,256]{2,1,0:T(8,128)(2,1)} %get-tuple-element.106), channel_id=1, source_target_pairs={{0,1},{1,0},{2,3},{3,2},{4,5},{5,4},{6,7},{7,6},{8,9},{9,8},{10,11... | collective-permute-start | bytes 1572872 | tf_op jit(solution)/shard_map/ppermute | solution.py:885
  24.5 15.2 %collective-permute-start.1 = (bf16[16,64,128]{2,1,0:T(8,128)(2,1)S(1)}, bf16[16,64,128]{2,1,0:T(8,128)(2,1)S(1)}, u32[]{:S(2)}, u32[]{:S(2)}) collective-permute-start(bf16[16,64,128]{2,1,0:T(8,128)(2,1)S(1)} %get-tuple-element.109.refs_1_), channel_id=1, source_target_pairs={{0,2},{1,3},{2,0},{3,1},{4,6},{5,7},{6,4},{7,5},{8,10},{9,11},{10,... | collective-permute-start | bytes 786440 | tf_op jit(solution)/shard_map/ppermute | solution.py:885
  26.5 20.0 %collective-permute-start.9 = (bf16[64,32]{1,0:T(8,128)(2,1)S(1)}, bf16[64,32]{1,0:T(8,128)(2,1)S(1)}, u32[]{:S(2)}, u32[]{:S(2)}) collective-permute-start(bf16[64,32]{1,0:T(8,128)(2,1)S(1)} %copy.55.refs_1_), channel_id=1, source_target_pairs={{0,2},{1,3},{2,0},{3,1},{4,6},{5,7},{6,4},{7,5},{8,10},{9,11},{10,... | collective-permute-start | bytes 12296 | tf_op jit(solution)/shard_map/ppermute | solution.py:885
  52.4 5.6 %collective-permute-start.5 = (bf16[8,9,64,128]{3,2,1,0:T(8,128)(2,1)}, bf16[8,9,64,128]{3,2,1,0:T(8,128)(2,1)S(1)}, u32[]{:S(2)}, u32[]{:S(2)}) collective-permute-start(bf16[8,9,64,128]{3,2,1,0:T(8,128)(2,1)} %after.12.refs_1_), channel_id=1, source_target_pairs={{0,1},{1,0},{2,3},{3,2},{4,5},{5,4},{6,7},{7,6},{8,9},{9,8},{10,11... | collective-permute-start | bytes 3538952 | tf_op jit(solution)/shard_map/ppermute | solution.py:885
  52.4 18.4 %all-to-all-start.1 = ((bf16[8,8,16,128]{3,2,1,0:T(8,128)(2,1)}), bf16[8,8,16,128]{3,2,1,0:T(8,128)(2,1)S(1)}, u32[]{:S(2)}, u32[]{:S(2)}) async-start(bf16[8,8,16,128]{3,2,1,0:T(8,128)(2,1)} %after.13), calls=%async_computation.1 | async-start | bytes 524288 | tf_op jit(solution)/shard_map/all_to_all | solution.py:923
  57.9 79.8 %all-gather.11.cloned.1.call-start = ((), (), s32[]{:S(2)}) async-start(), calls=%async_computation.9 | async-start | bytes 1310720 | tf_op jit(solution)/shard_map/all_gather | solution.py:1061
  68.7 25.9 %collective-permute-start.6 = (bf16[4,2,8,2,16,128]{5,4,3,2,1,0:T(8,128)(2,1)}, bf16[4,2,8,2,16,128]{5,4,3,2,1,0:T(8,128)(2,1)S(1)}, u32[]{:S(2)}, u32[]{:S(2)}) collective-permute-start(bf16[4,2,8,2,16,128]{5,4,3,2,1,0:T(8,128)(2,1)} %get-tuple-element.57.refs_1_), channel_id=1, source_target_pairs={{0,2},{1,3},{2,0},{3,1},{4,6},{5,7},{6,4},{7,5},{8,10},{9,11},{10,... | collective-permute-start | bytes 1572872 | tf_op jit(solution)/shard_map/ppermute | solution.py:885
  69.2 25.4 %collective-permute-start.7 = (bf16[4,2,8,2,16,128]{5,4,3,2,1,0:T(8,128)(2,1)}, bf16[4,2,8,2,16,128]{5,4,3,2,1,0:T(8,128)(2,1)S(1)}, u32[]{:S(2)}, u32[]{:S(2)}) collective-permute-start(bf16[4,2,8,2,16,128]{5,4,3,2,1,0:T(8,128)(2,1)} %get-tuple-element.58.refs_2_), channel_id=1, source_target_pairs={{0,2},{1,3},{2,0},{3,1},{4,6},{5,7},{6,4},{7,5},{8,10},{9,11},{10,... | collective-permute-start | bytes 1572872 | tf_op jit(solution)/shard_map/ppermute | solution.py:885
  97.2 3.9 %collective-permute-start.8 = (f32[3,16,128]{2,1,0:T(8,128)S(1)}, f32[3,16,128]{2,1,0:T(8,128)S(1)}, u32[]{:S(2)}, u32[]{:S(2)}) collective-permute-start(f32[3,16,128]{2,1,0:T(8,128)S(1)} %get-tuple-element.62.refs_5_.refs_1_), channel_id=1, source_target_pairs={{0,2},{1,3},{2,0},{3,1},{4,6},{5,7},{6,4},{7,5},{8,10},{9,11},{10,... | collective-permute-start | bytes 73736 | tf_op jit(solution)/shard_map/ppermute | solution.py:885
  101.7 3.0 %collective-permute-start.10 = (bf16[8,8,64,128]{3,2,1,0:T(8,128)(2,1)}, bf16[8,8,64,128]{3,2,1,0:T(8,128)(2,1)S(1)}, u32[]{:S(2)}, u32[]{:S(2)}) collective-permute-start(bf16[8,8,64,128]{3,2,1,0:T(8,128)(2,1)} %after.15.refs_1_), channel_id=1, source_target_pairs={{0,1},{1,0},{2,3},{3,2},{4,5},{5,4},{6,7},{7,6},{8,9},{9,8},{10,11... | collective-permute-start | bytes 3145736 | tf_op jit(solution)/shard_map/ppermute | solution.py:885
  101.8 17.6 %collective-permute-start.11 = (f32[3,16,128]{2,1,0:T(8,128)S(1)}, f32[3,16,128]{2,1,0:T(8,128)S(1)}, u32[]{:S(2)}, u32[]{:S(2)}) collective-permute-start(f32[3,16,128]{2,1,0:T(8,128)S(1)} %get-tuple-element.62.refs_5_.refs_1_), channel_id=1, source_target_pairs={{0,1},{1,0},{2,3},{3,2},{4,5},{5,4},{6,7},{7,6},{8,9},{9,8},{10,11... | collective-permute-start | bytes 73736 | tf_op jit(solution)/shard_map/ppermute | solution.py:885
  102.5 17.0 %collective-permute-start.12 = (f32[3,16,128]{2,1,0:T(8,128)S(1)}, f32[3,16,128]{2,1,0:T(8,128)S(1)}, u32[]{:S(2)}, u32[]{:S(2)}) collective-permute-start(f32[3,16,128]{2,1,0:T(8,128)S(1)} %copy-done.48), channel_id=1, source_target_pairs={{0,1},{1,0},{2,3},{3,2},{4,5},{5,4},{6,7},{7,6},{8,9},{9,8},{10,11... | collective-permute-start | bytes 73736 | tf_op jit(solution)/shard_map/ppermute | solution.py:885
  122.8 14.2 %all-to-all-start.3 = ((f32[16,24,128]{2,1,0:T(8,128)}), f32[16,24,128]{2,1,0:T(8,128)S(1)}, u32[]{:S(2)}, u32[]{:S(2)}) async-start(f32[16,24,128]{2,1,0:T(8,128)} %get-tuple-element.69), calls=%async_computation.3 | async-start | bytes 393216 | tf_op jit(solution)/shard_map/all_to_all | solution.py:951
  128.0 87.8 %all-gather.13.cloned.1.call-start = ((), (), s32[]{:S(2)}) async-start(), calls=%async_computation.10 | async-start | bytes 2359296 | tf_op jit(solution)/shard_map/all_gather | solution.py:1101
  150.0 4.1 %collective-permute-start.14 = (f32[3,16,128]{2,1,0:T(8,128)}, f32[3,16,128]{2,1,0:T(8,128)S(1)}, u32[]{:S(2)}, u32[]{:S(2)}) collective-permute-start(f32[3,16,128]{2,1,0:T(8,128)} %get-tuple-element.79), channel_id=1, source_target_pairs={{0,2},{1,3},{2,0},{3,1},{4,6},{5,7},{6,4},{7,5},{8,10},{9,11},{10,... | collective-permute-start | bytes 73736 | tf_op jit(solution)/shard_map/ppermute | solution.py:885
  154.7 32.9 %collective-permute-start.15 = (bf16[16,16,16,128]{3,2,1,0:T(8,128)(2,1)}, bf16[16,16,16,128]{3,2,1,0:T(8,128)(2,1)S(1)}, u32[]{:S(2)}, u32[]{:S(2)}) collective-permute-start(bf16[16,16,16,128]{3,2,1,0:T(8,128)(2,1)} %after.17), channel_id=1, source_target_pairs={{0,2},{1,3},{2,0},{3,1},{4,6},{5,7},{6,4},{7,5},{8,10},{9,11},{10,... | collective-permute-start | bytes 3145736 | tf_op jit(solution)/shard_map/ppermute | solution.py:885
  156.6 17.5 %all-to-all-start.4 = ((f32[16,8,128]{2,1,0:T(8,128)}), f32[16,8,128]{2,1,0:T(8,128)S(1)}, u32[]{:S(2)}, u32[]{:S(2)}) async-start(f32[16,8,128]{2,1,0:T(8,128)} %first_sums.1), calls=%async_computation.4 | async-start | bytes 131072 | tf_op jit(solution)/shard_map/all_to_all | solution.py:951
  181.8 26.9 %all-to-all-start.5 = ((bf16[8,384,128]{2,1,0:T(8,128)(2,1)}), bf16[8,384,128]{2,1,0:T(8,128)(2,1)S(1)}, u32[]{:S(2)}, u32[]{:S(2)}) async-start(bf16[8,384,128]{2,1,0:T(8,128)(2,1)} %get-tuple-element.86.refs_12_), calls=%async_computation.5 | async-start | bytes 1572864 | tf_op jit(solution)/shard_map/all_to_all | solution.py:923
  201.9 3.1 %collective-permute-start.18 = (bf16[8,9,64,128]{3,2,1,0:T(8,128)(2,1)}, bf16[8,9,64,128]{3,2,1,0:T(8,128)(2,1)S(1)}, u32[]{:S(2)}, u32[]{:S(2)}) collective-permute-start(bf16[8,9,64,128]{3,2,1,0:T(8,128)(2,1)} %get-tuple-element.91), channel_id=1, source_target_pairs={{0,1},{1,0},{2,3},{3,2},{4,5},{5,4},{6,7},{7,6},{8,9},{9,8},{10,11... | collective-permute-start | bytes 3538952 | tf_op jit(solution)/shard_map/ppermute | solution.py:885
  209.6 35.0 %all-to-all-start.6 = ((bf16[8,9,64,128]{3,2,1,0:T(8,128)(2,1)}), bf16[8,9,64,128]{3,2,1,0:T(8,128)(2,1)S(1)}, u32[]{:S(2)}, u32[]{:S(2)}) async-start(bf16[8,9,64,128]{3,2,1,0:T(8,128)(2,1)} %after.20.refs_3_.refs_2_), calls=%async_computation.6 | async-start | bytes 2359296 | tf_op jit(solution)/shard_map/all_to_all | solution.py:923
  215.8 6.4 %collective-permute-start.13 = (bf16[16,64,256]{2,1,0:T(8,128)(2,1)S(1)}, bf16[16,64,256]{2,1,0:T(8,128)(2,1)S(1)}, u32[]{:S(2)}, u32[]{:S(2)}) collective-permute-start(bf16[16,64,256]{2,1,0:T(8,128)(2,1)S(1)} %copy-done.59), channel_id=1, source_target_pairs={{0,1},{1,0},{2,3},{3,2},{4,5},{5,4},{6,7},{7,6},{8,9},{9,8},{10,11... | collective-permute-start | bytes 1572872 | tf_op jit(solution)/shard_map/ppermute | solution.py:885
  220.6 14.6 %collective-permute-start.19 = (bf16[32,8192]{1,0:T(8,128)(2,1)}, bf16[32,8192]{1,0:T(8,128)(2,1)S(1)}, u32[]{:S(2)}, u32[]{:S(2)}) collective-permute-start(bf16[32,8192]{1,0:T(8,128)(2,1)} %get-tuple-element.92.refs_3_), channel_id=1, source_target_pairs={{0,2},{1,3},{2,0},{3,1},{4,6},{5,7},{6,4},{7,5},{8,10},{9,11},{10,... | collective-permute-start | bytes 1572872 | tf_op jit(solution)/shard_map/ppermute | solution.py:885
  236.7 11.3 %collective-permute-start.23 = (bf16[32,4096]{1,0:T(8,128)(2,1)S(1)}, bf16[32,4096]{1,0:T(8,128)(2,1)S(1)}, u32[]{:S(2)}, u32[]{:S(2)}) collective-permute-start(bf16[32,4096]{1,0:T(8,128)(2,1)S(1)} %get-tuple-element.99), channel_id=1, source_target_pairs={{0,1},{1,0},{2,3},{3,2},{4,5},{5,4},{6,7},{7,6},{8,9},{9,8},{10,11... | collective-permute-start | bytes 786440 | tf_op jit(solution)/shard_map/ppermute | solution.py:885
  236.9 11.2 %collective-permute-start.22 = (bf16[16,64,128]{2,1,0:T(8,128)(2,1)}, bf16[16,64,128]{2,1,0:T(8,128)(2,1)S(1)}, u32[]{:S(2)}, u32[]{:S(2)}) collective-permute-start(bf16[16,64,128]{2,1,0:T(8,128)(2,1)} %after.23), channel_id=1, source_target_pairs={{0,3},{1,2},{2,1},{3,0},{4,7},{5,6},{6,5},{7,4},{8,11},{9,10},{10,... | collective-permute-start | bytes 786440 | tf_op jit(solution)/shard_map/ppermute | solution.py:885
  238.3 13.1 %collective-permute-start.21 = (bf16[16,64,128]{2,1,0:T(8,128)(2,1)}, bf16[16,64,128]{2,1,0:T(8,128)(2,1)S(1)}, u32[]{:S(2)}, u32[]{:S(2)}) collective-permute-start(bf16[16,64,128]{2,1,0:T(8,128)(2,1)} %after.22), channel_id=1, source_target_pairs={{0,2},{1,3},{2,0},{3,1},{4,6},{5,7},{6,4},{7,5},{8,10},{9,11},{10,... | collective-permute-start | bytes 786440 | tf_op jit(solution)/shard_map/ppermute | solution.py:885
  238.9 12.5 %collective-permute-start.20 = (bf16[16,64,128]{2,1,0:T(8,128)(2,1)}, bf16[16,64,128]{2,1,0:T(8,128)(2,1)S(1)}, u32[]{:S(2)}, u32[]{:S(2)}) collective-permute-start(bf16[16,64,128]{2,1,0:T(8,128)(2,1)} %after.21), channel_id=1, source_target_pairs={{0,1},{1,0},{2,3},{3,2},{4,5},{5,4},{6,7},{7,6},{8,9},{9,8},{10,11... | collective-permute-start | bytes 786440 | tf_op jit(solution)/shard_map/ppermute | solution.py:885
  (66 other events, 292.9 us)
Sparse Core Ops, SparseCore 0:
  10.4 22.7 all-gather.6
  34.7 16.2 all-gather.8
  53.1 43.7 all-gather.14
  101.8 16.3 all-gather.10
  137.8 46.9 all-gather.12

commit v5 on v4

--- a/solution.py
+++ b/solution.py
@@ -1248,12 +1248,6 @@
     )
     if eight:
         skip_recv = swap_with(skip_send, "chan", 2)
-        skip_own, skip_other = call(
-            skip_add_body,
-            [((32, 4096), f32), ((32, 4096), bf16)],
-            (idx, skip_keep, skip_recv),
-            "skip_add", plain=True,
-        )
         blocks = [blocks[0]] + [after(b, skip_recv) for b in blocks[1:]]
     got = [blocks[0]] + [swap_with(blocks[k], "chan", k) for k in range(1, 4)]
     if eight:
@@ -1267,6 +1261,14 @@
         )
         exciter_sum = exciter_sum.T
         refiner_sum = refiner_sum.transpose(0, 1, 3, 2)
+        skip_own, skip_other = call(
+            skip_add_body,
+            [((32, 4096), f32), ((32, 4096), bf16)],
+            (idx, skip_keep, skip_recv),
+            "skip_add",
+            plain=True,
+            deps=(squeezer_sum,),
+        )
         (widener_sum,) = call(
             widener_sum_body,
             [(widener.shape, f32)],

time: 264 us -> 267 us (1.011)
  waiting for transfers between devices: 31.2 us -> 34.1 us
    ppermute x24, waiting for transfers between devices: 21.2 us -> 24.2 us  [swap_with(): lax.ppermute(v, axis, [(n, n ^ k) for n in range(lax.axis_size(axis))])]
    unnamed x127 -> x129, local copies, waits for them, and re-layouts: 24.5 us -> 24.6 us
  transfers between devices with their start and end apart: 35 -> 35, of which waited for: 10 -> 11; matrix products, arithmetic and copies ran while one was open for 4% -> 4% of each run, Pallas kernels for 41% -> 41%
where the time goes in v5:
time: 267 us; the launch traced here: 265 us
  Pallas kernels  112 us (42%)
  starting transfers between devices  47 us (18%)
  waiting for transfers between devices  34.1 us (13%)
  local copies, waits for them, and re-layouts  33.9 us (13%)
  blocking collectives  20.4 us (8%)
  between operations  14.7 us (6%)
  other arithmetic  3.14 us (1%)
    pallas_call x23, Pallas kernels, call(): pl.pallas_call(kernel, out_shape=results, in_specs=[pl.BlockSpec(memory_s...  112 us
    all_to_all x4, starting transfers between devices, over_batch(): return lax.all_to_all(v, 'batch', 0, 0, tiled=True)  24.8 us
    unnamed x129, local copies, waits for them, and re-layouts  24.6 us
    ppermute x24, waiting for transfers between devices, swap_with(): lax.ppermute(v, axis, [(n, n ^ k) for n in range(lax.axis_size(axis))])  24.2 us
    all_to_all x1, blocking collectives, exchange(): lax.all_to_all(copies, ('batch', 'chan'), 0, 0, tiled=True, axis_index_gr...  20.4 us
    ppermute x24, starting transfers between devices, swap_with(): lax.ppermute(v, axis, [(n, n ^ k) for n in range(lax.axis_size(axis))])  12.9 us
    all_to_all x2, starting transfers between devices, exchange(): lax.all_to_all(copies, ('batch', 'chan'), 0, 0, tiled=True, axis_index_gr...  8.97 us
    all_to_all x2, waiting for transfers between devices, exchange(): lax.all_to_all(copies, ('batch', 'chan'), 0, 0, tiled=True, axis_index_gr...  7.61 us
  transfers between devices with their start and end apart: 35, of which 11 were waited for; matrix products, arithmetic and copies ran while one was open for 4% of the time, Pallas kernels for 41%

profile of v5, /device:TPU:0, one launch (start us, length us, event | category | flops | bytes accessed | tf_op | source)
XLA Modules:
  0.0 265.4 jit_solution(7672973813364546670)
XLA Ops:
  11.5 7.4 %all-to-all-start = ((bf16[8,9,64,128]{3,2,1,0:T(8,128)(2,1)}), bf16[8,9,64,128]{3,2,1,0:T(8,128)(2,1)S(1)}, u32[]{:S(2)}, u32[]{:S(2)}) async-start(bf16[8,9,64,128]{3,2,1,0:T(8,128)(2,1)} %pack_wide.1), calls=%async_computation | async-start | bytes 2359296 | tf_op jit(solution)/shard_map/all_to_all | solution.py:923
  19.8 1.8 constant_dynamic-slice_fusion.2
  29.5 5.3 %upstream_turned.1.refs_5_.refs_8_.refs_3_ = bf16[16,16,16,128]{3,2,1,0:T(8,128)(2,1)} custom-call(s32[4]{0:T(128)} %pad_add_fusion.refs_0_, bf16[16,64,256]{2,1,0:T(8,128)(2,1)} %get-tuple-element.107.refs_1_, bf16[16,64,256]{2,1,0:T(8,128)(2,1)} %copy-done.41), custom_call_target="tpu_custom_call" | custom-call | tf_op jit(solution)/shard_map/upstream_turned/pallas_call | solution.py:131
  34.9 4.9 %collective-permute-done.1.refs_3_ = bf16[16,64,128]{2,1,0:T(8,128)(2,1)S(1)} collective-permute-done((bf16[16,64,128]{2,1,0:T(8,128)(2,1)S(1)}, bf16[16,64,128]{2,1,0:T(8,128)(2,1)S(1)}, u32[]{:S(2)}, u32[]{:S(2)}) %collective-permute-start.1) | collective-permute-done | bytes 262176 | tf_op jit(solution)/shard_map/ppermute | solution.py:885
  41.1 5.4 %features_turned.1.refs_1_.refs_3_.refs_11_ = bf16[10,10,16,512]{3,2,1,0:T(8,128)(2,1)} custom-call(s32[4]{0:T(128)} %pad_add_fusion.refs_0_, bf16[16,64,128]{2,1,0:T(8,128)(2,1)} %copy-done.36, bf16[16,64,128]{2,1,0:T(8,128)(2,1)} %copy-done.42, bf16[16,64,128]{2,1,0:T(8,128)(2,1)} %copy-done.43, bf16[16,64,128]{2,1,0:T(8,128)(2,1)} %collective-permute-done.2.refs_4_, ...), custom_call_target="tpu_custom_call" | custom-call | tf_op jit(solution)/shard_map/features_turned/pallas_call | solution.py:131
  52.4 5.6 %all-to-all-start.1 = ((bf16[8,8,16,128]{3,2,1,0:T(8,128)(2,1)}), bf16[8,8,16,128]{3,2,1,0:T(8,128)(2,1)S(1)}, u32[]{:S(2)}, u32[]{:S(2)}) async-start(bf16[8,8,16,128]{3,2,1,0:T(8,128)(2,1)} %after.13), calls=%async_computation.1 | async-start | bytes 524288 | tf_op jit(solution)/shard_map/all_to_all | solution.py:923
  59.0 9.6 %conv_one.1 = (bf16[4,2,8,2,16,128]{5,4,3,2,1,0:T(8,128)(2,1)}, bf16[4,2,8,2,16,128]{5,4,3,2,1,0:T(8,128)(2,1)}, bf16[8,2,8,2,16,128]{5,4,3,2,1,0:T(8,128)(2,1)}...) custom-call(s32[4]{0:T(128)} %pad_add_fusion.refs_0_, ...), custom_call_target="tpu_custom_call" | custom-call | tf_op jit(solution)/shard_map/conv_one/pallas_call | solution.py:131
  71.4 2.7 %squeeze.5 = (bf16[64,2048]{1,0:T(8,128)(2,1)}, f32[16,32,128]{2,1,0:T(8,128)}) custom-call(bf16[8,8,16,128]{3,2,1,0:T(8,128)(2,1)} %copy-done.38, bf16[256,2048]{1,0:T(8,128)(2,1)} %all-gather.9.cloned.1.call-done.refs_1_, f32[16,128]{1,0:T(8,128)} %get-tuple-element.60.refs_2_), custom_call_target="tpu_custom_call" | custom-call | tf_op jit(solution)/shard_map/squeeze/pallas_call | solution.py:131
  74.1 20.4 %all_to_all.35.refs_0_ = f32[16,32,128]{2,1,0:T(8,128)} all-to-all(f32[16,32,128]{2,1,0:T(8,128)} %get-tuple-element.61), channel_id=1, replica_groups={{0,1,4,5,8,9,12,13,16,17,20,21,24,25,28,29},{2,3,6,7,10,11,14,15,18,19,..., dimensions={0} | all-to-all | bytes 524288 | tf_op jit(solution)/shard_map/all_to_all | solution.py:951
  97.8 3.2 %collective-permute-done.8.refs_6_.refs_3_.refs_1_ = f32[3,16,128]{2,1,0:T(8,128)S(1)} collective-permute-done((f32[3,16,128]{2,1,0:T(8,128)S(1)}, f32[3,16,128]{2,1,0:T(8,128)S(1)}, u32[]{:S(2)}, u32[]{:S(2)}) %collective-permute-start.8) | collective-permute-done | bytes 24608 | tf_op jit(solution)/shard_map/ppermute | solution.py:885
  102.4 2.3 collective-permute-done.10.refs_2_
  109.8 9.6 %conv_two.1 = (bf16[18,18,16,256]{3,2,1,0:T(8,128)(2,1)}, f32[16,16,16,128]{3,2,1,0:T(8,128)}, bf16[16,16,16,128]{3,2,1,0:T(8,128)(2,1)}, f32[4,16,128]{2,1,0:T(8,128)}) custom-call(s32[4]{0:T(128)} %pad_add_fusion.refs_0_, bf16[8,16,16,128]{3,2,1,0:T(8,128)(2,1)} %bitcast.35, bf16[8,16,16,128]{3,2,1,0:T(8,128)(2,1)} %bitcast.37, ...), custom_call_target="tpu_custom_call" | custom-call | tf_op jit(solution)/shard_map/conv_two/pallas_call | solution.py:131
  120.1 2.7 %gate.1 = (f32[2,16,128]{2,1,0:T(8,128)}, f32[32,256]{1,0:T(8,128)}, f32[16,24,128]{2,1,0:T(8,128)}) custom-call(s32[4]{0:T(128)} %pad_add_fusion.refs_0_, f32[3,16,128]{2,1,0:T(8,128)} %copy-done.19, f32[3,16,128]{2,1,0:T(8,128)} %copy-done.52, f32[3,16,128]{2,1,0:T(8,128)} %copy-done.48, f32[3,16,128]{2,1,0:T(8,128)} %copy-done.53, ...), custom_call_target="tpu_custom_call" | custom-call | tf_op jit(solution)/shard_map/gate/pallas_call | solution.py:131
  122.8 5.3 %all-to-all-start.3 = ((f32[16,24,128]{2,1,0:T(8,128)}), f32[16,24,128]{2,1,0:T(8,128)S(1)}, u32[]{:S(2)}, u32[]{:S(2)}) async-start(f32[16,24,128]{2,1,0:T(8,128)} %get-tuple-element.69), calls=%async_computation.3 | async-start | bytes 393216 | tf_op jit(solution)/shard_map/all_to_all | solution.py:951
  129.4 7.6 %all-to-all-done.3.refs_13_.refs_1_ = f32[16,24,128]{2,1,0:T(8,128)S(1)} async-done(((f32[16,24,128]{2,1,0:T(8,128)}), f32[16,24,128]{2,1,0:T(8,128)S(1)}, u32[]{:S(2)}, u32[]{:S(2)}) %all-to-all-start.3) | async-done | bytes 196640 | tf_op jit(solution)/shard_map/all_to_all | solution.py:951
  137.8 12.2 %back_two.1 = (bf16[18,18,16,256]{3,2,1,0:T(8,128)(2,1)}, bf16[16,16,16,128]{3,2,1,0:T(8,128)(2,1)}, bf16[16,16,16,128]{3,2,1,0:T(8,128)(2,1)}, f32[3,16,128]{2,...) custom-call(s32[4]{0:T(128)} %pad_add_fusion.refs_0_, f32[16,16,16,128]{3,2,1,0:T(8,128)} %get-tuple-element.64.refs_1_.refs_3_, ...), custom_call_target="tpu_custom_call" | custom-call | tf_op jit(solution)/shard_map/back_two/pallas_call | solution.py:131
  150.5 3.5 %collective-permute-done.14.refs_1_ = f32[3,16,128]{2,1,0:T(8,128)S(1)} collective-permute-done((f32[3,16,128]{2,1,0:T(8,128)}, f32[3,16,128]{2,1,0:T(8,128)S(1)}, u32[]{:S(2)}, u32[]{:S(2)}) %collective-permute-start.14) | collective-permute-done | bytes 24608 | tf_op jit(solution)/shard_map/ppermute | solution.py:885
  156.6 3.7 %all-to-all-start.4 = ((f32[16,8,128]{2,1,0:T(8,128)}), f32[16,8,128]{2,1,0:T(8,128)S(1)}, u32[]{:S(2)}, u32[]{:S(2)}) async-start(f32[16,8,128]{2,1,0:T(8,128)} %first_sums.1), calls=%async_computation.4 | async-start | bytes 131072 | tf_op jit(solution)/shard_map/all_to_all | solution.py:951
  160.3 13.8 %refiner_grad.1 = (bf16[8,5,64,128]{3,2,1,0:T(8,128)(2,1)}, bf16[8,5,64,128]{3,2,1,0:T(8,128)(2,1)}, bf16[16,64,256]{2,1,0:T(8,128)(2,1)}, bf16[16,64,256]{2,1,0:T(8,128)(2,1)}) custom-call(s32[4]{0:T(128)} %pad_add_fusion.refs_0_, bf16[18,18,16,256]{3,2,1,0:T(8,128)(2,1)} %get-tuple-element.71.refs_1_, bf16[18,18,16,256]{3,2,1,0:T(8,128)(2,1)} %get-tuple-element.72.refs_2_, ...), custom_call_target="tpu_custom_call" | custom-call | tf_op jit(solution)/shard_map/refiner_grad/pallas_call | solution.py:131
  177.9 3.9 %excite_back.1 = (bf16[32,128]{1,0:T(8,128)(2,1)}, bf16[8,384,128]{2,1,0:T(8,128)(2,1)}) custom-call(s32[4]{0:T(128)} %pad_add_fusion.refs_0_, f32[2,16,128]{2,1,0:T(8,128)} %copy-done.51, f32[2,16,128]{2,1,0:T(8,128)} %copy-done.54, f32[32,256]{1,0:T(8,128)} %get-tuple-element.82.refs_3_, bf16[128,256]{1,0:T(8,128)(2,1)} %copy-done.13, ...), custom_call_target="tpu_custom_call" | custom-call | tf_op jit(solution)/shard_map/excite_back/pallas_call | solution.py:131
  181.8 5.7 %all-to-all-start.5 = ((bf16[8,384,128]{2,1,0:T(8,128)(2,1)}), bf16[8,384,128]{2,1,0:T(8,128)(2,1)S(1)}, u32[]{:S(2)}, u32[]{:S(2)}) async-start(bf16[8,384,128]{2,1,0:T(8,128)(2,1)} %get-tuple-element.86.refs_12_), calls=%async_computation.5 | async-start | bytes 1572864 | tf_op jit(solution)/shard_map/all_to_all | solution.py:923
  188.6 13.4 %back_one.1 = (bf16[2,2,10,10,16,256]{5,4,3,2,1,0:T(8,128)(2,1)}, f32[8,128]{1,0:T(8,128)}, bf16[8,9,64,128]{3,2,1,0:T(8,128)(2,1)}, bf16[8,9,64,128]{3,2,1,0:T(8,128)(2,1)}) custom-call(s32[4]{0:T(128)} %pad_add_fusion.refs_0_, bf16[4,2,8,2,16,128]{5,4,3,2,1,0:T(8,128)(2,1)} %get-tuple-element.57.refs_1_, ...), custom_call_target="tpu_custom_call" | custom-call | tf_op jit(solution)/shard_map/back_one/pallas_call | solution.py:131
  202.0 3.0 %collective-permute-done.18.refs_1_ = bf16[8,9,64,128]{3,2,1,0:T(8,128)(2,1)S(1)} collective-permute-done((bf16[8,9,64,128]{3,2,1,0:T(8,128)(2,1)}, bf16[8,9,64,128]{3,2,1,0:T(8,128)(2,1)S(1)}, u32[]{:S(2)}, u32[]{:S(2)}) %collective-permute-start.18) | collective-permute-done | bytes 1179680 | tf_op jit(solution)/shard_map/ppermute | solution.py:885
  206.1 2.6 widener_pair.1.refs_0_
  209.6 6.1 %all-to-all-start.6 = ((bf16[8,9,64,128]{3,2,1,0:T(8,128)(2,1)}), bf16[8,9,64,128]{3,2,1,0:T(8,128)(2,1)S(1)}, u32[]{:S(2)}, u32[]{:S(2)}) async-start(bf16[8,9,64,128]{3,2,1,0:T(8,128)(2,1)} %after.20.refs_3_.refs_2_), calls=%async_computation.6 | async-start | bytes 2359296 | tf_op jit(solution)/shard_map/all_to_all | solution.py:923
  215.9 4.7 %skip_back.1 = (bf16[32,8192]{1,0:T(8,128)(2,1)}, bf16[32,8192]{1,0:T(8,128)(2,1)}) custom-call(s32[4]{0:T(128)} %pad_add_fusion.refs_0_, bf16[32,128]{1,0:T(8,128)(2,1)} %get-tuple-element.89.refs_1_, bf16[512,2048]{1,0:T(8,128)(2,1)} %all-gather.13.cloned.1.call-done.refs_2_, bf16[8,9,64,128]{3,2,1,0:T(8,128)(2,1)} %after.20.refs_3_.refs_2_), custom_call_target="tpu_custom_call" | custom-call | tf_op jit(solution)/shard_map/skip_back/pallas_call | solution.py:131
  224.0 2.9 %squeeze_back.1 = (f32[32,64]{1,0:T(8,128)}, f32[16,64,128]{2,1,0:T(8,128)}, f32[9,2,32,64]{3,2,1,0:T(8,128)}) custom-call(bf16[8,384,128]{2,1,0:T(8,128)(2,1)} %copy-done.26, bf16[256,2048]{1,0:T(8,128)(2,1)} %all-gather.11.cloned.1.call-done.refs_14_.refs_1_, bf16[8,9,64,128]{3,2,1,0:T(8,128)(2,1)} %after.20.refs_3_.refs_2_), custom_call_target="tpu_custom_call" | custom-call | tf_op jit(solution)/shard_map/squeeze_back/pallas_call | solution.py:131
  227.0 11.2 %input_back.1 = (bf16[16,64,128]{2,1,0:T(8,128)(2,1)}, bf16[16,64,128]{2,1,0:T(8,128)(2,1)}, bf16[16,64,128]{2,1,0:T(8,128)(2,1)}, bf16[16,64,128]{2,1,0:T(8,128)(2,1)}) custom-call(s32[4]{0:T(128)} %pad_add_fusion.refs_0_, bf16[2,2,10,10,16,256]{5,4,3,2,1,0:T(8,128)(2,1)} %get-tuple-element.87.refs_1_, bf16[16,256,512]{2,1,0:T(8,128)(2,1)} %get-tuple-element.88.refs_2_, ...), custom_call_target="tpu_custom_call" | custom-call | tf_op jit(solution)/shard_map/input_back/pallas_call | solution.py:131
  242.5 2.1 all-to-all-done.6.refs_0_
  245.7 2.4 widener_sum.1.refs_7_
  248.3 6.1 %collective-permute-done.21.refs_3_ = bf16[16,64,128]{2,1,0:T(8,128)(2,1)S(1)} collective-permute-done((bf16[16,64,128]{2,1,0:T(8,128)(2,1)}, bf16[16,64,128]{2,1,0:T(8,128)(2,1)S(1)}, u32[]{:S(2)}, u32[]{:S(2)}) %collective-permute-start.21) | collective-permute-done | bytes 262176 | tf_op jit(solution)/shard_map/ppermute | solution.py:885
  255.2 3.7 %last_join.1 = (f32[32,64,128]{2,1,0:T(8,128)}, f32[32,32,128]{2,1,0:T(8,128)}) custom-call(s32[4]{0:T(128)} %pad_add_fusion.refs_0_, bf16[16,64,128]{2,1,0:T(8,128)(2,1)} %get-tuple-element.93.refs_1_, bf16[16,64,128]{2,1,0:T(8,128)(2,1)} %copy-done.47, bf16[16,64,128]{2,1,0:T(8,128)(2,1)} %copy-done.46, bf16[16,64,128]{2,1,0:T(8,128)(2,1)} %copy-done.45, ...), custom_call_target="tpu_custom_call" | custom-call | tf_op jit(solution)/shard_map/last_join/pallas_call | solution.py:131
  (233 shorter events, 56.0 us)
Async XLA Ops:
  7.2 41.6 %all-gather.7.cloned.1.call-start = ((), (), s32[]{:S(2)}) async-start(), calls=%async_computation.7 | async-start | bytes 1310720 | tf_op jit(solution)/shard_map/all_gather | solution.py:980
  11.5 39.8 %all-to-all-start = ((bf16[8,9,64,128]{3,2,1,0:T(8,128)(2,1)}), bf16[8,9,64,128]{3,2,1,0:T(8,128)(2,1)S(1)}, u32[]{:S(2)}, u32[]{:S(2)}) async-start(bf16[8,9,64,128]{3,2,1,0:T(8,128)(2,1)} %pack_wide.1), calls=%async_computation | async-start | bytes 2359296 | tf_op jit(solution)/shard_map/all_to_all | solution.py:923
  18.9 51.8 %all-gather.9.cloned.1.call-start = ((), (), s32[]{:S(2)}) async-start(), calls=%async_computation.8 | async-start | bytes 1310720 | tf_op jit(solution)/shard_map/all_gather | solution.py:982
  19.7 81.9 %all-gather.15.cloned.1.call-start = ((), (), s32[]{:S(2)}) async-start(), calls=%async_computation.11 | async-start | bytes 1179648 | tf_op jit(solution)/shard_map/all_gather | solution.py:1002
  21.7 13.2 %collective-permute-start = (bf16[16,64,128]{2,1,0:T(8,128)(2,1)}, bf16[16,64,128]{2,1,0:T(8,128)(2,1)S(1)}, u32[]{:S(2)}, u32[]{:S(2)}) collective-permute-start(bf16[16,64,128]{2,1,0:T(8,128)(2,1)} %get-tuple-element.108), channel_id=1, source_target_pairs={{0,1},{1,0},{2,3},{3,2},{4,5},{5,4},{6,7},{7,6},{8,9},{9,8},{10,11... | collective-permute-start | bytes 786440 | tf_op jit(solution)/shard_map/ppermute | solution.py:885
  21.8 18.0 %collective-permute-start.2 = (bf16[16,64,128]{2,1,0:T(8,128)(2,1)}, bf16[16,64,128]{2,1,0:T(8,128)(2,1)}, u32[]{:S(2)}, u32[]{:S(2)}) collective-permute-start(bf16[16,64,128]{2,1,0:T(8,128)(2,1)} %get-tuple-element.108), channel_id=1, source_target_pairs={{0,3},{1,2},{2,1},{3,0},{4,7},{5,6},{6,5},{7,4},{8,11},{9,10},{10,... | collective-permute-start | bytes 786440 | tf_op jit(solution)/shard_map/ppermute | solution.py:885
  24.4 4.3 %collective-permute-start.3 = (bf16[16,64,256]{2,1,0:T(8,128)(2,1)}, bf16[16,64,256]{2,1,0:T(8,128)(2,1)S(1)}, u32[]{:S(2)}, u32[]{:S(2)}) collective-permute-start(bf16[16,64,256]{2,1,0:T(8,128)(2,1)} %get-tuple-element.106), channel_id=1, source_target_pairs={{0,1},{1,0},{2,3},{3,2},{4,5},{5,4},{6,7},{7,6},{8,9},{9,8},{10,11... | collective-permute-start | bytes 1572872 | tf_op jit(solution)/shard_map/ppermute | solution.py:885
  24.5 15.2 %collective-permute-start.1 = (bf16[16,64,128]{2,1,0:T(8,128)(2,1)S(1)}, bf16[16,64,128]{2,1,0:T(8,128)(2,1)S(1)}, u32[]{:S(2)}, u32[]{:S(2)}) collective-permute-start(bf16[16,64,128]{2,1,0:T(8,128)(2,1)S(1)} %get-tuple-element.109.refs_1_), channel_id=1, source_target_pairs={{0,2},{1,3},{2,0},{3,1},{4,6},{5,7},{6,4},{7,5},{8,10},{9,11},{10,... | collective-permute-start | bytes 786440 | tf_op jit(solution)/shard_map/ppermute | solution.py:885
  26.5 20.0 %collective-permute-start.9 = (bf16[64,32]{1,0:T(8,128)(2,1)S(1)}, bf16[64,32]{1,0:T(8,128)(2,1)S(1)}, u32[]{:S(2)}, u32[]{:S(2)}) collective-permute-start(bf16[64,32]{1,0:T(8,128)(2,1)S(1)} %copy.55.refs_1_), channel_id=1, source_target_pairs={{0,2},{1,3},{2,0},{3,1},{4,6},{5,7},{6,4},{7,5},{8,10},{9,11},{10,... | collective-permute-start | bytes 12296 | tf_op jit(solution)/shard_map/ppermute | solution.py:885
  52.3 5.6 %collective-permute-start.5 = (bf16[8,9,64,128]{3,2,1,0:T(8,128)(2,1)}, bf16[8,9,64,128]{3,2,1,0:T(8,128)(2,1)S(1)}, u32[]{:S(2)}, u32[]{:S(2)}) collective-permute-start(bf16[8,9,64,128]{3,2,1,0:T(8,128)(2,1)} %after.12.refs_1_), channel_id=1, source_target_pairs={{0,1},{1,0},{2,3},{3,2},{4,5},{5,4},{6,7},{7,6},{8,9},{9,8},{10,11... | collective-permute-start | bytes 3538952 | tf_op jit(solution)/shard_map/ppermute | solution.py:885
  52.4 18.4 %all-to-all-start.1 = ((bf16[8,8,16,128]{3,2,1,0:T(8,128)(2,1)}), bf16[8,8,16,128]{3,2,1,0:T(8,128)(2,1)S(1)}, u32[]{:S(2)}, u32[]{:S(2)}) async-start(bf16[8,8,16,128]{3,2,1,0:T(8,128)(2,1)} %after.13), calls=%async_computation.1 | async-start | bytes 524288 | tf_op jit(solution)/shard_map/all_to_all | solution.py:923
  57.9 79.9 %all-gather.11.cloned.1.call-start = ((), (), s32[]{:S(2)}) async-start(), calls=%async_computation.9 | async-start | bytes 1310720 | tf_op jit(solution)/shard_map/all_gather | solution.py:1061
  68.6 25.9 %collective-permute-start.6 = (bf16[4,2,8,2,16,128]{5,4,3,2,1,0:T(8,128)(2,1)}, bf16[4,2,8,2,16,128]{5,4,3,2,1,0:T(8,128)(2,1)S(1)}, u32[]{:S(2)}, u32[]{:S(2)}) collective-permute-start(bf16[4,2,8,2,16,128]{5,4,3,2,1,0:T(8,128)(2,1)} %get-tuple-element.57.refs_1_), channel_id=1, source_target_pairs={{0,2},{1,3},{2,0},{3,1},{4,6},{5,7},{6,4},{7,5},{8,10},{9,11},{10,... | collective-permute-start | bytes 1572872 | tf_op jit(solution)/shard_map/ppermute | solution.py:885
  69.2 25.4 %collective-permute-start.7 = (bf16[4,2,8,2,16,128]{5,4,3,2,1,0:T(8,128)(2,1)}, bf16[4,2,8,2,16,128]{5,4,3,2,1,0:T(8,128)(2,1)S(1)}, u32[]{:S(2)}, u32[]{:S(2)}) collective-permute-start(bf16[4,2,8,2,16,128]{5,4,3,2,1,0:T(8,128)(2,1)} %get-tuple-element.58.refs_2_), channel_id=1, source_target_pairs={{0,2},{1,3},{2,0},{3,1},{4,6},{5,7},{6,4},{7,5},{8,10},{9,11},{10,... | collective-permute-start | bytes 1572872 | tf_op jit(solution)/shard_map/ppermute | solution.py:885
  97.1 3.9 %collective-permute-start.8 = (f32[3,16,128]{2,1,0:T(8,128)S(1)}, f32[3,16,128]{2,1,0:T(8,128)S(1)}, u32[]{:S(2)}, u32[]{:S(2)}) collective-permute-start(f32[3,16,128]{2,1,0:T(8,128)S(1)} %get-tuple-element.62.refs_5_.refs_1_), channel_id=1, source_target_pairs={{0,2},{1,3},{2,0},{3,1},{4,6},{5,7},{6,4},{7,5},{8,10},{9,11},{10,... | collective-permute-start | bytes 73736 | tf_op jit(solution)/shard_map/ppermute | solution.py:885
  101.7 3.0 %collective-permute-start.10 = (bf16[8,8,64,128]{3,2,1,0:T(8,128)(2,1)}, bf16[8,8,64,128]{3,2,1,0:T(8,128)(2,1)S(1)}, u32[]{:S(2)}, u32[]{:S(2)}) collective-permute-start(bf16[8,8,64,128]{3,2,1,0:T(8,128)(2,1)} %after.15.refs_1_), channel_id=1, source_target_pairs={{0,1},{1,0},{2,3},{3,2},{4,5},{5,4},{6,7},{7,6},{8,9},{9,8},{10,11... | collective-permute-start | bytes 3145736 | tf_op jit(solution)/shard_map/ppermute | solution.py:885
  101.8 17.6 %collective-permute-start.11 = (f32[3,16,128]{2,1,0:T(8,128)S(1)}, f32[3,16,128]{2,1,0:T(8,128)S(1)}, u32[]{:S(2)}, u32[]{:S(2)}) collective-permute-start(f32[3,16,128]{2,1,0:T(8,128)S(1)} %get-tuple-element.62.refs_5_.refs_1_), channel_id=1, source_target_pairs={{0,1},{1,0},{2,3},{3,2},{4,5},{5,4},{6,7},{7,6},{8,9},{9,8},{10,11... | collective-permute-start | bytes 73736 | tf_op jit(solution)/shard_map/ppermute | solution.py:885
  102.4 17.0 %collective-permute-start.12 = (f32[3,16,128]{2,1,0:T(8,128)S(1)}, f32[3,16,128]{2,1,0:T(8,128)S(1)}, u32[]{:S(2)}, u32[]{:S(2)}) collective-permute-start(f32[3,16,128]{2,1,0:T(8,128)S(1)} %copy-done.49), channel_id=1, source_target_pairs={{0,1},{1,0},{2,3},{3,2},{4,5},{5,4},{6,7},{7,6},{8,9},{9,8},{10,11... | collective-permute-start | bytes 73736 | tf_op jit(solution)/shard_map/ppermute | solution.py:885
  122.8 14.3 %all-to-all-start.3 = ((f32[16,24,128]{2,1,0:T(8,128)}), f32[16,24,128]{2,1,0:T(8,128)S(1)}, u32[]{:S(2)}, u32[]{:S(2)}) async-start(f32[16,24,128]{2,1,0:T(8,128)} %get-tuple-element.69), calls=%async_computation.3 | async-start | bytes 393216 | tf_op jit(solution)/shard_map/all_to_all | solution.py:951
  128.0 87.8 %all-gather.13.cloned.1.call-start = ((), (), s32[]{:S(2)}) async-start(), calls=%async_computation.10 | async-start | bytes 2359296 | tf_op jit(solution)/shard_map/all_gather | solution.py:1101
  150.0 4.1 %collective-permute-start.14 = (f32[3,16,128]{2,1,0:T(8,128)}, f32[3,16,128]{2,1,0:T(8,128)S(1)}, u32[]{:S(2)}, u32[]{:S(2)}) collective-permute-start(f32[3,16,128]{2,1,0:T(8,128)} %get-tuple-element.79), channel_id=1, source_target_pairs={{0,2},{1,3},{2,0},{3,1},{4,6},{5,7},{6,4},{7,5},{8,10},{9,11},{10,... | collective-permute-start | bytes 73736 | tf_op jit(solution)/shard_map/ppermute | solution.py:885
  154.7 32.9 %collective-permute-start.15 = (bf16[16,16,16,128]{3,2,1,0:T(8,128)(2,1)}, bf16[16,16,16,128]{3,2,1,0:T(8,128)(2,1)S(1)}, u32[]{:S(2)}, u32[]{:S(2)}) collective-permute-start(bf16[16,16,16,128]{3,2,1,0:T(8,128)(2,1)} %after.17), channel_id=1, source_target_pairs={{0,2},{1,3},{2,0},{3,1},{4,6},{5,7},{6,4},{7,5},{8,10},{9,11},{10,... | collective-permute-start | bytes 3145736 | tf_op jit(solution)/shard_map/ppermute | solution.py:885
  156.6 17.5 %all-to-all-start.4 = ((f32[16,8,128]{2,1,0:T(8,128)}), f32[16,8,128]{2,1,0:T(8,128)S(1)}, u32[]{:S(2)}, u32[]{:S(2)}) async-start(f32[16,8,128]{2,1,0:T(8,128)} %first_sums.1), calls=%async_computation.4 | async-start | bytes 131072 | tf_op jit(solution)/shard_map/all_to_all | solution.py:951
  181.8 26.9 %all-to-all-start.5 = ((bf16[8,384,128]{2,1,0:T(8,128)(2,1)}), bf16[8,384,128]{2,1,0:T(8,128)(2,1)S(1)}, u32[]{:S(2)}, u32[]{:S(2)}) async-start(bf16[8,384,128]{2,1,0:T(8,128)(2,1)} %get-tuple-element.86.refs_12_), calls=%async_computation.5 | async-start | bytes 1572864 | tf_op jit(solution)/shard_map/all_to_all | solution.py:923
  201.9 3.1 %collective-permute-start.18 = (bf16[8,9,64,128]{3,2,1,0:T(8,128)(2,1)}, bf16[8,9,64,128]{3,2,1,0:T(8,128)(2,1)S(1)}, u32[]{:S(2)}, u32[]{:S(2)}) collective-permute-start(bf16[8,9,64,128]{3,2,1,0:T(8,128)(2,1)} %get-tuple-element.91), channel_id=1, source_target_pairs={{0,1},{1,0},{2,3},{3,2},{4,5},{5,4},{6,7},{7,6},{8,9},{9,8},{10,11... | collective-permute-start | bytes 3538952 | tf_op jit(solution)/shard_map/ppermute | solution.py:885
  209.6 35.0 %all-to-all-start.6 = ((bf16[8,9,64,128]{3,2,1,0:T(8,128)(2,1)}), bf16[8,9,64,128]{3,2,1,0:T(8,128)(2,1)S(1)}, u32[]{:S(2)}, u32[]{:S(2)}) async-start(bf16[8,9,64,128]{3,2,1,0:T(8,128)(2,1)} %after.20.refs_3_.refs_2_), calls=%async_computation.6 | async-start | bytes 2359296 | tf_op jit(solution)/shard_map/all_to_all | solution.py:923
  215.8 6.4 %collective-permute-start.13 = (bf16[16,64,256]{2,1,0:T(8,128)(2,1)S(1)}, bf16[16,64,256]{2,1,0:T(8,128)(2,1)S(1)}, u32[]{:S(2)}, u32[]{:S(2)}) collective-permute-start(bf16[16,64,256]{2,1,0:T(8,128)(2,1)S(1)} %copy-done.60), channel_id=1, source_target_pairs={{0,1},{1,0},{2,3},{3,2},{4,5},{5,4},{6,7},{7,6},{8,9},{9,8},{10,11... | collective-permute-start | bytes 1572872 | tf_op jit(solution)/shard_map/ppermute | solution.py:885
  220.6 17.6 %collective-permute-start.19 = (bf16[32,8192]{1,0:T(8,128)(2,1)}, bf16[32,8192]{1,0:T(8,128)(2,1)S(1)}, u32[]{:S(2)}, u32[]{:S(2)}) collective-permute-start(bf16[32,8192]{1,0:T(8,128)(2,1)} %get-tuple-element.92.refs_3_), channel_id=1, source_target_pairs={{0,2},{1,3},{2,0},{3,1},{4,6},{5,7},{6,4},{7,5},{8,10},{9,11},{10,... | collective-permute-start | bytes 1572872 | tf_op jit(solution)/shard_map/ppermute | solution.py:885
  239.7 8.3 %collective-permute-start.23 = (bf16[32,4096]{1,0:T(8,128)(2,1)S(1)}, bf16[32,4096]{1,0:T(8,128)(2,1)S(1)}, u32[]{:S(2)}, u32[]{:S(2)}) collective-permute-start(bf16[32,4096]{1,0:T(8,128)(2,1)S(1)} %get-tuple-element.100), channel_id=1, source_target_pairs={{0,1},{1,0},{2,3},{3,2},{4,5},{5,4},{6,7},{7,6},{8,9},{9,8},{10,11... | collective-permute-start | bytes 786440 | tf_op jit(solution)/shard_map/ppermute | solution.py:885
  239.9 8.4 %collective-permute-start.22 = (bf16[16,64,128]{2,1,0:T(8,128)(2,1)}, bf16[16,64,128]{2,1,0:T(8,128)(2,1)S(1)}, u32[]{:S(2)}, u32[]{:S(2)}) collective-permute-start(bf16[16,64,128]{2,1,0:T(8,128)(2,1)} %after.23), channel_id=1, source_target_pairs={{0,3},{1,2},{2,1},{3,0},{4,7},{5,6},{6,5},{7,4},{8,11},{9,10},{10,... | collective-permute-start | bytes 786440 | tf_op jit(solution)/shard_map/ppermute | solution.py:885
  240.4 14.0 %collective-permute-start.21 = (bf16[16,64,128]{2,1,0:T(8,128)(2,1)}, bf16[16,64,128]{2,1,0:T(8,128)(2,1)S(1)}, u32[]{:S(2)}, u32[]{:S(2)}) collective-permute-start(bf16[16,64,128]{2,1,0:T(8,128)(2,1)} %after.22), channel_id=1, source_target_pairs={{0,2},{1,3},{2,0},{3,1},{4,6},{5,7},{6,4},{7,5},{8,10},{9,11},{10,... | collective-permute-start | bytes 786440 | tf_op jit(solution)/shard_map/ppermute | solution.py:885
  241.9 12.5 %collective-permute-start.20 = (bf16[16,64,128]{2,1,0:T(8,128)(2,1)}, bf16[16,64,128]{2,1,0:T(8,128)(2,1)S(1)}, u32[]{:S(2)}, u32[]{:S(2)}) collective-permute-start(bf16[16,64,128]{2,1,0:T(8,128)(2,1)} %after.21), channel_id=1, source_target_pairs={{0,1},{1,0},{2,3},{3,2},{4,5},{5,4},{6,7},{7,6},{8,9},{9,8},{10,11... | collective-permute-start | bytes 786440 | tf_op jit(solution)/shard_map/ppermute | solution.py:885
  (67 other events, 309.9 us)
Sparse Core Ops, SparseCore 0:
  10.4 22.7 all-gather.6
  34.7 16.2 all-gather.8
  53.1 43.6 all-gather.14
  101.8 16.3 all-gather.10
  137.9 46.7 all-gather.12

commit v6 on v4

--- a/solution.py
+++ b/solution.py
@@ -483,7 +483,9 @@
         )
 
     none = jnp.zeros((16, 128), f32)
-    squares, plain, cross = lax.fori_loop(0, 16, spread, (none, none, none))
+    squares, plain, cross = lax.fori_loop(
+        0, 16, spread, (none, none, none), unroll=2
+    )
     sums[0] = mean_s
     sums[1] = plain
     sums[2] = cross
@@ -688,7 +690,7 @@
                     grad[a, b, i + 1, 1:9, :, 128:256] = (d * g * (1.0 - s)).astype(bf16)
             return carry
 
-        lax.fori_loop(0, 8, step, 0)
+        lax.fori_loop(0, 8, step, 0, unroll=2)
         io.send(0)
         io.need(9)
         widener_grad(idx[1], grad, x, keep, send, work)
@@ -822,14 +824,12 @@
         [dot(d_squeezed.astype(bf16), pick_out), dot(d_excited, pick_out)], axis=-1
     ).astype(bf16)
     vectors[...] = both
-    pick_in = onehot((iota((256, 1024), 0) // 32 == iota((256, 1024), 1) // 128)
-                     & (iota((256, 1024), 0) % 32 == iota((256, 1024), 1) % 128))
-    picked = dot(swish, pick_in).astype(bf16)
+    none = jnp.zeros((32, 96), bf16)
     total = (fine[...].astype(f32) + recv[...].astype(f32)).astype(bf16)
     out[:, :320] = total.reshape(8, 320, 128)
     for k in range(8):
         out[k, 320:352] = both
-        out[k, 352:384] = picked[:, k * 128 : k * 128 + 128]
+        out[k, 352:384] = jnp.concatenate([swish[:, k * 32 : k * 32 + 32], none], axis=-1)
 
 
 def quarters_first(v):
@@ -874,8 +874,10 @@
     send[...] = jnp.where(first, hi, lo).astype(bf16)
 
 
-def last_join_body(idx, b0, b1, b2, b3, own, other, out, skip):
+def last_join_body(io, idx, b0, b1, b2, b3, own, other, out, skip):
     input_join_body(idx, b0, b1, b2, b3, out)
+    io.send(0)
+    io.need(4, 5)
     for r in range(32):
         lanes = slice(r * 128, r * 128 + 128)
         skip[:, r, :] = own[:, lanes] + other[:, lanes].astype(f32)
@@ -1279,6 +1281,7 @@
             [(features.shape, f32), (skip_feature.shape, f32)],
             (idx, *got, skip_own, swap_with(skip_other, "chan", 1)),
             "last_join",
+            late=(4, 5),
             deps=(widener_sum, squeezer_sum, output),
         )
     else:

time: 264 us -> 264 us (level)
  no operation moved by 1% of the time
where the time goes in v6:
time: 264 us; the launch traced here: 262 us
  Pallas kernels  112 us (42%)
  starting transfers between devices  46.9 us (18%)
  local copies, waits for them, and re-layouts  33.9 us (13%)
  waiting for transfers between devices  31.2 us (12%)
  blocking collectives  20.4 us (8%)
  between operations  14.6 us (6%)
  other arithmetic  3.14 us (1%)
    pallas_call x23, Pallas kernels, call(): pl.pallas_call(kernel, out_shape=results, in_specs=[pl.BlockSpec(memory_s...  112 us
    all_to_all x4, starting transfers between devices, over_batch(): return lax.all_to_all(v, 'batch', 0, 0, tiled=True)  24.8 us
    unnamed x127, local copies, waits for them, and re-layouts  24.5 us
    ppermute x24, waiting for transfers between devices, swap_with(): lax.ppermute(v, axis, [(n, n ^ k) for n in range(lax.axis_size(axis))])  21.2 us
    all_to_all x1, blocking collectives, exchange(): lax.all_to_all(copies, ('batch', 'chan'), 0, 0, tiled=True, axis_index_gr...  20.4 us
    ppermute x24, starting transfers between devices, swap_with(): lax.ppermute(v, axis, [(n, n ^ k) for n in range(lax.axis_size(axis))])  13 us
    all_to_all x2, starting transfers between devices, exchange(): lax.all_to_all(copies, ('batch', 'chan'), 0, 0, tiled=True, axis_index_gr...  8.93 us
    all_to_all x2, waiting for transfers between devices, exchange(): lax.all_to_all(copies, ('batch', 'chan'), 0, 0, tiled=True, axis_index_gr...  7.61 us
  transfers between devices with their start and end apart: 35, of which 10 were waited for; matrix products, arithmetic and copies ran while one was open for 4% of the time, Pallas kernels for 41%

profile of v6, /device:TPU:0, one launch (start us, length us, event | category | flops | bytes accessed | tf_op | source)
XLA Modules:
  0.0 262.2 jit_solution(10783932033571448206)
XLA Ops:
  11.5 7.4 %all-to-all-start = ((bf16[8,9,64,128]{3,2,1,0:T(8,128)(2,1)}), bf16[8,9,64,128]{3,2,1,0:T(8,128)(2,1)S(1)}, u32[]{:S(2)}, u32[]{:S(2)}) async-start(bf16[8,9,64,128]{3,2,1,0:T(8,128)(2,1)} %pack_wide.1), calls=%async_computation | async-start | bytes 2359296 | tf_op jit(solution)/shard_map/all_to_all | solution.py:925
  19.8 1.8 constant_dynamic-slice_fusion.2
  29.5 5.3 %upstream_turned.1.refs_5_.refs_8_.refs_3_ = bf16[16,16,16,128]{3,2,1,0:T(8,128)(2,1)} custom-call(s32[4]{0:T(128)} %pad_add_fusion.refs_0_, bf16[16,64,256]{2,1,0:T(8,128)(2,1)} %get-tuple-element.107.refs_1_, bf16[16,64,256]{2,1,0:T(8,128)(2,1)} %copy-done.40), custom_call_target="tpu_custom_call" | custom-call | tf_op jit(solution)/shard_map/upstream_turned/pallas_call | solution.py:131
  34.9 4.9 %collective-permute-done.1.refs_3_ = bf16[16,64,128]{2,1,0:T(8,128)(2,1)S(1)} collective-permute-done((bf16[16,64,128]{2,1,0:T(8,128)(2,1)S(1)}, bf16[16,64,128]{2,1,0:T(8,128)(2,1)S(1)}, u32[]{:S(2)}, u32[]{:S(2)}) %collective-permute-start.1) | collective-permute-done | bytes 262176 | tf_op jit(solution)/shard_map/ppermute | solution.py:887
  41.1 5.4 %features_turned.1.refs_1_.refs_3_.refs_11_ = bf16[10,10,16,512]{3,2,1,0:T(8,128)(2,1)} custom-call(s32[4]{0:T(128)} %pad_add_fusion.refs_0_, bf16[16,64,128]{2,1,0:T(8,128)(2,1)} %copy-done.35, bf16[16,64,128]{2,1,0:T(8,128)(2,1)} %copy-done.41, bf16[16,64,128]{2,1,0:T(8,128)(2,1)} %copy-done.42, bf16[16,64,128]{2,1,0:T(8,128)(2,1)} %collective-permute-done.2.refs_4_, ...), custom_call_target="tpu_custom_call" | custom-call | tf_op jit(solution)/shard_map/features_turned/pallas_call | solution.py:131
  52.4 5.5 %all-to-all-start.1 = ((bf16[8,8,16,128]{3,2,1,0:T(8,128)(2,1)}), bf16[8,8,16,128]{3,2,1,0:T(8,128)(2,1)S(1)}, u32[]{:S(2)}, u32[]{:S(2)}) async-start(bf16[8,8,16,128]{3,2,1,0:T(8,128)(2,1)} %after.13), calls=%async_computation.1 | async-start | bytes 524288 | tf_op jit(solution)/shard_map/all_to_all | solution.py:925
  59.0 9.6 %conv_one.1 = (bf16[4,2,8,2,16,128]{5,4,3,2,1,0:T(8,128)(2,1)}, bf16[4,2,8,2,16,128]{5,4,3,2,1,0:T(8,128)(2,1)}, bf16[8,2,8,2,16,128]{5,4,3,2,1,0:T(8,128)(2,1)}...) custom-call(s32[4]{0:T(128)} %pad_add_fusion.refs_0_, ...), custom_call_target="tpu_custom_call" | custom-call | tf_op jit(solution)/shard_map/conv_one/pallas_call | solution.py:131
  71.5 2.7 %squeeze.5 = (bf16[64,2048]{1,0:T(8,128)(2,1)}, f32[16,32,128]{2,1,0:T(8,128)}) custom-call(bf16[8,8,16,128]{3,2,1,0:T(8,128)(2,1)} %copy-done.37, bf16[256,2048]{1,0:T(8,128)(2,1)} %all-gather.9.cloned.1.call-done.refs_1_, f32[16,128]{1,0:T(8,128)} %get-tuple-element.60.refs_2_), custom_call_target="tpu_custom_call" | custom-call | tf_op jit(solution)/shard_map/squeeze/pallas_call | solution.py:131
  74.2 20.4 %all_to_all.35.refs_0_ = f32[16,32,128]{2,1,0:T(8,128)} all-to-all(f32[16,32,128]{2,1,0:T(8,128)} %get-tuple-element.61), channel_id=1, replica_groups={{0,1,4,5,8,9,12,13,16,17,20,21,24,25,28,29},{2,3,6,7,10,11,14,15,18,19,..., dimensions={0} | all-to-all | bytes 524288 | tf_op jit(solution)/shard_map/all_to_all | solution.py:953
  97.9 3.2 %collective-permute-done.8.refs_6_.refs_3_.refs_1_ = f32[3,16,128]{2,1,0:T(8,128)S(1)} collective-permute-done((f32[3,16,128]{2,1,0:T(8,128)S(1)}, f32[3,16,128]{2,1,0:T(8,128)S(1)}, u32[]{:S(2)}, u32[]{:S(2)}) %collective-permute-start.8) | collective-permute-done | bytes 24608 | tf_op jit(solution)/shard_map/ppermute | solution.py:887
  102.5 2.3 collective-permute-done.10.refs_2_
  109.9 9.5 %conv_two.1 = (bf16[18,18,16,256]{3,2,1,0:T(8,128)(2,1)}, f32[16,16,16,128]{3,2,1,0:T(8,128)}, bf16[16,16,16,128]{3,2,1,0:T(8,128)(2,1)}, f32[4,16,128]{2,1,0:T(8,128)}) custom-call(s32[4]{0:T(128)} %pad_add_fusion.refs_0_, bf16[8,16,16,128]{3,2,1,0:T(8,128)(2,1)} %bitcast.35, bf16[8,16,16,128]{3,2,1,0:T(8,128)(2,1)} %bitcast.37, ...), custom_call_target="tpu_custom_call" | custom-call | tf_op jit(solution)/shard_map/conv_two/pallas_call | solution.py:131
  120.0 2.7 %gate.1 = (f32[2,16,128]{2,1,0:T(8,128)}, f32[32,256]{1,0:T(8,128)}, f32[16,24,128]{2,1,0:T(8,128)}) custom-call(s32[4]{0:T(128)} %pad_add_fusion.refs_0_, f32[3,16,128]{2,1,0:T(8,128)} %copy-done.18, f32[3,16,128]{2,1,0:T(8,128)} %copy-done.51, f32[3,16,128]{2,1,0:T(8,128)} %copy-done.47, f32[3,16,128]{2,1,0:T(8,128)} %copy-done.52, ...), custom_call_target="tpu_custom_call" | custom-call | tf_op jit(solution)/shard_map/gate/pallas_call | solution.py:131
  122.8 5.2 %all-to-all-start.3 = ((f32[16,24,128]{2,1,0:T(8,128)}), f32[16,24,128]{2,1,0:T(8,128)S(1)}, u32[]{:S(2)}, u32[]{:S(2)}) async-start(f32[16,24,128]{2,1,0:T(8,128)} %get-tuple-element.69), calls=%async_computation.3 | async-start | bytes 393216 | tf_op jit(solution)/shard_map/all_to_all | solution.py:953
  129.4 7.6 %all-to-all-done.3.refs_13_.refs_1_ = f32[16,24,128]{2,1,0:T(8,128)S(1)} async-done(((f32[16,24,128]{2,1,0:T(8,128)}), f32[16,24,128]{2,1,0:T(8,128)S(1)}, u32[]{:S(2)}, u32[]{:S(2)}) %all-to-all-start.3) | async-done | bytes 196640 | tf_op jit(solution)/shard_map/all_to_all | solution.py:953
  137.7 12.2 %back_two.1 = (bf16[18,18,16,256]{3,2,1,0:T(8,128)(2,1)}, bf16[16,16,16,128]{3,2,1,0:T(8,128)(2,1)}, bf16[16,16,16,128]{3,2,1,0:T(8,128)(2,1)}, f32[3,16,128]{2,...) custom-call(s32[4]{0:T(128)} %pad_add_fusion.refs_0_, f32[16,16,16,128]{3,2,1,0:T(8,128)} %get-tuple-element.64.refs_1_.refs_3_, ...), custom_call_target="tpu_custom_call" | custom-call | tf_op jit(solution)/shard_map/back_two/pallas_call | solution.py:131
  150.5 3.5 %collective-permute-done.14.refs_1_ = f32[3,16,128]{2,1,0:T(8,128)S(1)} collective-permute-done((f32[3,16,128]{2,1,0:T(8,128)}, f32[3,16,128]{2,1,0:T(8,128)S(1)}, u32[]{:S(2)}, u32[]{:S(2)}) %collective-permute-start.14) | collective-permute-done | bytes 24608 | tf_op jit(solution)/shard_map/ppermute | solution.py:887
  156.5 3.7 %all-to-all-start.4 = ((f32[16,8,128]{2,1,0:T(8,128)}), f32[16,8,128]{2,1,0:T(8,128)S(1)}, u32[]{:S(2)}, u32[]{:S(2)}) async-start(f32[16,8,128]{2,1,0:T(8,128)} %first_sums.1), calls=%async_computation.4 | async-start | bytes 131072 | tf_op jit(solution)/shard_map/all_to_all | solution.py:953
  160.3 13.8 %refiner_grad.1 = (bf16[8,5,64,128]{3,2,1,0:T(8,128)(2,1)}, bf16[8,5,64,128]{3,2,1,0:T(8,128)(2,1)}, bf16[16,64,256]{2,1,0:T(8,128)(2,1)}, bf16[16,64,256]{2,1,0:T(8,128)(2,1)}) custom-call(s32[4]{0:T(128)} %pad_add_fusion.refs_0_, bf16[18,18,16,256]{3,2,1,0:T(8,128)(2,1)} %get-tuple-element.71.refs_1_, bf16[18,18,16,256]{3,2,1,0:T(8,128)(2,1)} %get-tuple-element.72.refs_2_, ...), custom_call_target="tpu_custom_call" | custom-call | tf_op jit(solution)/shard_map/refiner_grad/pallas_call | solution.py:131
  177.8 4.0 %excite_back.1 = (bf16[32,128]{1,0:T(8,128)(2,1)}, bf16[8,384,128]{2,1,0:T(8,128)(2,1)}) custom-call(s32[4]{0:T(128)} %pad_add_fusion.refs_0_, f32[2,16,128]{2,1,0:T(8,128)} %copy-done.50, f32[2,16,128]{2,1,0:T(8,128)} %copy-done.53, f32[32,256]{1,0:T(8,128)} %get-tuple-element.82.refs_3_, bf16[128,256]{1,0:T(8,128)(2,1)} %copy-done.12, ...), custom_call_target="tpu_custom_call" | custom-call | tf_op jit(solution)/shard_map/excite_back/pallas_call | solution.py:131
  181.8 5.8 %all-to-all-start.5 = ((bf16[8,384,128]{2,1,0:T(8,128)(2,1)}), bf16[8,384,128]{2,1,0:T(8,128)(2,1)S(1)}, u32[]{:S(2)}, u32[]{:S(2)}) async-start(bf16[8,384,128]{2,1,0:T(8,128)(2,1)} %get-tuple-element.86.refs_12_), calls=%async_computation.5 | async-start | bytes 1572864 | tf_op jit(solution)/shard_map/all_to_all | solution.py:925
  188.5 13.4 %back_one.1 = (bf16[2,2,10,10,16,256]{5,4,3,2,1,0:T(8,128)(2,1)}, f32[8,128]{1,0:T(8,128)}, bf16[8,9,64,128]{3,2,1,0:T(8,128)(2,1)}, bf16[8,9,64,128]{3,2,1,0:T(8,128)(2,1)}) custom-call(s32[4]{0:T(128)} %pad_add_fusion.refs_0_, bf16[4,2,8,2,16,128]{5,4,3,2,1,0:T(8,128)(2,1)} %get-tuple-element.57.refs_1_, ...), custom_call_target="tpu_custom_call" | custom-call | tf_op jit(solution)/shard_map/back_one/pallas_call | solution.py:131
  201.9 3.0 %collective-permute-done.18.refs_1_ = bf16[8,9,64,128]{3,2,1,0:T(8,128)(2,1)S(1)} collective-permute-done((bf16[8,9,64,128]{3,2,1,0:T(8,128)(2,1)}, bf16[8,9,64,128]{3,2,1,0:T(8,128)(2,1)S(1)}, u32[]{:S(2)}, u32[]{:S(2)}) %collective-permute-start.18) | collective-permute-done | bytes 1179680 | tf_op jit(solution)/shard_map/ppermute | solution.py:887
  206.0 2.6 %widener_pair.1.refs_0_ = bf16[8,9,64,128]{3,2,1,0:T(8,128)(2,1)} custom-call(bf16[8,9,64,128]{3,2,1,0:T(8,128)(2,1)} %get-tuple-element.90.refs_0_, bf16[8,9,64,128]{3,2,1,0:T(8,128)(2,1)} %copy-done.31), custom_call_target="tpu_custom_call" | custom-call | tf_op jit(solution)/shard_map/widener_pair/pallas_call | solution.py:131
  209.6 6.1 %all-to-all-start.6 = ((bf16[8,9,64,128]{3,2,1,0:T(8,128)(2,1)}), bf16[8,9,64,128]{3,2,1,0:T(8,128)(2,1)S(1)}, u32[]{:S(2)}, u32[]{:S(2)}) async-start(bf16[8,9,64,128]{3,2,1,0:T(8,128)(2,1)} %after.20.refs_3_.refs_2_), calls=%async_computation.6 | async-start | bytes 2359296 | tf_op jit(solution)/shard_map/all_to_all | solution.py:925
  215.8 4.7 %skip_back.1 = (bf16[32,8192]{1,0:T(8,128)(2,1)}, bf16[32,8192]{1,0:T(8,128)(2,1)}) custom-call(s32[4]{0:T(128)} %pad_add_fusion.refs_0_, bf16[32,128]{1,0:T(8,128)(2,1)} %get-tuple-element.89.refs_1_, bf16[512,2048]{1,0:T(8,128)(2,1)} %all-gather.13.cloned.1.call-done.refs_2_, bf16[8,9,64,128]{3,2,1,0:T(8,128)(2,1)} %after.20.refs_3_.refs_2_), custom_call_target="tpu_custom_call" | custom-call | tf_op jit(solution)/shard_map/skip_back/pallas_call | solution.py:131
  223.9 11.2 %input_back.1 = (bf16[16,64,128]{2,1,0:T(8,128)(2,1)}, bf16[16,64,128]{2,1,0:T(8,128)(2,1)}, bf16[16,64,128]{2,1,0:T(8,128)(2,1)}, bf16[16,64,128]{2,1,0:T(8,128)(2,1)}) custom-call(s32[4]{0:T(128)} %pad_add_fusion.refs_0_, bf16[2,2,10,10,16,256]{5,4,3,2,1,0:T(8,128)(2,1)} %get-tuple-element.87.refs_1_, bf16[16,256,512]{2,1,0:T(8,128)(2,1)} %get-tuple-element.88.refs_2_, ...), custom_call_target="tpu_custom_call" | custom-call | tf_op jit(solution)/shard_map/input_back/pallas_call | solution.py:131
  239.5 2.9 %squeeze_back.1 = (f32[32,64]{1,0:T(8,128)}, f32[16,64,128]{2,1,0:T(8,128)}, f32[9,2,32,64]{3,2,1,0:T(8,128)}) custom-call(bf16[8,384,128]{2,1,0:T(8,128)(2,1)} %copy-done.25, bf16[256,2048]{1,0:T(8,128)(2,1)} %all-gather.11.cloned.1.call-done.refs_14_.refs_1_, bf16[8,9,64,128]{3,2,1,0:T(8,128)(2,1)} %after.20.refs_3_.refs_2_), custom_call_target="tpu_custom_call" | custom-call | tf_op jit(solution)/shard_map/squeeze_back/pallas_call | solution.py:131
  242.4 2.2 all-to-all-done.6.refs_0_
  245.6 2.4 widener_sum.1.refs_7_
  248.0 3.3 %collective-permute-done.21.refs_3_ = bf16[16,64,128]{2,1,0:T(8,128)(2,1)S(1)} collective-permute-done((bf16[16,64,128]{2,1,0:T(8,128)(2,1)}, bf16[16,64,128]{2,1,0:T(8,128)(2,1)S(1)}, u32[]{:S(2)}, u32[]{:S(2)}) %collective-permute-start.21) | collective-permute-done | bytes 262176 | tf_op jit(solution)/shard_map/ppermute | solution.py:887
  252.1 3.6 %last_join.1 = (f32[32,64,128]{2,1,0:T(8,128)}, f32[32,32,128]{2,1,0:T(8,128)}) custom-call(s32[4]{0:T(128)} %pad_add_fusion.refs_0_, bf16[16,64,128]{2,1,0:T(8,128)(2,1)} %get-tuple-element.93.refs_1_, bf16[16,64,128]{2,1,0:T(8,128)(2,1)} %copy-done.46, bf16[16,64,128]{2,1,0:T(8,128)(2,1)} %copy-done.45, bf16[16,64,128]{2,1,0:T(8,128)(2,1)} %copy-done.44, ...), custom_call_target="tpu_custom_call" | custom-call | tf_op jit(solution)/shard_map/last_join/pallas_call | solution.py:131
  (231 shorter events, 55.8 us)
Async XLA Ops:
  7.2 41.6 %all-gather.7.cloned.1.call-start = ((), (), s32[]{:S(2)}) async-start(), calls=%async_computation.7 | async-start | bytes 1310720 | tf_op jit(solution)/shard_map/all_gather | solution.py:982
  11.5 39.8 %all-to-all-start = ((bf16[8,9,64,128]{3,2,1,0:T(8,128)(2,1)}), bf16[8,9,64,128]{3,2,1,0:T(8,128)(2,1)S(1)}, u32[]{:S(2)}, u32[]{:S(2)}) async-start(bf16[8,9,64,128]{3,2,1,0:T(8,128)(2,1)} %pack_wide.1), calls=%async_computation | async-start | bytes 2359296 | tf_op jit(solution)/shard_map/all_to_all | solution.py:925
  18.9 51.8 %all-gather.9.cloned.1.call-start = ((), (), s32[]{:S(2)}) async-start(), calls=%async_computation.8 | async-start | bytes 1310720 | tf_op jit(solution)/shard_map/all_gather | solution.py:984
  19.7 82.0 %all-gather.15.cloned.1.call-start = ((), (), s32[]{:S(2)}) async-start(), calls=%async_computation.11 | async-start | bytes 1179648 | tf_op jit(solution)/shard_map/all_gather | solution.py:1004
  21.7 13.2 %collective-permute-start = (bf16[16,64,128]{2,1,0:T(8,128)(2,1)}, bf16[16,64,128]{2,1,0:T(8,128)(2,1)S(1)}, u32[]{:S(2)}, u32[]{:S(2)}) collective-permute-start(bf16[16,64,128]{2,1,0:T(8,128)(2,1)} %get-tuple-element.108), channel_id=1, source_target_pairs={{0,1},{1,0},{2,3},{3,2},{4,5},{5,4},{6,7},{7,6},{8,9},{9,8},{10,11... | collective-permute-start | bytes 786440 | tf_op jit(solution)/shard_map/ppermute | solution.py:887
  21.8 18.0 %collective-permute-start.2 = (bf16[16,64,128]{2,1,0:T(8,128)(2,1)}, bf16[16,64,128]{2,1,0:T(8,128)(2,1)}, u32[]{:S(2)}, u32[]{:S(2)}) collective-permute-start(bf16[16,64,128]{2,1,0:T(8,128)(2,1)} %get-tuple-element.108), channel_id=1, source_target_pairs={{0,3},{1,2},{2,1},{3,0},{4,7},{5,6},{6,5},{7,4},{8,11},{9,10},{10,... | collective-permute-start | bytes 786440 | tf_op jit(solution)/shard_map/ppermute | solution.py:887
  24.4 4.3 %collective-permute-start.3 = (bf16[16,64,256]{2,1,0:T(8,128)(2,1)}, bf16[16,64,256]{2,1,0:T(8,128)(2,1)S(1)}, u32[]{:S(2)}, u32[]{:S(2)}) collective-permute-start(bf16[16,64,256]{2,1,0:T(8,128)(2,1)} %get-tuple-element.106), channel_id=1, source_target_pairs={{0,1},{1,0},{2,3},{3,2},{4,5},{5,4},{6,7},{7,6},{8,9},{9,8},{10,11... | collective-permute-start | bytes 1572872 | tf_op jit(solution)/shard_map/ppermute | solution.py:887
  24.5 15.2 %collective-permute-start.1 = (bf16[16,64,128]{2,1,0:T(8,128)(2,1)S(1)}, bf16[16,64,128]{2,1,0:T(8,128)(2,1)S(1)}, u32[]{:S(2)}, u32[]{:S(2)}) collective-permute-start(bf16[16,64,128]{2,1,0:T(8,128)(2,1)S(1)} %get-tuple-element.109.refs_1_), channel_id=1, source_target_pairs={{0,2},{1,3},{2,0},{3,1},{4,6},{5,7},{6,4},{7,5},{8,10},{9,11},{10,... | collective-permute-start | bytes 786440 | tf_op jit(solution)/shard_map/ppermute | solution.py:887
  26.5 20.0 %collective-permute-start.9 = (bf16[64,32]{1,0:T(8,128)(2,1)S(1)}, bf16[64,32]{1,0:T(8,128)(2,1)S(1)}, u32[]{:S(2)}, u32[]{:S(2)}) collective-permute-start(bf16[64,32]{1,0:T(8,128)(2,1)S(1)} %copy.55.refs_1_), channel_id=1, source_target_pairs={{0,2},{1,3},{2,0},{3,1},{4,6},{5,7},{6,4},{7,5},{8,10},{9,11},{10,... | collective-permute-start | bytes 12296 | tf_op jit(solution)/shard_map/ppermute | solution.py:887
  52.4 5.6 %collective-permute-start.5 = (bf16[8,9,64,128]{3,2,1,0:T(8,128)(2,1)}, bf16[8,9,64,128]{3,2,1,0:T(8,128)(2,1)S(1)}, u32[]{:S(2)}, u32[]{:S(2)}) collective-permute-start(bf16[8,9,64,128]{3,2,1,0:T(8,128)(2,1)} %after.12.refs_1_), channel_id=1, source_target_pairs={{0,1},{1,0},{2,3},{3,2},{4,5},{5,4},{6,7},{7,6},{8,9},{9,8},{10,11... | collective-permute-start | bytes 3538952 | tf_op jit(solution)/shard_map/ppermute | solution.py:887
  52.4 18.4 %all-to-all-start.1 = ((bf16[8,8,16,128]{3,2,1,0:T(8,128)(2,1)}), bf16[8,8,16,128]{3,2,1,0:T(8,128)(2,1)S(1)}, u32[]{:S(2)}, u32[]{:S(2)}) async-start(bf16[8,8,16,128]{3,2,1,0:T(8,128)(2,1)} %after.13), calls=%async_computation.1 | async-start | bytes 524288 | tf_op jit(solution)/shard_map/all_to_all | solution.py:925
  57.9 79.8 %all-gather.11.cloned.1.call-start = ((), (), s32[]{:S(2)}) async-start(), calls=%async_computation.9 | async-start | bytes 1310720 | tf_op jit(solution)/shard_map/all_gather | solution.py:1063
  68.7 25.9 %collective-permute-start.6 = (bf16[4,2,8,2,16,128]{5,4,3,2,1,0:T(8,128)(2,1)}, bf16[4,2,8,2,16,128]{5,4,3,2,1,0:T(8,128)(2,1)S(1)}, u32[]{:S(2)}, u32[]{:S(2)}) collective-permute-start(bf16[4,2,8,2,16,128]{5,4,3,2,1,0:T(8,128)(2,1)} %get-tuple-element.57.refs_1_), channel_id=1, source_target_pairs={{0,2},{1,3},{2,0},{3,1},{4,6},{5,7},{6,4},{7,5},{8,10},{9,11},{10,... | collective-permute-start | bytes 1572872 | tf_op jit(solution)/shard_map/ppermute | solution.py:887
  69.2 25.4 %collective-permute-start.7 = (bf16[4,2,8,2,16,128]{5,4,3,2,1,0:T(8,128)(2,1)}, bf16[4,2,8,2,16,128]{5,4,3,2,1,0:T(8,128)(2,1)S(1)}, u32[]{:S(2)}, u32[]{:S(2)}) collective-permute-start(bf16[4,2,8,2,16,128]{5,4,3,2,1,0:T(8,128)(2,1)} %get-tuple-element.58.refs_2_), channel_id=1, source_target_pairs={{0,2},{1,3},{2,0},{3,1},{4,6},{5,7},{6,4},{7,5},{8,10},{9,11},{10,... | collective-permute-start | bytes 1572872 | tf_op jit(solution)/shard_map/ppermute | solution.py:887
  97.2 3.9 %collective-permute-start.8 = (f32[3,16,128]{2,1,0:T(8,128)S(1)}, f32[3,16,128]{2,1,0:T(8,128)S(1)}, u32[]{:S(2)}, u32[]{:S(2)}) collective-permute-start(f32[3,16,128]{2,1,0:T(8,128)S(1)} %get-tuple-element.62.refs_5_.refs_1_), channel_id=1, source_target_pairs={{0,2},{1,3},{2,0},{3,1},{4,6},{5,7},{6,4},{7,5},{8,10},{9,11},{10,... | collective-permute-start | bytes 73736 | tf_op jit(solution)/shard_map/ppermute | solution.py:887
  101.7 3.0 %collective-permute-start.10 = (bf16[8,8,64,128]{3,2,1,0:T(8,128)(2,1)}, bf16[8,8,64,128]{3,2,1,0:T(8,128)(2,1)S(1)}, u32[]{:S(2)}, u32[]{:S(2)}) collective-permute-start(bf16[8,8,64,128]{3,2,1,0:T(8,128)(2,1)} %after.15.refs_1_), channel_id=1, source_target_pairs={{0,1},{1,0},{2,3},{3,2},{4,5},{5,4},{6,7},{7,6},{8,9},{9,8},{10,11... | collective-permute-start | bytes 3145736 | tf_op jit(solution)/shard_map/ppermute | solution.py:887
  101.8 17.6 %collective-permute-start.11 = (f32[3,16,128]{2,1,0:T(8,128)S(1)}, f32[3,16,128]{2,1,0:T(8,128)S(1)}, u32[]{:S(2)}, u32[]{:S(2)}) collective-permute-start(f32[3,16,128]{2,1,0:T(8,128)S(1)} %get-tuple-element.62.refs_5_.refs_1_), channel_id=1, source_target_pairs={{0,1},{1,0},{2,3},{3,2},{4,5},{5,4},{6,7},{7,6},{8,9},{9,8},{10,11... | collective-permute-start | bytes 73736 | tf_op jit(solution)/shard_map/ppermute | solution.py:887
  102.5 17.0 %collective-permute-start.12 = (f32[3,16,128]{2,1,0:T(8,128)S(1)}, f32[3,16,128]{2,1,0:T(8,128)S(1)}, u32[]{:S(2)}, u32[]{:S(2)}) collective-permute-start(f32[3,16,128]{2,1,0:T(8,128)S(1)} %copy-done.48), channel_id=1, source_target_pairs={{0,1},{1,0},{2,3},{3,2},{4,5},{5,4},{6,7},{7,6},{8,9},{9,8},{10,11... | collective-permute-start | bytes 73736 | tf_op jit(solution)/shard_map/ppermute | solution.py:887
  122.8 14.2 %all-to-all-start.3 = ((f32[16,24,128]{2,1,0:T(8,128)}), f32[16,24,128]{2,1,0:T(8,128)S(1)}, u32[]{:S(2)}, u32[]{:S(2)}) async-start(f32[16,24,128]{2,1,0:T(8,128)} %get-tuple-element.69), calls=%async_computation.3 | async-start | bytes 393216 | tf_op jit(solution)/shard_map/all_to_all | solution.py:953
  128.0 87.8 %all-gather.13.cloned.1.call-start = ((), (), s32[]{:S(2)}) async-start(), calls=%async_computation.10 | async-start | bytes 2359296 | tf_op jit(solution)/shard_map/all_gather | solution.py:1103
  149.9 4.1 %collective-permute-start.14 = (f32[3,16,128]{2,1,0:T(8,128)}, f32[3,16,128]{2,1,0:T(8,128)S(1)}, u32[]{:S(2)}, u32[]{:S(2)}) collective-permute-start(f32[3,16,128]{2,1,0:T(8,128)} %get-tuple-element.79), channel_id=1, source_target_pairs={{0,2},{1,3},{2,0},{3,1},{4,6},{5,7},{6,4},{7,5},{8,10},{9,11},{10,... | collective-permute-start | bytes 73736 | tf_op jit(solution)/shard_map/ppermute | solution.py:887
  154.6 32.9 %collective-permute-start.15 = (bf16[16,16,16,128]{3,2,1,0:T(8,128)(2,1)}, bf16[16,16,16,128]{3,2,1,0:T(8,128)(2,1)S(1)}, u32[]{:S(2)}, u32[]{:S(2)}) collective-permute-start(bf16[16,16,16,128]{3,2,1,0:T(8,128)(2,1)} %after.17), channel_id=1, source_target_pairs={{0,2},{1,3},{2,0},{3,1},{4,6},{5,7},{6,4},{7,5},{8,10},{9,11},{10,... | collective-permute-start | bytes 3145736 | tf_op jit(solution)/shard_map/ppermute | solution.py:887
  156.5 17.5 %all-to-all-start.4 = ((f32[16,8,128]{2,1,0:T(8,128)}), f32[16,8,128]{2,1,0:T(8,128)S(1)}, u32[]{:S(2)}, u32[]{:S(2)}) async-start(f32[16,8,128]{2,1,0:T(8,128)} %first_sums.1), calls=%async_computation.4 | async-start | bytes 131072 | tf_op jit(solution)/shard_map/all_to_all | solution.py:953
  181.8 26.9 %all-to-all-start.5 = ((bf16[8,384,128]{2,1,0:T(8,128)(2,1)}), bf16[8,384,128]{2,1,0:T(8,128)(2,1)S(1)}, u32[]{:S(2)}, u32[]{:S(2)}) async-start(bf16[8,384,128]{2,1,0:T(8,128)(2,1)} %get-tuple-element.86.refs_12_), calls=%async_computation.5 | async-start | bytes 1572864 | tf_op jit(solution)/shard_map/all_to_all | solution.py:925
  201.9 3.1 %collective-permute-start.18 = (bf16[8,9,64,128]{3,2,1,0:T(8,128)(2,1)}, bf16[8,9,64,128]{3,2,1,0:T(8,128)(2,1)S(1)}, u32[]{:S(2)}, u32[]{:S(2)}) collective-permute-start(bf16[8,9,64,128]{3,2,1,0:T(8,128)(2,1)} %get-tuple-element.91), channel_id=1, source_target_pairs={{0,1},{1,0},{2,3},{3,2},{4,5},{5,4},{6,7},{7,6},{8,9},{9,8},{10,11... | collective-permute-start | bytes 3538952 | tf_op jit(solution)/shard_map/ppermute | solution.py:887
  209.6 35.0 %all-to-all-start.6 = ((bf16[8,9,64,128]{3,2,1,0:T(8,128)(2,1)}), bf16[8,9,64,128]{3,2,1,0:T(8,128)(2,1)S(1)}, u32[]{:S(2)}, u32[]{:S(2)}) async-start(bf16[8,9,64,128]{3,2,1,0:T(8,128)(2,1)} %after.20.refs_3_.refs_2_), calls=%async_computation.6 | async-start | bytes 2359296 | tf_op jit(solution)/shard_map/all_to_all | solution.py:925
  215.7 6.4 %collective-permute-start.13 = (bf16[16,64,256]{2,1,0:T(8,128)(2,1)S(1)}, bf16[16,64,256]{2,1,0:T(8,128)(2,1)S(1)}, u32[]{:S(2)}, u32[]{:S(2)}) collective-permute-start(bf16[16,64,256]{2,1,0:T(8,128)(2,1)S(1)} %copy-done.59), channel_id=1, source_target_pairs={{0,1},{1,0},{2,3},{3,2},{4,5},{5,4},{6,7},{7,6},{8,9},{9,8},{10,11... | collective-permute-start | bytes 1572872 | tf_op jit(solution)/shard_map/ppermute | solution.py:887
  220.5 14.6 %collective-permute-start.19 = (bf16[32,8192]{1,0:T(8,128)(2,1)}, bf16[32,8192]{1,0:T(8,128)(2,1)S(1)}, u32[]{:S(2)}, u32[]{:S(2)}) collective-permute-start(bf16[32,8192]{1,0:T(8,128)(2,1)} %get-tuple-element.92.refs_3_), channel_id=1, source_target_pairs={{0,2},{1,3},{2,0},{3,1},{4,6},{5,7},{6,4},{7,5},{8,10},{9,11},{10,... | collective-permute-start | bytes 1572872 | tf_op jit(solution)/shard_map/ppermute | solution.py:887
  236.7 11.3 %collective-permute-start.23 = (bf16[32,4096]{1,0:T(8,128)(2,1)S(1)}, bf16[32,4096]{1,0:T(8,128)(2,1)S(1)}, u32[]{:S(2)}, u32[]{:S(2)}) collective-permute-start(bf16[32,4096]{1,0:T(8,128)(2,1)S(1)} %get-tuple-element.99), channel_id=1, source_target_pairs={{0,1},{1,0},{2,3},{3,2},{4,5},{5,4},{6,7},{7,6},{8,9},{9,8},{10,11... | collective-permute-start | bytes 786440 | tf_op jit(solution)/shard_map/ppermute | solution.py:887
  236.9 11.2 %collective-permute-start.22 = (bf16[16,64,128]{2,1,0:T(8,128)(2,1)}, bf16[16,64,128]{2,1,0:T(8,128)(2,1)S(1)}, u32[]{:S(2)}, u32[]{:S(2)}) collective-permute-start(bf16[16,64,128]{2,1,0:T(8,128)(2,1)} %after.23), channel_id=1, source_target_pairs={{0,3},{1,2},{2,1},{3,0},{4,7},{5,6},{6,5},{7,4},{8,11},{9,10},{10,... | collective-permute-start | bytes 786440 | tf_op jit(solution)/shard_map/ppermute | solution.py:887
  238.2 13.1 %collective-permute-start.21 = (bf16[16,64,128]{2,1,0:T(8,128)(2,1)}, bf16[16,64,128]{2,1,0:T(8,128)(2,1)S(1)}, u32[]{:S(2)}, u32[]{:S(2)}) collective-permute-start(bf16[16,64,128]{2,1,0:T(8,128)(2,1)} %after.22), channel_id=1, source_target_pairs={{0,2},{1,3},{2,0},{3,1},{4,6},{5,7},{6,4},{7,5},{8,10},{9,11},{10,... | collective-permute-start | bytes 786440 | tf_op jit(solution)/shard_map/ppermute | solution.py:887
  238.8 12.5 %collective-permute-start.20 = (bf16[16,64,128]{2,1,0:T(8,128)(2,1)}, bf16[16,64,128]{2,1,0:T(8,128)(2,1)S(1)}, u32[]{:S(2)}, u32[]{:S(2)}) collective-permute-start(bf16[16,64,128]{2,1,0:T(8,128)(2,1)} %after.21), channel_id=1, source_target_pairs={{0,1},{1,0},{2,3},{3,2},{4,5},{5,4},{6,7},{7,6},{8,9},{9,8},{10,11... | collective-permute-start | bytes 786440 | tf_op jit(solution)/shard_map/ppermute | solution.py:887
  (66 other events, 292.9 us)
Sparse Core Ops, SparseCore 0:
  10.4 22.7 all-gather.6
  34.7 16.2 all-gather.8
  53.1 43.7 all-gather.14
  101.8 16.3 all-gather.10
  137.8 46.9 all-gather.12
